TPU v7x, 128 devices: a whole 4x4x4 slice. The times are simulated.
128 devices in a mesh: expert: 32 (over x, y, core), hidden: 4 (over z).
Axes of the slice: x: 4, y: 4, z: 4, core: 2. Of those that a mesh axis runs over, the one named last changes fastest.
Arguments:
- tokens: bfloat16 [8192, 2048], P('expert', 'hidden'), may hold values from -6 to 6
- cotangent: bfloat16 [8192, 2048], P('expert', 'hidden'), may hold values from -6 to 6
- zone_ids: int32 [8192, 2], P('expert'), may hold values from 0 to 127, all different within a row; in each aligned block of 256 rows (0 to 255, 256 to 511, ...) at most 8 rows name the same one
- gate_weights: float32 [8192, 2], P('expert'), may hold values from 0.1 to 1
- gate_proj: bfloat16 [128, 2048, 1024], P('expert', None, 'hidden'), may hold values from -0.125 to 0.125
- up_proj: bfloat16 [128, 2048, 1024], P('expert', None, 'hidden'), may hold values from -0.125 to 0.125
- down_proj: bfloat16 [128, 1024, 2048], P('expert', 'hidden'), may hold values from -0.1875 to 0.1875
Outputs:
- input_grad: bfloat16 [8192, 2048], P('expert', 'hidden')
- mix_grad: float32 [8192, 2], P('expert')
- gate_grad: bfloat16 [128, 2048, 1024], P('expert', None, 'hidden')
- up_grad: bfloat16 [128, 2048, 1024], P('expert', None, 'hidden')
- down_grad: bfloat16 [128, 1024, 2048], P('expert', 'hidden')
Inputs may be any that keep to these rules, and one draw needn't show every extreme that they name: `zone_ids`: each row names two different experts. Among the rows of one device (aligned blocks of 256 rows) no expert is named more than 8 times, and in every draw some expert is named exactly 8 times in some block.
All inputs are finite; a program needn't handle non-finite values.
Results may differ from a plain program's by a relative error of at most 0.017.
Values may be sent and summed in bfloat16 or wider, within the bound.
No kernel may reach another device: no remote copies, remote signals or barrier semaphores. Data moves between devices by JAX's collectives and lax.ppermute only.
A program may use at most 128 MiB of HBM per device.

v0:
```python
import jax
import jax.numpy as jnp
from jax import lax
from jax.sharding import PartitionSpec as P

D = 2048


def slot_table(block_ids, experts, cap):
    names = jnp.arange(experts, dtype=jnp.int32)
    onehot = (block_ids[:, None] == names[None, :]).astype(jnp.int32)
    earlier = jnp.cumsum(onehot, axis=0) - onehot
    rank = jnp.sum(earlier * onehot, axis=1)
    count = block_ids.shape[0]
    source_of = (
        jnp.full((experts * cap,), -1, jnp.int32)
        .at[block_ids * cap + rank]
        .set(jnp.arange(count, dtype=jnp.int32))
    )
    return (rank, source_of)


def to_experts(received, local, owners, cap):
    width = received.shape[-1]
    arranged = received.reshape(owners, local, cap, width).transpose(1, 0, 2, 3)
    return arranged.reshape(local, owners * cap, width)


def to_owners(slots, local, owners, cap):
    width = slots.shape[-1]
    arranged = slots.reshape(local, owners, cap, width).transpose(1, 0, 2, 3)
    return arranged.reshape(owners, local * cap, width)


def return_slots(partial_value, local, owners, cap):
    summed = lax.psum_scatter(
        partial_value.astype(jnp.bfloat16), "hidden", scatter_dimension=2, tiled=True
    )
    back = lax.all_to_all(
        to_owners(summed, local, owners, cap), "expert", split_axis=0, concat_axis=0, tiled=True
    )
    return back.reshape(owners * local * cap, back.shape[-1])


def on_device(tokens, cotangent, zone_ids, gate_weights, gate_proj, up_proj, down_proj):
    owners = lax.axis_size("expert")
    local = gate_proj.shape[0]
    experts = local * owners
    tok_rows = tokens.shape[0]
    cap = 4 * tok_rows // experts
    flat_ids = zone_ids.reshape(-1)
    rank, source_of = slot_table(flat_ids, experts, cap)
    valid = source_of >= 0
    safe = jnp.maximum(source_of, 0)
    token_of = safe // 2
    weight_of = jnp.where(valid, gate_weights.reshape(-1)[safe], 0.0)
    dest = flat_ids * cap + rank
    full_tokens, full_cot = (
        lax.all_gather(tokens, "hidden", axis=1, tiled=True),
        lax.all_gather(cotangent, "hidden", axis=1, tiled=True),
    )
    x_buf = jnp.where(valid[:, None], full_tokens[token_of], jnp.zeros((), jnp.bfloat16))
    dy_buf = (full_cot[token_of].astype(jnp.float32) * weight_of[:, None]).astype(jnp.bfloat16)
    width = x_buf.shape[-1]
    x_buf, dy_buf = (
        x_buf.reshape(owners, local * cap, width),
        dy_buf.reshape(owners, local * cap, width),
    )
    x_in, dy_in = (
        lax.all_to_all(x_buf, "expert", split_axis=0, concat_axis=0, tiled=True),
        lax.all_to_all(dy_buf, "expert", split_axis=0, concat_axis=0, tiled=True),
    )
    x_slots = to_experts(x_in, local, owners, cap)
    dy_slots = to_experts(dy_in, local, owners, cap)
    g = jnp.einsum("erd,edf->erf", x_slots, gate_proj, preferred_element_type=jnp.float32)
    u = jnp.einsum("erd,edf->erf", x_slots, up_proj, preferred_element_type=jnp.float32)
    sig = jax.nn.sigmoid(g)
    silu_g = g * sig
    h = (silu_g * u).astype(jnp.bfloat16)
    dh = jnp.einsum("erd,efd->erf", dy_slots, down_proj, preferred_element_type=jnp.float32)
    out_part = jnp.einsum("erf,efd->erd", h, down_proj, preferred_element_type=jnp.float32)
    out_back = return_slots(out_part, local, owners, cap)
    out_pairs = out_back[dest].astype(jnp.float32)
    dy_pairs = jnp.repeat(cotangent, 2, axis=0).astype(jnp.float32)
    mix_terms = (jnp.sum(dy_pairs * out_pairs, axis=1) * D ** (-0.5)).reshape(tok_rows, 2)
    mix_grad = lax.psum(mix_terms, "hidden")
    down_grad = jnp.einsum("erf,erd->efd", h, dy_slots, preferred_element_type=jnp.float32).astype(
        jnp.bfloat16
    )
    dg = (dh * u * sig * (1.0 + g * (1.0 - sig))).astype(jnp.bfloat16)
    du = (dh * silu_g).astype(jnp.bfloat16)
    gate_grad = jnp.einsum("erd,erf->edf", x_slots, dg, preferred_element_type=jnp.float32).astype(
        jnp.bfloat16
    )
    up_grad = jnp.einsum("erd,erf->edf", x_slots, du, preferred_element_type=jnp.float32).astype(
        jnp.bfloat16
    )
    dx_part = jnp.einsum("erf,edf->erd", dg, gate_proj, preferred_element_type=jnp.float32)
    dx_part = dx_part + jnp.einsum("erf,edf->erd", du, up_proj, preferred_element_type=jnp.float32)
    dx_back = return_slots(dx_part, local, owners, cap)
    dx_pairs = dx_back[dest].astype(jnp.float32)
    input_grad = jnp.sum(dx_pairs.reshape(tok_rows, 2, dx_pairs.shape[-1]), axis=1).astype(
        jnp.bfloat16
    )
    return (input_grad, mix_grad, gate_grad, up_grad, down_grad)


def solution(mesh):
    return jax.shard_map(
        on_device,
        mesh=mesh,
        in_specs=(
            P("expert", "hidden"),
            P("expert", "hidden"),
            P("expert", None),
            P("expert", None),
            P("expert", None, "hidden"),
            P("expert", None, "hidden"),
            P("expert", "hidden", None),
        ),
        out_specs=(
            P("expert", "hidden"),
            P("expert", None),
            P("expert", None, "hidden"),
            P("expert", None, "hidden"),
            P("expert", "hidden", None),
        ),
        check_vma=False,
    )
```

profile of v0, /device:TPU:1, one launch (start us, length us, event | category | flops | bytes accessed | tf_op | source)
XLA Modules:
  0.0 337.2 jit_solution(1082059732886794880)
XLA Ops:
  14.1 6.9 %gather_fusion.1 = f32[1024]{0:T(1024)S(1)} fusion(f32[512]{0:T(512)S(1)} %reshape.125, s32[1024]{0:T(1024)S(1)} %get-tuple-element.15), kind=kCustom, calls=%fused_computation.1 | custom fusion | bytes 12288 | tf_op jit(solution)/shard_map/gather | solution.py:56
  21.1 15.1 %all-gather.5.cloned.1.call-done = bf16[256,2048]{1,0:T(8,128)(2,1)} async-done(((bf16[256,512]{1,0:T(8,128)(2,1)}), bf16[256,2048]{1,0:T(8,128)(2,1)}) %all-gather.5.cloned.1.call-update) | async-done | bytes 1048592 | tf_op jit(solution)/shard_map/all_gather | solution.py:59
  36.2 10.2 %gather_fusion.2 = bf16[1024,2048]{1,0:T(8,128)(2,1)} fusion(bf16[256,2048]{1,0:T(8,128)(2,1)} %all-gather.5.cloned.1.call-done, s32[1024]{0:T(1024)S(1)} %get-tuple-element.16), kind=kCustom, calls=%fused_computation.2 | custom fusion | bytes 8392704 | tf_op jit(solution)/shard_map/gather | solution.py:62
  46.4 4.6 %broadcast_select_fusion = bf16[32,32,2048]{2,1,0:T(8,128)(2,1)} fusion(bf16[32,32,2048]{2,1,0:T(8,128)(2,1)} %bitcast.95, pred[32,32]{1,0:T(8,128)(4,1)S(1)} %broadcast_in_dim.43), kind=kLoop, calls=%fused_computation.21 | loop fusion | flops 2097152 | bytes 8389632 | tf_op jit(solution)/shard_map/jit(_where)/select_n | solution.py:62
  50.9 8.5 %all-to-all-start.1 = ((bf16[32,32,2048]{2,1,0:T(8,128)(2,1)}), bf16[32,32,2048]{2,1,0:T(8,128)(2,1)}, u32[]{:S(2)}, u32[]{:S(2)}) async-start(bf16[32,32,2048]{2,1,0:T(8,128)(2,1)} %broadcast_select_fusion), calls=%async_computation.1 | async-start | bytes 8388608 | tf_op jit(solution)/shard_map/all_to_all | solution.py:70
  60.2 25.2 %all-gather.3.cloned.1.call-done = bf16[256,2048]{1,0:T(8,128)(2,1)} async-done(((bf16[256,512]{1,0:T(8,128)(2,1)}), bf16[256,2048]{1,0:T(8,128)(2,1)}) %all-gather.3.cloned.1.call-update) | async-done | bytes 1048592 | tf_op jit(solution)/shard_map/all_gather | solution.py:60
  85.5 10.2 %gather_fusion = bf16[1024,2048]{1,0:T(8,128)(2,1)} fusion(bf16[256,2048]{1,0:T(8,128)(2,1)} %all-gather.3.cloned.1.call-done, s32[1024]{0:T(1024)S(1)} %get-tuple-element.16), kind=kCustom, calls=%fused_computation | custom fusion | bytes 8392704 | tf_op jit(solution)/shard_map/gather | solution.py:63
  95.7 4.9 %fusion = bf16[32,32,2048]{2,1,0:T(8,128)(2,1)} fusion(bf16[32,32,2048]{2,1,0:T(8,128)(2,1)} %bitcast.94, f32[32,32]{1,0:T(8,128)S(1)} %mul.69), kind=kLoop, calls=%fused_computation.7 | loop fusion | flops 6291456 | bytes 8392704 | tf_op jit(solution)/shard_map/convert_element_type | solution.py:63
  100.6 11.0 %all-to-all-done.1 = bf16[32,32,2048]{2,1,0:T(8,128)(2,1)} async-done(((bf16[32,32,2048]{2,1,0:T(8,128)(2,1)}), bf16[32,32,2048]{2,1,0:T(8,128)(2,1)}, u32[]{:S(2)}, u32[]{:S(2)}) %all-to-all-start.1) | async-done | bytes 4194336 | tf_op jit(solution)/shard_map/all_to_all | solution.py:70
  111.6 7.2 %all-to-all-start = ((bf16[32,32,2048]{2,1,0:T(8,128)(2,1)}), bf16[32,32,2048]{2,1,0:T(8,128)(2,1)}, u32[]{:S(2)}, u32[]{:S(2)}) async-start(bf16[32,32,2048]{2,1,0:T(8,128)(2,1)} %fusion), calls=%async_computation | async-start | bytes 8388608 | tf_op jit(solution)/shard_map/all_to_all | solution.py:71
  119.0 4.7 %fusion.5 = f32[4,256,256]{2,1,0:T(8,128)S(1)} fusion(bf16[4,2048,256]{2,1,0:T(8,128)(2,1)} %param.11, bf16[32,32,2048]{2,1,0:T(8,128)(2,1)} %all-to-all-done.1), kind=kOutput, calls=%fused_computation.13 | convolution fusion | flops 1073741824 | bytes 9437184 | tf_op jit(solution)/shard_map/erd,edf->erf/dot_general | solution.py:75
  123.8 47.3 %all-to-all-done = bf16[32,32,2048]{2,1,0:T(8,128)(2,1)} async-done(((bf16[32,32,2048]{2,1,0:T(8,128)(2,1)}), bf16[32,32,2048]{2,1,0:T(8,128)(2,1)}, u32[]{:S(2)}, u32[]{:S(2)}) %all-to-all-start) | async-done | bytes 4194336 | tf_op jit(solution)/shard_map/all_to_all | solution.py:71
  171.0 4.9 %fusion.11 = f32[4,256,256]{2,1,0:T(8,128)S(1)} fusion(bf16[4,256,2048]{2,1,0:T(8,128)(2,1)} %param.13, bf16[32,32,2048]{2,1,0:T(8,128)(2,1)} %all-to-all-done), kind=kOutput, calls=%fused_computation.19 | convolution fusion | flops 1073741824 | bytes 9437184 | tf_op jit(solution)/shard_map/erd,efd->erf/dot_general | solution.py:80
  175.9 4.0 %multiply_convert_fusion = (bf16[4,256,256]{2,1,0:T(8,128)(2,1)S(1)}, bf16[4,256,256]{2,1,0:T(8,128)(2,1)S(1)}, bf16[4,256,256]{2,1,0:T(8,128)(2,1)S(1)}) fusion(f32[4,256,256]{2,1,0:T(8,128)S(1)} %fusion.5, f32[4,256,256]{2,1,0:T(8,128)S(1)} %fusion.11, bf16[4,2048,256]{2,1,0:T(8,128)(2,1)S(1)} %copy-done.1, bf16[32,32,2048]{2,1,0:T(8,128)(2,1)} %all-to-all-done.1), kind=kOutput, calls=%fused_computation.35 | convolution fusion | flops 1077673984 | bytes 12058624 | tf_op jit(solution)/shard_map/erd,edf->erf/dot_general | solution.py:76
  181.3 3.3 add_convert_fusion
  184.7 5.5 %convolution_convert_fusion = bf16[4,256,2048]{2,1,0:T(8,128)(2,1)} fusion(bf16[4,256,256]{2,1,0:T(8,128)(2,1)S(1)} %get-tuple-element.12, bf16[4,256,2048]{2,1,0:T(8,128)(2,1)} %param.13), kind=kOutput, calls=%fused_computation.25 | convolution fusion | flops 1075838976 | bytes 8912896 | tf_op jit(solution)/shard_map/erf,efd->erd/dot_general | solution.py:81
  190.2 41.7 %reduce-scatter.3.cloned.1.call-done = bf16[4,256,512]{2,1,0:T(8,128)(2,1)} async-done(((bf16[4,256,2048]{2,1,0:T(8,128)(2,1)}), bf16[4,256,512]{2,1,0:T(8,128)(2,1)}) %reduce-scatter.3.cloned.1.call-update) | async-done | bytes 1048592 | tf_op jit(solution)/shard_map/reduce_scatter | solution.py:36
  234.2 7.5 %all-to-all-start.2 = ((bf16[32,32,512]{2,1,0:T(8,128)(2,1)}), bf16[32,32,512]{2,1,0:T(8,128)(2,1)S(1)}, u32[]{:S(2)}, u32[]{:S(2)}) async-start(bf16[32,32,512]{2,1,0:T(8,128)(2,1)} %copy_bitcast_fusion.1), calls=%async_computation.3 | async-start | bytes 2097152 | tf_op jit(solution)/shard_map/all_to_all | solution.py:39
  242.7 38.8 %reduce-scatter.5.cloned.1.call-done = bf16[4,256,512]{2,1,0:T(8,128)(2,1)} async-done(((bf16[4,256,2048]{2,1,0:T(8,128)(2,1)}), bf16[4,256,512]{2,1,0:T(8,128)(2,1)}) %reduce-scatter.5.cloned.1.call-update) | async-done | bytes 1048592 | tf_op jit(solution)/shard_map/reduce_scatter | solution.py:36
  283.8 7.5 %all-to-all-start.3 = ((bf16[32,32,512]{2,1,0:T(8,128)(2,1)}), bf16[32,32,512]{2,1,0:T(8,128)(2,1)S(1)}, u32[]{:S(2)}, u32[]{:S(2)}) async-start(bf16[32,32,512]{2,1,0:T(8,128)(2,1)} %copy_bitcast_fusion), calls=%async_computation.5 | async-start | bytes 2097152 | tf_op jit(solution)/shard_map/all_to_all | solution.py:39
  291.4 5.7 %fusion.13 = bf16[4,256,2048]{2,1,0:T(8,128)(2,1)} fusion(bf16[4,256,256]{2,1,0:T(8,128)(2,1)} %copy-done.4, bf16[32,32,2048]{2,1,0:T(8,128)(2,1)} %all-to-all-done), kind=kOutput, calls=%fused_computation.22 | convolution fusion | flops 1075838976 | bytes 8912896 | tf_op jit(solution)/shard_map/erf,erd->efd/dot_general | solution.py:87
  297.1 5.9 %fusion.16 = bf16[4,2048,256]{2,1,0:T(8,128)(2,1)} fusion(bf16[4,256,256]{2,1,0:T(8,128)(2,1)S(1)} %copy-done.3, bf16[32,32,2048]{2,1,0:T(8,128)(2,1)} %all-to-all-done.1), kind=kOutput, calls=%fused_computation.23 | convolution fusion | flops 1075838976 | bytes 8912896 | tf_op jit(solution)/shard_map/erd,erf->edf/dot_general | solution.py:92
  303.0 5.9 %fusion.19 = bf16[4,2048,256]{2,1,0:T(8,128)(2,1)} fusion(bf16[4,256,256]{2,1,0:T(8,128)(2,1)S(1)} %copy-done.6, bf16[32,32,2048]{2,1,0:T(8,128)(2,1)} %all-to-all-done.1), kind=kOutput, calls=%fused_computation.24 | convolution fusion | flops 1075838976 | bytes 8912896 | tf_op jit(solution)/shard_map/erd,erf->edf/dot_general | solution.py:95
  315.1 12.8 %psum.7 = f32[256,2]{1,0:T(8,128)S(1)} all-reduce(f32[256,2]{1,0:T(8,128)S(1)} %mul.82), channel_id=1, replica_groups=mesh['expert'=32,'hidden'=4] {'hidden'}, use_global_device_ids=true, to_apply=%region_8.9 | all-reduce | flops 512 | bytes 4096 | tf_op jit(solution)/shard_map/psum | solution.py:86
  (64 shorter events, 24.0 us)
Async XLA Ops:
  7.2 29.0 %all-gather.5.cloned.1.call-start = ((), (), s32[]{:S(2)}) async-start(), calls=%async_computation.7 | async-start | bytes 1310720 | tf_op jit(solution)/shard_map/all_gather | solution.py:59
  50.9 60.7 %all-to-all-start.1 = ((bf16[32,32,2048]{2,1,0:T(8,128)(2,1)}), bf16[32,32,2048]{2,1,0:T(8,128)(2,1)}, u32[]{:S(2)}, u32[]{:S(2)}) async-start(bf16[32,32,2048]{2,1,0:T(8,128)(2,1)} %broadcast_select_fusion), calls=%async_computation.1 | async-start | bytes 8388608 | tf_op jit(solution)/shard_map/all_to_all | solution.py:70
  59.4 26.1 %all-gather.3.cloned.1.call-start = ((), (), s32[]{:S(2)}) async-start(), calls=%async_computation.6 | async-start | bytes 1310720 | tf_op jit(solution)/shard_map/all_gather | solution.py:60
  111.6 59.4 %all-to-all-start = ((bf16[32,32,2048]{2,1,0:T(8,128)(2,1)}), bf16[32,32,2048]{2,1,0:T(8,128)(2,1)}, u32[]{:S(2)}, u32[]{:S(2)}) async-start(bf16[32,32,2048]{2,1,0:T(8,128)(2,1)} %fusion), calls=%async_computation | async-start | bytes 8388608 | tf_op jit(solution)/shard_map/all_to_all | solution.py:71
  118.8 113.0 %reduce-scatter.3.cloned.1.call-start = ((), (), s32[]{:S(2)}) async-start(), calls=%async_computation.8 | async-start | bytes 5242880 | tf_op jit(solution)/shard_map/reduce_scatter | solution.py:36
  171.0 4.9 %copy-start.1 = (bf16[4,2048,256]{2,1,0:T(8,128)(2,1)S(1)}, bf16[4,2048,256]{2,1,0:T(8,128)(2,1)}, u32[]{:S(2)}) copy-start(bf16[4,2048,256]{2,1,0:T(8,128)(2,1)} %param.12) | copy-start | bytes 12582916
  175.9 4.0 %copy-start = (bf16[4,2048,256]{2,1,0:T(8,128)(2,1)S(1)}, bf16[4,2048,256]{2,1,0:T(8,128)(2,1)}, u32[]{:S(2)}) copy-start(bf16[4,2048,256]{2,1,0:T(8,128)(2,1)} %param.11) | copy-start | bytes 12582916
  179.9 1.3 copy-start.2
  179.9 1.3 copy-start.5
  180.0 4.7 %copy-start.4 = (bf16[4,256,256]{2,1,0:T(8,128)(2,1)}, bf16[4,256,256]{2,1,0:T(8,128)(2,1)S(1)}, u32[]{:S(2)}) copy-start(bf16[4,256,256]{2,1,0:T(8,128)(2,1)S(1)} %get-tuple-element.12) | copy-start | bytes 1572868
  184.6 96.8 %reduce-scatter.5.cloned.1.call-start = ((), (), s32[]{:S(2)}) async-start(), calls=%async_computation.9 | async-start | bytes 5242880 | tf_op jit(solution)/shard_map/reduce_scatter | solution.py:36
  190.1 51.5 %copy-start.7 = (bf16[256,512]{1,0:T(8,128)(2,1)S(1)}, bf16[256,512]{1,0:T(8,128)(2,1)}, u32[]{:S(2)}) copy-start(bf16[256,512]{1,0:T(8,128)(2,1)} %param.8) | copy-start | bytes 786436
  234.2 49.7 %all-to-all-start.2 = ((bf16[32,32,512]{2,1,0:T(8,128)(2,1)}), bf16[32,32,512]{2,1,0:T(8,128)(2,1)S(1)}, u32[]{:S(2)}, u32[]{:S(2)}) async-start(bf16[32,32,512]{2,1,0:T(8,128)(2,1)} %copy_bitcast_fusion.1), calls=%async_computation.3 | async-start | bytes 2097152 | tf_op jit(solution)/shard_map/all_to_all | solution.py:39
  283.8 28.9 %all-to-all-start.3 = ((bf16[32,32,512]{2,1,0:T(8,128)(2,1)}), bf16[32,32,512]{2,1,0:T(8,128)(2,1)S(1)}, u32[]{:S(2)}, u32[]{:S(2)}) async-start(bf16[32,32,512]{2,1,0:T(8,128)(2,1)} %copy_bitcast_fusion), calls=%async_computation.5 | async-start | bytes 2097152 | tf_op jit(solution)/shard_map/all_to_all | solution.py:39
  291.4 5.7 %copy-start.3 = (bf16[4,256,256]{2,1,0:T(8,128)(2,1)S(1)}, bf16[4,256,256]{2,1,0:T(8,128)(2,1)}, u32[]{:S(2)}) copy-start(bf16[4,256,256]{2,1,0:T(8,128)(2,1)} %copy-done.2) | copy-start | bytes 1572868
  297.1 5.9 %copy-start.6 = (bf16[4,256,256]{2,1,0:T(8,128)(2,1)S(1)}, bf16[4,256,256]{2,1,0:T(8,128)(2,1)}, u32[]{:S(2)}) copy-start(bf16[4,256,256]{2,1,0:T(8,128)(2,1)} %copy-done.5) | copy-start | bytes 1572868
Sparse Core Ops, SparseCore 0:
  9.7 26.4 all-gather.4
  61.9 23.5 all-gather.2
  184.7 47.0 reduce-scatter.2
  234.8 46.5 reduce-scatter.4
where the time goes:
time: 341 us; the launch traced here: 337 us
  waiting for transfers between devices  180 us (53%)
  local copies, waits for them, and re-layouts  44.7 us (13%)
  matrix products  41.2 us (12%)
  starting transfers between devices  31 us (9%)
  between operations  14.1 us (4%)
  other arithmetic  13 us (4%)
  blocking collectives  12.8 us (4%)
    reduce_scatter x2, waiting for transfers between devices, return_slots(): lax.psum_scatter(partial_value.astype(jnp.bfloat16), 'hidden', scatter_di...  80.4 us
    all_to_all x1, waiting for transfers between devices, on_device(): lax.all_to_all(dy_buf, 'expert', split_axis=0, concat_axis=0, tiled=True)  47.3 us
    all_gather x1, waiting for transfers between devices, on_device(): lax.all_gather(cotangent, 'hidden', axis=1, tiled=True)  25.2 us
    all_gather x1, waiting for transfers between devices, on_device(): lax.all_gather(tokens, 'hidden', axis=1, tiled=True)  15.1 us
    all_to_all x2, starting transfers between devices, return_slots(): lax.all_to_all(to_owners(summed, local, owners, cap), 'expert', split_axi...  15 us
    psum x1, blocking collectives, on_device(): mix_grad = lax.psum(mix_terms, 'hidden')  12.8 us
    all_to_all x1, waiting for transfers between devices, on_device(): lax.all_to_all(x_buf, 'expert', split_axis=0, concat_axis=0, tiled=True)  11 us
    gather x1, local copies, waits for them, and re-layouts, on_device(): full_cot[token_of].astype(jnp.float32) * weight_of[:, None]  10.2 us
  transfers between devices with their start and end apart: 8, of which 6 were waited for; matrix products, arithmetic and copies ran while one was open for 19% of the time, Pallas kernels for 0%

commit v1 on v0

v1 whole, which is shorter than its diff:
```python
import jax
import jax.numpy as jnp
from jax import lax
from jax.experimental import pallas as pl
from jax.experimental.pallas import tpu as pltpu
from jax.sharding import PartitionSpec as P

D = 2048
SCALE = D ** (-0.5)
OWN = 32
NZ = 4
LOC = 4
CAP = 8
TOK = 256
QF = D // NZ
QH = 256
FA = 128
FB = QF - FA
RA = 384
RB = QF - RA
WA = QF + FA
WB = NZ * FB
WR = NZ * RB + 128
BF = jnp.bfloat16
F32 = jnp.float32
VMEM = 48 * 1024 * 1024


def dot(a, b, ca, cb):
    return lax.dot_general(a, b, (((ca,), (cb,)), ((), ())), preferred_element_type=F32)


def shift(x, d):
    return lax.ppermute(x, "hidden", [(i, (i + d) % NZ) for i in range(NZ)])


def params(**kw):
    return pltpu.CompilerParams(vmem_limit_bytes=VMEM, **kw)


def slots_of(dest, base, rows):
    slot = lax.broadcasted_iota(jnp.int32, (rows, TOK), 0) + base
    return slot == dest[0:1, :], slot == dest[1:2, :]


def route_first(zones, weights, tokens, cot, pay, dest_out, dest):
    step = pl.program_id(0)

    @pl.when(step == 0)
    def _():
        expert = lax.broadcasted_iota(jnp.int32, (OWN * LOC, TOK), 0)
        hit0 = expert == zones[0:1, :]
        hit1 = expert == zones[1:2, :]
        both = jnp.where(hit0 | hit1, 1.0, 0.0).astype(BF)
        earlier = lax.broadcasted_iota(jnp.int32, (TOK, TOK), 0) < lax.broadcasted_iota(
            jnp.int32, (TOK, TOK), 1
        )
        count = dot(both, jnp.where(earlier, 1.0, 0.0).astype(BF), 1, 0)
        rank0 = jnp.sum(jnp.where(hit0, count, 0.0), axis=0, keepdims=True)
        rank1 = jnp.sum(jnp.where(hit1, count, 0.0), axis=0, keepdims=True)
        dest[0:1, :] = zones[0:1, :] * CAP + rank0.astype(jnp.int32)
        dest[1:2, :] = zones[1:2, :] * CAP + rank1.astype(jnp.int32)
        dest_out[...] = dest[...]

    at0, at1 = slots_of(dest, step * 256, 256)
    pick = jnp.where(at0 | at1, 1.0, 0.0).astype(BF)
    w = jnp.sum(
        jnp.where(at0, weights[0:1, :], 0.0) + jnp.where(at1, weights[1:2, :], 0.0),
        axis=1,
        keepdims=True,
    )
    x = dot(pick, tokens[...], 1, 0).astype(BF)
    pay[:, :, :QF] = x.reshape(8, 32, QF)
    dy = (dot(pick, cot[:, :FA], 1, 0) * w).astype(BF)
    pay[:, :, QF:] = dy.reshape(8, 32, FA)


def route_rest(dest, weights, c0, c1, c2, c3, pay):
    at0, at1 = slots_of(dest, pl.program_id(0) * 256, 256)
    pick = jnp.where(at0 | at1, 1.0, 0.0).astype(BF)
    w = jnp.sum(
        jnp.where(at0, weights[0:1, :], 0.0) + jnp.where(at1, weights[1:2, :], 0.0),
        axis=1,
        keepdims=True,
    )
    for off, c in enumerate((c0, c1, c2, c3)):
        dy = (dot(pick, c[:, FA:], 1, 0) * w).astype(BF)
        pay[:, :, off * FB : (off + 1) * FB] = dy.reshape(8, 32, FB)


def merged(v):
    n, r, f = v.shape
    return v.astype(F32).reshape(n * r, f).astype(BF)


def assemble(z, own, left, right, far_a, far_b, rest, xs, dys):
    for off, parts in ((0, (own,)), (3, (left,)), (1, (right,)), (2, (far_a, far_b))):
        q = lax.rem(z + off, NZ)
        row = 0
        for part in parts:
            n = part.shape[0] * CAP
            xs[q, row : row + n, :] = merged(part[:, 0, :, :QF])
            dys[q, row : row + n, :FA] = merged(part[:, 0, :, QF:])
            row += n
        dys[q, :, FA:] = merged(rest[:, 0, :, off * FB : (off + 1) * FB])


def parted(v):
    return v.reshape(v.shape[0] // CAP, CAP, v.shape[1]).astype(BF)


def middle(
    z_ref, own, left, right, far_a, far_b, rest, wg, wu, wd,
    o0, o1t, o1b, o2t, o2b, o3t, o3b, part_out, h_out, dg_out, du_out, xs, dys,
):
    z = z_ref[0]
    assemble(z, own, left, right, far_a, far_b, rest, xs, dys)
    g = u = dh = 0.0
    for q in range(NZ):
        rows = slice(q * QF, (q + 1) * QF)
        g = g + dot(xs[q], wg[0, rows, :], 1, 0)
        u = u + dot(xs[q], wu[0, rows, :], 1, 0)
        dh = dh + dot(dys[q], wd[0, :, rows], 1, 1)
    sig = jax.nn.sigmoid(g)
    silu = g * sig
    h = (silu * u).astype(BF)
    dg = (dh * u * sig * (1.0 + g * (1.0 - sig))).astype(BF)
    du = (dh * silu).astype(BF)
    h_out[0] = h
    dg_out[0] = dg
    du_out[0] = du
    mix = jnp.sum(h.astype(F32) * dh, axis=1, keepdims=True)
    high = mix.astype(BF).astype(F32)
    lane = lax.broadcasted_iota(jnp.int32, (OWN * CAP, 128), 1)
    mix = jnp.where(lane == 0, high, jnp.where(lane == 1, mix - high, 0.0))
    part_out[:, 0, :, NZ * RB :] = parted(mix)
    for off, outs in ((2, (o2t, o2b)), (1, (o1t, o1b)), (3, (o3t, o3b)), (0, (o0,))):
        rows = pl.ds(pl.multiple_of(lax.rem(z + off, NZ) * QF, QF), QF)
        dx = dot(dg, wg[0, rows, :], 1, 1) + dot(du, wu[0, rows, :], 1, 1)
        row = 0
        for out in outs:
            n = out.shape[0] * CAP
            out[:, 0] = parted(dx[row : row + n, :RA])
            row += n
        part_out[:, 0, :, off * RB : (off + 1) * RB] = parted(dx[:, RA:])


def grads(
    z_ref, own, left, right, far_a, far_b, rest, h, dg, du,
    gate_out, up_out, down_out, xs, dys,
):
    assemble(z_ref[0], own, left, right, far_a, far_b, rest, xs, dys)
    for q in range(NZ):
        rows = slice(q * QF, (q + 1) * QF)
        gate_out[0, rows, :] = dot(xs[q], dg[0], 0, 0).astype(BF)
        up_out[0, rows, :] = dot(xs[q], du[0], 0, 0).astype(BF)
        down_out[0, :, rows] = dot(h[0], dys[q], 0, 0).astype(BF)


def pick_pairs(dest, back, y0, y1, y2, y3, mix_out):
    at0, at1 = slots_of(dest, 0, OWN * LOC * CAP)
    one0 = jnp.where(at0, 1.0, 0.0).astype(BF)
    one1 = jnp.where(at1, 1.0, 0.0).astype(BF)
    y = dot(one0 + one1, back[:, : NZ * RB], 0, 0).astype(BF)
    for off, out in enumerate((y0, y1, y2, y3)):
        out[...] = y[:, off * RB : (off + 1) * RB]
    m0 = dot(back[:, NZ * RB :], one0, 0, 0)
    m1 = dot(back[:, NZ * RB :], one1, 0, 0)
    mix_out[...] = jnp.zeros_like(mix_out)
    mix_out[0:1, :] = m0[0:1, :] + m0[1:2, :]
    mix_out[1:2, :] = m1[0:1, :] + m1[1:2, :]


def finish(dest, weights, back, y0, y1, y2, y3, m0, m1, m2, m3, grad_out, mix_out):
    at0, at1 = slots_of(dest, 0, OWN * LOC * CAP)
    pick = jnp.where(at0 | at1, 1.0, 0.0).astype(BF)
    grad_out[:, :RA] = dot(pick, back[...], 0, 0).astype(BF)
    y = (y0[...].astype(F32) + y2[...].astype(F32)) + (y1[...].astype(F32) + y3[...].astype(F32))
    grad_out[:, RA:] = y.astype(BF)
    total = (m0[...] + m2[...]) + (m1[...] + m3[...])
    mix_out[...] = total[0:2, :] * SCALE / weights[...]


def shape(dims, dtype=BF):
    return jax.ShapeDtypeStruct(dims, dtype)


def cost(flops, size):
    return pl.CostEstimate(flops=int(flops), bytes_accessed=int(size), transcendentals=0)


def whole(dims):
    return pl.BlockSpec(dims, lambda i: (0,) * len(dims))


def by_expert(n, width):
    return pl.BlockSpec((n, 1, CAP, width), lambda e: (0, e, 0, 0))


def leading(*dims):
    return pl.BlockSpec((1,) + dims, lambda e: (e,) + (0,) * len(dims))


def on_device(tokens, cotangent, zone_ids, gate_weights, gate_proj, up_proj, down_proj):
    z = lax.axis_index("hidden").astype(jnp.int32).reshape(1)
    zones, weights = zone_ids.T, gate_weights.T
    cots = (cotangent, shift(cotangent, -1), shift(cotangent, 2), shift(cotangent, 1))

    pay, dest = pl.pallas_call(
        route_first,
        grid=(4,),
        in_specs=[whole((2, TOK)), whole((2, TOK)), whole((TOK, QF)), whole((TOK, QF))],
        out_specs=[pl.BlockSpec((8, 32, WA), lambda i: (i, 0, 0)), whole((2, TOK))],
        out_shape=[shape((OWN, 32, WA)), shape((2, TOK), jnp.int32)],
        scratch_shapes=[pltpu.VMEM((2, TOK), jnp.int32)],
        compiler_params=params(),
        cost_estimate=cost(5e8, 4e6),
        name="route_first",
    )(zones, weights, tokens, cotangent)
    got = lax.all_to_all(pay, "expert", split_axis=0, concat_axis=0, tiled=True)

    pay_rest = pl.pallas_call(
        route_rest,
        grid=(4,),
        in_specs=[whole((2, TOK)), whole((2, TOK))] + [whole((TOK, QF))] * 4,
        out_specs=pl.BlockSpec((8, 32, WB), lambda i: (i, 0, 0)),
        out_shape=shape((OWN, 32, WB)),
        compiler_params=params(),
        cost_estimate=cost(8e8, 6e6),
        name="route_rest",
    )(dest, weights, *cots)
    rest = lax.all_to_all(pay_rest, "expert", split_axis=0, concat_axis=0, tiled=True)
    rest = rest.reshape(OWN, LOC, CAP, WB)

    half = OWN // 2
    got = got.reshape(OWN, LOC, CAP, WA)
    top, bot = got[:half], got[half:]
    left_t = shift(top, 1)
    right_b = shift(bot, -1)
    left_b = shift(bot, 1)
    right_t = shift(top, -1)
    far_t = shift(left_t, 1)
    far_b = shift(right_b, -1)
    left = jnp.concatenate([left_t, left_b], axis=0)
    right = jnp.concatenate([right_t, right_b], axis=0)

    act_in = (z, got, left, right, far_t, far_b, rest)
    act_specs = [
        pl.BlockSpec(memory_space=pltpu.SMEM),
        by_expert(OWN, WA), by_expert(OWN, WA), by_expert(OWN, WA),
        by_expert(half, WA), by_expert(half, WA), by_expert(OWN, WB),
    ]
    act_scratch = [pltpu.VMEM((NZ, OWN * CAP, QF), BF), pltpu.VMEM((NZ, OWN * CAP, QF), BF)]
    hid = shape((LOC, OWN * CAP, QH))
    whole_part = shape((OWN, LOC, CAP, RA))
    half_part = shape((half, LOC, CAP, RA))
    o0, o1t, o1b, o2t, o2b, o3t, o3b, part, h, dg, du = pl.pallas_call(
        middle,
        grid=(LOC,),
        in_specs=act_specs + [leading(D, QH), leading(D, QH), leading(QH, D)],
        out_specs=[by_expert(OWN, RA)] + [by_expert(half, RA)] * 6 + [by_expert(OWN, WR)]
        + [leading(OWN * CAP, QH)] * 3,
        out_shape=[whole_part] + [half_part] * 6 + [shape((OWN, LOC, CAP, WR)), hid, hid, hid],
        scratch_shapes=act_scratch,
        compiler_params=params(),
        cost_estimate=cost(5.4e9, 27e6),
        name="middle",
    )(*act_in, gate_proj, up_proj, down_proj)

    relay_t = shift(o2t, 1)
    relay_b = shift(o2b, -1)
    from_l_b = shift(o1b, 1)
    from_r_t = shift(o3t, -1)
    from_l_t = shift((o1t.astype(F32) + relay_t.astype(F32)).astype(BF), 1)
    from_r_b = shift((o3b.astype(F32) + relay_b.astype(F32)).astype(BF), -1)

    part_back = lax.all_to_all(
        part.reshape(OWN, 32, WR), "expert", split_axis=0, concat_axis=0, tiled=True
    ).reshape(OWN * 32, WR)

    sum_t = o0[:half].astype(F32) + from_l_t.astype(F32) + from_r_t.astype(F32)
    sum_b = o0[half:].astype(F32) + from_l_b.astype(F32) + from_r_b.astype(F32)
    sums = jnp.concatenate([sum_t.astype(BF), sum_b.astype(BF)], axis=0)
    back = lax.all_to_all(
        sums.reshape(OWN, 32, RA), "expert", split_axis=0, concat_axis=0, tiled=True
    ).reshape(OWN * 32, RA)

    y_shape = shape((TOK, RB))
    y0, y1, y2, y3, mix = pl.pallas_call(
        pick_pairs,
        out_shape=[y_shape] * 4 + [shape((8, TOK), F32)],
        compiler_params=params(),
        cost_estimate=cost(4e8, 3e6),
        name="pick_pairs",
    )(dest, part_back)
    ys = (y0, shift(y1, 1), shift(y2, 2), shift(y3, -1))
    mixes = (mix, shift(mix, 1), shift(mix, 2), shift(mix, -1))

    gate_grad, up_grad, down_grad = pl.pallas_call(
        grads,
        grid=(LOC,),
        in_specs=act_specs + [leading(OWN * CAP, QH)] * 3,
        out_specs=[leading(D, QH), leading(D, QH), leading(QH, D)],
        out_shape=[shape((LOC, D, QH)), shape((LOC, D, QH)), shape((LOC, QH, D))],
        scratch_shapes=act_scratch,
        compiler_params=params(),
        cost_estimate=cost(3.3e9, 30e6),
        name="grads",
    )(*act_in, h, dg, du)

    input_grad, mix_t = pl.pallas_call(
        finish,
        out_shape=[shape((TOK, QF)), shape((2, TOK), F32)],
        compiler_params=params(),
        cost_estimate=cost(4e8, 3e6),
        name="finish",
    )(dest, weights, back, *ys, *mixes)
    return (input_grad, mix_t.T, gate_grad, up_grad, down_grad)


def solution(mesh):
    return jax.shard_map(
        on_device,
        mesh=mesh,
        in_specs=(
            P("expert", "hidden"),
            P("expert", "hidden"),
            P("expert", None),
            P("expert", None),
            P("expert", None, "hidden"),
            P("expert", None, "hidden"),
            P("expert", "hidden", None),
        ),
        out_specs=(
            P("expert", "hidden"),
            P("expert", None),
            P("expert", None, "hidden"),
            P("expert", None, "hidden"),
            P("expert", "hidden", None),
        ),
        check_vma=False,
    )
```

time: 341 us -> 186 us (0.55)
  waiting for transfers between devices: 180 us -> 61.6 us
  matrix products: 41.2 us -> 0 us
  Pallas kernels: 0 us -> 31 us
  starting transfers between devices: 31 us -> 61.9 us
  local copies, waits for them, and re-layouts: 44.7 us -> 26.7 us
  between operations: 14.1 us -> 0.88 us
  blocking collectives: 12.8 us -> 0 us
  other arithmetic: 13 us -> 1.48 us
    reduce_scatter x2 -> x0, waiting for transfers between devices: 80.4 us -> none  [return_slots(): lax.psum_scatter(partial_value.astype(jnp.bfloat16), 'hidden', scatter_di...]
    ppermute x0 -> x21, waiting for transfers between devices: none -> 61.2 us  [shift(): return lax.ppermute(x, 'hidden', [(i, (i + d) % NZ) for i in range(NZ)])]
    all_to_all x4, waiting for transfers between devices: 58.3 us -> 0.36 us  [the longest x1 0.35 us: on_device(): got = lax.all_to_all(pay, 'expert', split_axis=0, concat_axis=0, tiled=True)]
    dot_general x9 -> x0, matrix products: 41.2 us -> none  [the longest x1 5.93 us: on_device(): jnp.einsum('erd,erf->edf', x_slots, dg, preferred_element_type=jnp.float32)]
    all_gather x2 -> x0, waiting for transfers between devices: 40.4 us -> none  [the longest x1 25.2 us: on_device(): lax.all_gather(cotangent, 'hidden', axis=1, tiled=True)]
    gather x6 -> x0, local copies, waits for them, and re-layouts: 33 us -> none  [the longest x1 10.2 us: on_device(): full_cot[token_of].astype(jnp.float32) * weight_of[:, None]]
    pallas_call x0 -> x6, Pallas kernels: none -> 31 us  [the longest x1 12.9 us: on_device(): pl.pallas_call(middle, grid=(LOC,), in_specs=act_specs + [leading(D, QH),...]
    ppermute x0 -> x21, starting transfers between devices: none -> 27.7 us  [shift(): return lax.ppermute(x, 'hidden', [(i, (i + d) % NZ) for i in range(NZ)])]
  transfers between devices with their start and end apart: 8 -> 25, of which waited for: 6 -> 11; matrix products, arithmetic and copies ran while one was open for 19% -> 4% of each run, Pallas kernels for 0% -> 8%
where the time goes in v1:
time: 186 us; the launch traced here: 183 us
  starting transfers between devices  61.9 us (33%)
  waiting for transfers between devices  61.6 us (33%)
  Pallas kernels  31 us (17%)
  local copies, waits for them, and re-layouts  26.7 us (14%)
    ppermute x21, waiting for transfers between devices, shift(): return lax.ppermute(x, 'hidden', [(i, (i + d) % NZ) for i in range(NZ)])  61.2 us
    ppermute x21, starting transfers between devices, shift(): return lax.ppermute(x, 'hidden', [(i, (i + d) % NZ) for i in range(NZ)])  27.7 us
    unnamed x78, local copies, waits for them, and re-layouts  23.2 us
    pallas_call x1, Pallas kernels, on_device(): pl.pallas_call(middle, grid=(LOC,), in_specs=act_specs + [leading(D, QH),...  12.9 us
    all_to_all x1, starting transfers between devices, on_device(): lax.all_to_all(part.reshape(OWN, 32, WR), 'expert', split_axis=0, concat_...  9.22 us
    pallas_call x1, Pallas kernels, on_device(): pl.pallas_call(grads, grid=(LOC,), in_specs=act_specs + [leading(OWN * CA...  9.12 us
    all_to_all x1, starting transfers between devices, on_device(): got = lax.all_to_all(pay, 'expert', split_axis=0, concat_axis=0, tiled=True)  8.72 us
    all_to_all x1, starting transfers between devices, on_device(): lax.all_to_all(sums.reshape(OWN, 32, RA), 'expert', split_axis=0, concat_...  8.41 us
  transfers between devices with their start and end apart: 25, of which 11 were waited for; matrix products, arithmetic and copies ran while one was open for 4% of the time, Pallas kernels for 8%

profile of v1, /device:TPU:1, one launch (start us, length us, event | category | flops | bytes accessed | tf_op | source)
XLA Modules:
  0.0 183.5 jit_solution(15264885017564353459)
XLA Ops:
  3.9 2.6 %route_first.1 = (bf16[32,32,640]{2,1,0:T(8,128)(2,1)}, s32[2,256]{1,0:T(2,128)S(1)}) custom-call(s32[2,256]{1,0:T(2,128)S(1)} %bitcast.21, f32[2,256]{1,0:T(2,128)S(1)} %bitcast.18, bf16[256,512]{1,0:T(8,128)(2,1)S(1)} %copy-done.25, bf16[256,512]{1,0:T(8,128)(2,1)S(1)} %copy-done.11), custom_call_target="tpu_custom_call" | custom-call | flops 500000000 | bytes 4000000 | tf_op jit(solution)/shard_map/route_first/pallas_call | solution.py:209
  6.5 8.7 %all-to-all-start = ((bf16[32,32,640]{2,1,0:T(8,128)(2,1)}), bf16[32,32,640]{2,1,0:T(8,128)(2,1)S(1)}, u32[]{:S(2)}, u32[]{:S(2)}) async-start(bf16[32,32,640]{2,1,0:T(8,128)(2,1)} %get-tuple-element.29), calls=%async_computation | async-start | bytes 2621440 | tf_op jit(solution)/shard_map/all_to_all | solution.py:220
  15.2 3.7 %collective-permute-start.7 = (bf16[256,512]{1,0:T(8,128)(2,1)S(1)}, bf16[256,512]{1,0:T(8,128)(2,1)S(1)}, u32[]{:S(2)}, u32[]{:S(2)}) collective-permute-start(bf16[256,512]{1,0:T(8,128)(2,1)S(1)} %copy-done.12), channel_id=1, source_target_pairs={{0,2},{1,3},{2,0},{3,1},{4,6},{5,7},{6,4},{7,5},{8,10},{9,11},{10,... | collective-permute-start | bytes 786440 | tf_op jit(solution)/shard_map/ppermute | solution.py:34
  20.4 5.1 %collective-permute-done.7.c2 = bf16[256,512]{1,0:T(8,128)(2,1)S(1)} collective-permute-done((bf16[256,512]{1,0:T(8,128)(2,1)S(1)}, bf16[256,512]{1,0:T(8,128)(2,1)S(1)}, u32[]{:S(2)}, u32[]{:S(2)}) %collective-permute-start.7) | collective-permute-done | bytes 262176 | tf_op jit(solution)/shard_map/ppermute | solution.py:34
  25.5 6.0 %collective-permute-done.6.c1 = bf16[256,512]{1,0:T(8,128)(2,1)S(1)} collective-permute-done((bf16[256,512]{1,0:T(8,128)(2,1)S(1)}, bf16[256,512]{1,0:T(8,128)(2,1)S(1)}, u32[]{:S(2)}, u32[]{:S(2)}) %collective-permute-start.6) | collective-permute-done | bytes 262176 | tf_op jit(solution)/shard_map/ppermute | solution.py:34
  31.5 3.1 %route_rest.1 = bf16[32,32,1536]{2,1,0:T(8,128)(2,1)} custom-call(s32[2,256]{1,0:T(2,128)S(1)} %get-tuple-element.28.dest, f32[2,256]{1,0:T(2,128)S(1)} %bitcast.19, bf16[256,512]{1,0:T(8,128)(2,1)S(1)} %copy-done.12, bf16[256,512]{1,0:T(8,128)(2,1)S(1)} %collective-permute-done.6.c1, bf16[256,512]{1,0:T(8,128)(2,1)S(1)} %collective-permute-done.7.c2, ...), custom_call_target="tpu_custom_call" | custom-call | flops 800000000 | bytes 6000000 | tf_op jit(solution)/shard_map/route_rest/pallas_call | solution.py:222
  35.0 7.8 %all-to-all-start.1 = ((bf16[32,32,1536]{2,1,0:T(8,128)(2,1)}), bf16[32,32,1536]{2,1,0:T(8,128)(2,1)}, u32[]{:S(2)}, u32[]{:S(2)}) async-start(bf16[32,32,1536]{2,1,0:T(8,128)(2,1)} %route_rest.1), calls=%async_computation.1 | async-start | bytes 6291456 | tf_op jit(solution)/shard_map/all_to_all | solution.py:232
  44.0 2.3 %collective-permute-start.3 = (bf16[16,4,8,640]{3,2,1,0:T(8,128)(2,1)}, bf16[16,4,8,640]{3,2,1,0:T(8,128)(2,1)}, u32[]{:S(2)}, u32[]{:S(2)}) collective-permute-start(bf16[16,4,8,640]{3,2,1,0:T(8,128)(2,1)} %get-tuple-element.51), channel_id=1, source_target_pairs={{0,3},{1,0},{2,1},{3,2},{4,7},{5,4},{6,5},{7,6},{8,11},{9,8},{10,9... | collective-permute-start | bytes 1966088 | tf_op jit(solution)/shard_map/ppermute | solution.py:34
  46.3 2.7 %collective-permute-start.2 = (bf16[16,4,8,640]{3,2,1,0:T(8,128)(2,1)}, bf16[16,4,8,640]{3,2,1,0:T(8,128)(2,1)}, u32[]{:S(2)}, u32[]{:S(2)}) collective-permute-start(bf16[16,4,8,640]{3,2,1,0:T(8,128)(2,1)} %get-tuple-element.52), channel_id=1, source_target_pairs={{0,3},{1,0},{2,1},{3,2},{4,7},{5,4},{6,5},{7,6},{8,11},{9,8},{10,9... | collective-permute-start | bytes 1966088 | tf_op jit(solution)/shard_map/ppermute | solution.py:34
  49.0 11.5 %collective-permute-done.3 = bf16[16,4,8,640]{3,2,1,0:T(8,128)(2,1)} collective-permute-done((bf16[16,4,8,640]{3,2,1,0:T(8,128)(2,1)}, bf16[16,4,8,640]{3,2,1,0:T(8,128)(2,1)}, u32[]{:S(2)}, u32[]{:S(2)}) %collective-permute-start.3) | collective-permute-done | bytes 655392 | tf_op jit(solution)/shard_map/ppermute | solution.py:34
  60.4 3.4 %collective-permute-start.5 = (bf16[16,4,8,640]{3,2,1,0:T(8,128)(2,1)}, bf16[16,4,8,640]{3,2,1,0:T(8,128)(2,1)S(1)}, u32[]{:S(2)}, u32[]{:S(2)}) collective-permute-start(bf16[16,4,8,640]{3,2,1,0:T(8,128)(2,1)} %collective-permute-done.3), channel_id=1, source_target_pairs={{0,3},{1,0},{2,1},{3,2},{4,7},{5,4},{6,5},{7,6},{8,11},{9,8},{10,9... | collective-permute-start | bytes 1966088 | tf_op jit(solution)/shard_map/ppermute | solution.py:34
  65.0 9.4 %collective-permute-done.2 = bf16[16,4,8,640]{3,2,1,0:T(8,128)(2,1)} collective-permute-done((bf16[16,4,8,640]{3,2,1,0:T(8,128)(2,1)}, bf16[16,4,8,640]{3,2,1,0:T(8,128)(2,1)}, u32[]{:S(2)}, u32[]{:S(2)}) %collective-permute-start.2) | collective-permute-done | bytes 655392 | tf_op jit(solution)/shard_map/ppermute | solution.py:34
  78.8 9.8 %collective-permute-done.5.far_b = bf16[16,4,8,640]{3,2,1,0:T(8,128)(2,1)S(1)} collective-permute-done((bf16[16,4,8,640]{3,2,1,0:T(8,128)(2,1)}, bf16[16,4,8,640]{3,2,1,0:T(8,128)(2,1)S(1)}, u32[]{:S(2)}, u32[]{:S(2)}) %collective-permute-start.5) | collective-permute-done | bytes 655392 | tf_op jit(solution)/shard_map/ppermute | solution.py:34
  88.5 3.0 %collective-permute-done.4.far_a = bf16[16,4,8,640]{3,2,1,0:T(8,128)(2,1)S(1)} collective-permute-done((bf16[16,4,8,640]{3,2,1,0:T(8,128)(2,1)}, bf16[16,4,8,640]{3,2,1,0:T(8,128)(2,1)S(1)}, u32[]{:S(2)}, u32[]{:S(2)}) %collective-permute-start.4) | collective-permute-done | bytes 655392 | tf_op jit(solution)/shard_map/ppermute | solution.py:34
  93.5 12.9 %middle.1 = (bf16[32,4,8,384]{3,2,1,0:T(8,128)(2,1)S(1)}, bf16[16,4,8,384]{3,2,1,0:T(8,128)(2,1)S(1)}, bf16[16,4,8,384]{3,2,1,0:T(8,128)(2,1)S(1)}, bf16[16,4,8,...) custom-call(s32[1]{0:T(128)} %bitcast.2.z_ref, ...), custom_call_target="tpu_custom_call" | custom-call | flops 5400000000 | bytes 27000000 | tf_op jit(solution)/shard_map/middle/pallas_call | solution.py:257
  111.1 2.7 %collective-permute-start.13 = (bf16[16,4,8,384]{3,2,1,0:T(8,128)(2,1)}, bf16[16,4,8,384]{3,2,1,0:T(8,128)(2,1)S(1)}, u32[]{:S(2)}, u32[]{:S(2)}) collective-permute-start(bf16[16,4,8,384]{3,2,1,0:T(8,128)(2,1)} %get-tuple-element.36), channel_id=1, source_target_pairs={{0,3},{1,0},{2,1},{3,2},{4,7},{5,4},{6,5},{7,6},{8,11},{9,8},{10,9... | collective-permute-start | bytes 1179656 | tf_op jit(solution)/shard_map/ppermute | solution.py:34
  113.8 9.2 %all-to-all-start.3 = ((bf16[32,32,640]{2,1,0:T(8,128)(2,1)}), bf16[32,32,640]{2,1,0:T(8,128)(2,1)}, u32[]{:S(2)}, u32[]{:S(2)}) async-start(bf16[32,32,640]{2,1,0:T(8,128)(2,1)} %bitcast.22), calls=%async_computation.3 | async-start | bytes 2621440 | tf_op jit(solution)/shard_map/all_to_all | solution.py:277
  124.9 2.7 %collective-permute-start.14 = (bf16[16,4,8,384]{3,2,1,0:T(8,128)(2,1)S(1)}, bf16[16,4,8,384]{3,2,1,0:T(8,128)(2,1)S(1)}, u32[]{:S(2)}, u32[]{:S(2)}) collective-permute-start(bf16[16,4,8,384]{3,2,1,0:T(8,128)(2,1)S(1)} %add_convert_fusion.1), channel_id=1, source_target_pairs={{0,3},{1,0},{2,1},{3,2},{4,7},{5,4},{6,5},{7,6},{8,11},{9,8},{10,9... | collective-permute-start | bytes 1179656 | tf_op jit(solution)/shard_map/ppermute | solution.py:34
  127.6 6.0 %collective-permute-done.11 = bf16[16,4,8,384]{3,2,1,0:T(8,128)(2,1)S(1)} collective-permute-done((bf16[16,4,8,384]{3,2,1,0:T(8,128)(2,1)S(1)}, bf16[16,4,8,384]{3,2,1,0:T(8,128)(2,1)S(1)}, u32[]{:S(2)}, u32[]{:S(2)}) %collective-permute-start.11) | collective-permute-done | bytes 393248 | tf_op jit(solution)/shard_map/ppermute | solution.py:34
  134.9 8.3 %collective-permute-done.10 = bf16[16,4,8,384]{3,2,1,0:T(8,128)(2,1)S(1)} collective-permute-done((bf16[16,4,8,384]{3,2,1,0:T(8,128)(2,1)S(1)}, bf16[16,4,8,384]{3,2,1,0:T(8,128)(2,1)S(1)}, u32[]{:S(2)}, u32[]{:S(2)}) %collective-permute-start.10) | collective-permute-done | bytes 393248 | tf_op jit(solution)/shard_map/ppermute | solution.py:34
  144.5 8.4 %all-to-all-start.2 = ((bf16[32,32,384]{2,1,0:T(8,128)(2,1)}), bf16[32,32,384]{2,1,0:T(8,128)(2,1)S(1)}, u32[]{:S(2)}, u32[]{:S(2)}) async-start(bf16[32,32,384]{2,1,0:T(8,128)(2,1)} %maximum_bitcast_fusion), calls=%async_computation.2 | async-start | bytes 1572864 | tf_op jit(solution)/shard_map/all_to_all | solution.py:284
  152.9 2.1 %pick_pairs.1 = (bf16[256,128]{1,0:T(8,128)(2,1)S(1)}, bf16[256,128]{1,0:T(8,128)(2,1)S(1)}, bf16[256,128]{1,0:T(8,128)(2,1)S(1)}, bf16[256,128]{1,0:T(8,128)(2,1)S(1)}, f32[8,256]{1,0:T(8,128)S(1)}) custom-call(s32[2,256]{1,0:T(2,128)S(1)} %get-tuple-element.28.dest, bf16[1024,640]{1,0:T(8,128)(2,1)} %bitcast.10.back), custom_call_target="tpu_custom_call" | custom-call | flops 400000000 | bytes 3000000 | tf_op jit(solution)/shard_map/pick_pairs/pallas_call | solution.py:289
  157.9 3.1 %collective-permute-start.16 = (bf16[256,128]{1,0:T(8,128)(2,1)S(1)}, bf16[256,128]{1,0:T(8,128)(2,1)S(1)}, u32[]{:S(2)}, u32[]{:S(2)}) collective-permute-start(bf16[256,128]{1,0:T(8,128)(2,1)S(1)} %get-tuple-element.40), channel_id=1, source_target_pairs={{0,2},{1,3},{2,0},{3,1},{4,6},{5,7},{6,4},{7,5},{8,10},{9,11},{10,... | collective-permute-start | bytes 196616 | tf_op jit(solution)/shard_map/ppermute | solution.py:34
  167.6 9.1 %grads.1 = (bf16[4,2048,256]{2,1,0:T(8,128)(2,1)}, bf16[4,2048,256]{2,1,0:T(8,128)(2,1)}, bf16[4,256,2048]{2,1,0:T(8,128)(2,1)}) custom-call(s32[1]{0:T(128)} %bitcast.2.z_ref, bf16[32,4,8,640]{3,2,1,0:T(8,128)(2,1)S(1)} %bitcast.16, bf16[32,4,8,640]{3,2,1,0:T(8,128)(2,1)S(1)} %copy-done.3, bf16[32,4,8,640]{3,2,1,0:T(8,128)(2,1)} %copy-done.37, ...), custom_call_target="tpu_custom_call" | custom-call | flops 3300000000 | bytes 30000000 | tf_op jit(solution)/shard_map/grads/pallas_call | solution.py:299
  (117 shorter events, 39.0 us)
Async XLA Ops:
  6.5 28.5 %all-to-all-start = ((bf16[32,32,640]{2,1,0:T(8,128)(2,1)}), bf16[32,32,640]{2,1,0:T(8,128)(2,1)S(1)}, u32[]{:S(2)}, u32[]{:S(2)}) async-start(bf16[32,32,640]{2,1,0:T(8,128)(2,1)} %get-tuple-element.29), calls=%async_computation | async-start | bytes 2621440 | tf_op jit(solution)/shard_map/all_to_all | solution.py:220
  15.2 10.3 %collective-permute-start.7 = (bf16[256,512]{1,0:T(8,128)(2,1)S(1)}, bf16[256,512]{1,0:T(8,128)(2,1)S(1)}, u32[]{:S(2)}, u32[]{:S(2)}) collective-permute-start(bf16[256,512]{1,0:T(8,128)(2,1)S(1)} %copy-done.12), channel_id=1, source_target_pairs={{0,2},{1,3},{2,0},{3,1},{4,6},{5,7},{6,4},{7,5},{8,10},{9,11},{10,... | collective-permute-start | bytes 786440 | tf_op jit(solution)/shard_map/ppermute | solution.py:34
  18.9 12.6 %collective-permute-start.6 = (bf16[256,512]{1,0:T(8,128)(2,1)S(1)}, bf16[256,512]{1,0:T(8,128)(2,1)S(1)}, u32[]{:S(2)}, u32[]{:S(2)}) collective-permute-start(bf16[256,512]{1,0:T(8,128)(2,1)S(1)} %copy-done.12), channel_id=1, source_target_pairs={{0,3},{1,0},{2,1},{3,2},{4,7},{5,4},{6,5},{7,6},{8,11},{9,8},{10,9... | collective-permute-start | bytes 786440 | tf_op jit(solution)/shard_map/ppermute | solution.py:34
  19.3 12.2 %collective-permute-start.8 = (bf16[256,512]{1,0:T(8,128)(2,1)S(1)}, bf16[256,512]{1,0:T(8,128)(2,1)S(1)}, u32[]{:S(2)}, u32[]{:S(2)}) collective-permute-start(bf16[256,512]{1,0:T(8,128)(2,1)S(1)} %copy-done.12), channel_id=1, source_target_pairs={{0,1},{1,2},{2,3},{3,0},{4,5},{5,6},{6,7},{7,4},{8,9},{9,10},{10,1... | collective-permute-start | bytes 786440 | tf_op jit(solution)/shard_map/ppermute | solution.py:34
  35.0 57.4 %all-to-all-start.1 = ((bf16[32,32,1536]{2,1,0:T(8,128)(2,1)}), bf16[32,32,1536]{2,1,0:T(8,128)(2,1)}, u32[]{:S(2)}, u32[]{:S(2)}) async-start(bf16[32,32,1536]{2,1,0:T(8,128)(2,1)} %route_rest.1), calls=%async_computation.1 | async-start | bytes 6291456 | tf_op jit(solution)/shard_map/all_to_all | solution.py:232
  44.0 16.5 %collective-permute-start.3 = (bf16[16,4,8,640]{3,2,1,0:T(8,128)(2,1)}, bf16[16,4,8,640]{3,2,1,0:T(8,128)(2,1)}, u32[]{:S(2)}, u32[]{:S(2)}) collective-permute-start(bf16[16,4,8,640]{3,2,1,0:T(8,128)(2,1)} %get-tuple-element.51), channel_id=1, source_target_pairs={{0,3},{1,0},{2,1},{3,2},{4,7},{5,4},{6,5},{7,6},{8,11},{9,8},{10,9... | collective-permute-start | bytes 1966088 | tf_op jit(solution)/shard_map/ppermute | solution.py:34
  46.3 17.6 %collective-permute-start = (bf16[16,4,8,640]{3,2,1,0:T(8,128)(2,1)}, bf16[16,4,8,640]{3,2,1,0:T(8,128)(2,1)}, u32[]{:S(2)}, u32[]{:S(2)}) collective-permute-start(bf16[16,4,8,640]{3,2,1,0:T(8,128)(2,1)} %get-tuple-element.52), channel_id=1, source_target_pairs={{0,1},{1,2},{2,3},{3,0},{4,5},{5,6},{6,7},{7,4},{8,9},{9,10},{10,1... | collective-permute-start | bytes 1966088 | tf_op jit(solution)/shard_map/ppermute | solution.py:34
  46.3 28.2 %collective-permute-start.2 = (bf16[16,4,8,640]{3,2,1,0:T(8,128)(2,1)}, bf16[16,4,8,640]{3,2,1,0:T(8,128)(2,1)}, u32[]{:S(2)}, u32[]{:S(2)}) collective-permute-start(bf16[16,4,8,640]{3,2,1,0:T(8,128)(2,1)} %get-tuple-element.52), channel_id=1, source_target_pairs={{0,3},{1,0},{2,1},{3,2},{4,7},{5,4},{6,5},{7,6},{8,11},{9,8},{10,9... | collective-permute-start | bytes 1966088 | tf_op jit(solution)/shard_map/ppermute | solution.py:34
  49.0 28.6 %collective-permute-start.1 = (bf16[16,4,8,640]{3,2,1,0:T(8,128)(2,1)}, bf16[16,4,8,640]{3,2,1,0:T(8,128)(2,1)}, u32[]{:S(2)}, u32[]{:S(2)}) collective-permute-start(bf16[16,4,8,640]{3,2,1,0:T(8,128)(2,1)} %get-tuple-element.51), channel_id=1, source_target_pairs={{0,1},{1,2},{2,3},{3,0},{4,5},{5,6},{6,7},{7,4},{8,9},{9,10},{10,1... | collective-permute-start | bytes 1966088 | tf_op jit(solution)/shard_map/ppermute | solution.py:34
  60.4 28.1 %collective-permute-start.5 = (bf16[16,4,8,640]{3,2,1,0:T(8,128)(2,1)}, bf16[16,4,8,640]{3,2,1,0:T(8,128)(2,1)S(1)}, u32[]{:S(2)}, u32[]{:S(2)}) collective-permute-start(bf16[16,4,8,640]{3,2,1,0:T(8,128)(2,1)} %collective-permute-done.3), channel_id=1, source_target_pairs={{0,3},{1,0},{2,1},{3,2},{4,7},{5,4},{6,5},{7,6},{8,11},{9,8},{10,9... | collective-permute-start | bytes 1966088 | tf_op jit(solution)/shard_map/ppermute | solution.py:34
  63.9 27.7 %collective-permute-start.4 = (bf16[16,4,8,640]{3,2,1,0:T(8,128)(2,1)}, bf16[16,4,8,640]{3,2,1,0:T(8,128)(2,1)S(1)}, u32[]{:S(2)}, u32[]{:S(2)}) collective-permute-start(bf16[16,4,8,640]{3,2,1,0:T(8,128)(2,1)} %collective-permute-done), channel_id=1, source_target_pairs={{0,1},{1,2},{2,3},{3,0},{4,5},{5,6},{6,7},{7,4},{8,9},{9,10},{10,1... | collective-permute-start | bytes 1966088 | tf_op jit(solution)/shard_map/ppermute | solution.py:34
  111.1 13.5 %collective-permute-start.9 = (bf16[16,4,8,384]{3,2,1,0:T(8,128)(2,1)}, bf16[16,4,8,384]{3,2,1,0:T(8,128)(2,1)S(1)}, u32[]{:S(2)}, u32[]{:S(2)}) collective-permute-start(bf16[16,4,8,384]{3,2,1,0:T(8,128)(2,1)} %get-tuple-element.32), channel_id=1, source_target_pairs={{0,1},{1,2},{2,3},{3,0},{4,5},{5,6},{6,7},{7,4},{8,9},{9,10},{10,1... | collective-permute-start | bytes 1179656 | tf_op jit(solution)/shard_map/ppermute | solution.py:34
  111.1 13.7 %collective-permute-start.13 = (bf16[16,4,8,384]{3,2,1,0:T(8,128)(2,1)}, bf16[16,4,8,384]{3,2,1,0:T(8,128)(2,1)S(1)}, u32[]{:S(2)}, u32[]{:S(2)}) collective-permute-start(bf16[16,4,8,384]{3,2,1,0:T(8,128)(2,1)} %get-tuple-element.36), channel_id=1, source_target_pairs={{0,3},{1,0},{2,1},{3,2},{4,7},{5,4},{6,5},{7,6},{8,11},{9,8},{10,9... | collective-permute-start | bytes 1179656 | tf_op jit(solution)/shard_map/ppermute | solution.py:34
  113.8 30.7 %all-to-all-start.3 = ((bf16[32,32,640]{2,1,0:T(8,128)(2,1)}), bf16[32,32,640]{2,1,0:T(8,128)(2,1)}, u32[]{:S(2)}, u32[]{:S(2)}) async-start(bf16[32,32,640]{2,1,0:T(8,128)(2,1)} %bitcast.22), calls=%async_computation.3 | async-start | bytes 2621440 | tf_op jit(solution)/shard_map/all_to_all | solution.py:277
  123.0 10.6 %collective-permute-start.11 = (bf16[16,4,8,384]{3,2,1,0:T(8,128)(2,1)S(1)}, bf16[16,4,8,384]{3,2,1,0:T(8,128)(2,1)S(1)}, u32[]{:S(2)}, u32[]{:S(2)}) collective-permute-start(bf16[16,4,8,384]{3,2,1,0:T(8,128)(2,1)S(1)} %copy-done.24), channel_id=1, source_target_pairs={{0,3},{1,0},{2,1},{3,2},{4,7},{5,4},{6,5},{7,6},{8,11},{9,8},{10,9... | collective-permute-start | bytes 1179656 | tf_op jit(solution)/shard_map/ppermute | solution.py:34
  123.1 11.8 %collective-permute-start.12 = (bf16[16,4,8,384]{3,2,1,0:T(8,128)(2,1)S(1)}, bf16[16,4,8,384]{3,2,1,0:T(8,128)(2,1)S(1)}, u32[]{:S(2)}, u32[]{:S(2)}) collective-permute-start(bf16[16,4,8,384]{3,2,1,0:T(8,128)(2,1)S(1)} %copy-done.22), channel_id=1, source_target_pairs={{0,1},{1,2},{2,3},{3,0},{4,5},{5,6},{6,7},{7,4},{8,9},{9,10},{10,1... | collective-permute-start | bytes 1179656 | tf_op jit(solution)/shard_map/ppermute | solution.py:34
  124.7 18.6 %collective-permute-start.10 = (bf16[16,4,8,384]{3,2,1,0:T(8,128)(2,1)S(1)}, bf16[16,4,8,384]{3,2,1,0:T(8,128)(2,1)S(1)}, u32[]{:S(2)}, u32[]{:S(2)}) collective-permute-start(bf16[16,4,8,384]{3,2,1,0:T(8,128)(2,1)S(1)} %add_convert_fusion.3), channel_id=1, source_target_pairs={{0,1},{1,2},{2,3},{3,0},{4,5},{5,6},{6,7},{7,4},{8,9},{9,10},{10,1... | collective-permute-start | bytes 1179656 | tf_op jit(solution)/shard_map/ppermute | solution.py:34
  124.9 18.4 %collective-permute-start.14 = (bf16[16,4,8,384]{3,2,1,0:T(8,128)(2,1)S(1)}, bf16[16,4,8,384]{3,2,1,0:T(8,128)(2,1)S(1)}, u32[]{:S(2)}, u32[]{:S(2)}) collective-permute-start(bf16[16,4,8,384]{3,2,1,0:T(8,128)(2,1)S(1)} %add_convert_fusion.1), channel_id=1, source_target_pairs={{0,3},{1,0},{2,1},{3,2},{4,7},{5,4},{6,5},{7,6},{8,11},{9,8},{10,9... | collective-permute-start | bytes 1179656 | tf_op jit(solution)/shard_map/ppermute | solution.py:34
  144.5 34.0 %all-to-all-start.2 = ((bf16[32,32,384]{2,1,0:T(8,128)(2,1)}), bf16[32,32,384]{2,1,0:T(8,128)(2,1)S(1)}, u32[]{:S(2)}, u32[]{:S(2)}) async-start(bf16[32,32,384]{2,1,0:T(8,128)(2,1)} %maximum_bitcast_fusion), calls=%async_computation.2 | async-start | bytes 1572864 | tf_op jit(solution)/shard_map/all_to_all | solution.py:284
  155.1 21.5 %collective-permute-start.19 = (f32[8,256]{1,0:T(8,128)S(1)}, f32[8,256]{1,0:T(8,128)S(1)}, u32[]{:S(2)}, u32[]{:S(2)}) collective-permute-start(f32[8,256]{1,0:T(8,128)S(1)} %get-tuple-element.42.m0), channel_id=1, source_target_pairs={{0,2},{1,3},{2,0},{3,1},{4,6},{5,7},{6,4},{7,5},{8,10},{9,11},{10,... | collective-permute-start | bytes 24584 | tf_op jit(solution)/shard_map/ppermute | solution.py:34
  157.1 20.2 %collective-permute-start.18 = (f32[8,256]{1,0:T(8,128)S(1)}, f32[8,256]{1,0:T(8,128)S(1)}, u32[]{:S(2)}, u32[]{:S(2)}) collective-permute-start(f32[8,256]{1,0:T(8,128)S(1)} %get-tuple-element.42.m0), channel_id=1, source_target_pairs={{0,1},{1,2},{2,3},{3,0},{4,5},{5,6},{6,7},{7,4},{8,9},{9,10},{10,1... | collective-permute-start | bytes 24584 | tf_op jit(solution)/shard_map/ppermute | solution.py:34
  157.1 20.8 %collective-permute-start.15 = (bf16[256,128]{1,0:T(8,128)(2,1)S(1)}, bf16[256,128]{1,0:T(8,128)(2,1)S(1)}, u32[]{:S(2)}, u32[]{:S(2)}) collective-permute-start(bf16[256,128]{1,0:T(8,128)(2,1)S(1)} %get-tuple-element.39), channel_id=1, source_target_pairs={{0,1},{1,2},{2,3},{3,0},{4,5},{5,6},{6,7},{7,4},{8,9},{9,10},{10,1... | collective-permute-start | bytes 196616 | tf_op jit(solution)/shard_map/ppermute | solution.py:34
  157.9 20.0 %collective-permute-start.16 = (bf16[256,128]{1,0:T(8,128)(2,1)S(1)}, bf16[256,128]{1,0:T(8,128)(2,1)S(1)}, u32[]{:S(2)}, u32[]{:S(2)}) collective-permute-start(bf16[256,128]{1,0:T(8,128)(2,1)S(1)} %get-tuple-element.40), channel_id=1, source_target_pairs={{0,2},{1,3},{2,0},{3,1},{4,6},{5,7},{6,4},{7,5},{8,10},{9,11},{10,... | collective-permute-start | bytes 196616 | tf_op jit(solution)/shard_map/ppermute | solution.py:34
  160.9 16.9 %collective-permute-start.17 = (bf16[256,128]{1,0:T(8,128)(2,1)S(1)}, bf16[256,128]{1,0:T(8,128)(2,1)S(1)}, u32[]{:S(2)}, u32[]{:S(2)}) collective-permute-start(bf16[256,128]{1,0:T(8,128)(2,1)S(1)} %get-tuple-element.41), channel_id=1, source_target_pairs={{0,3},{1,0},{2,1},{3,2},{4,7},{5,4},{6,5},{7,6},{8,11},{9,8},{10,9... | collective-permute-start | bytes 196616 | tf_op jit(solution)/shard_map/ppermute | solution.py:34
  (39 other events, 213.7 us)

commit v2 on v1

v2 whole, which is shorter than its diff:
```python
import jax
import jax.numpy as jnp
from jax import lax
from jax.experimental import pallas as pl
from jax.experimental.pallas import tpu as pltpu
from jax.sharding import PartitionSpec as P

D = 2048
SCALE = D ** (-0.5)
OWN = 32
NZ = 4
LOC = 4
CAP = 8
TOK = 256
QF = D // NZ
QH = 256
RA = 384
RB = QF - RA
WR = NZ * RB + 128
BF = jnp.bfloat16
F32 = jnp.float32
VMEM = 63 * 1024 * 1024


def dot(a, b, ca, cb):
    return lax.dot_general(a, b, (((ca,), (cb,)), ((), ())), preferred_element_type=F32)


def shift(x, d):
    return lax.ppermute(x, "hidden", [(i, (i + d) % NZ) for i in range(NZ)])


def params(**kw):
    return pltpu.CompilerParams(vmem_limit_bytes=VMEM, **kw)


def slots_of(dest, base, rows):
    slot = lax.broadcasted_iota(jnp.int32, (rows, TOK), 0) + base
    return slot == dest[0:1, :], slot == dest[1:2, :]


def route_first(zones, tokens, pay, dest_out, dest):
    step = pl.program_id(0)

    @pl.when(step == 0)
    def _():
        expert = lax.broadcasted_iota(jnp.int32, (OWN * LOC, TOK), 0)
        hit0 = expert == zones[0:1, :]
        hit1 = expert == zones[1:2, :]
        both = jnp.where(hit0 | hit1, 1.0, 0.0).astype(BF)
        earlier = lax.broadcasted_iota(jnp.int32, (TOK, TOK), 0) < lax.broadcasted_iota(
            jnp.int32, (TOK, TOK), 1
        )
        count = dot(both, jnp.where(earlier, 1.0, 0.0).astype(BF), 1, 0)
        rank0 = jnp.sum(jnp.where(hit0, count, 0.0), axis=0, keepdims=True)
        rank1 = jnp.sum(jnp.where(hit1, count, 0.0), axis=0, keepdims=True)
        dest[0:1, :] = zones[0:1, :] * CAP + rank0.astype(jnp.int32)
        dest[1:2, :] = zones[1:2, :] * CAP + rank1.astype(jnp.int32)
        dest_out[...] = dest[...]

    at0, at1 = slots_of(dest, step * 256, 256)
    pick = jnp.where(at0 | at1, 1.0, 0.0).astype(BF)
    pay[...] = dot(pick, tokens[...], 1, 0).astype(BF).reshape(8, 32, QF)


def route_rest(z_ref, dest, weights, c0, c1, c2, c3, pay):
    at0, at1 = slots_of(dest, pl.program_id(0) * 256, 256)
    pick = jnp.where(at0 | at1, 1.0, 0.0).astype(BF)
    w = jnp.sum(
        jnp.where(at0, weights[0:1, :], 0.0) + jnp.where(at1, weights[1:2, :], 0.0),
        axis=1,
        keepdims=True,
    )
    for off, c in enumerate((c0, c1, c2, c3)):
        dy = (dot(pick, c[...], 1, 0) * w).astype(BF)
        q = lax.rem(z_ref[0] + off, NZ)
        pay[:, :, pl.ds(pl.multiple_of(q * QF, QF), QF)] = dy.reshape(8, 32, QF)


def merged(v):
    n, r, f = v.shape
    return v.astype(F32).reshape(n * r, f).astype(BF)


def parted(v):
    return v.reshape(v.shape[0] // CAP, CAP, v.shape[1]).astype(BF)


def gates(
    z_ref, own, left_a, left_b, right_a, right_b, far_a, far_b, wg, wu,
    x_out, h_out, silu_out, slope_out, xs,
):
    pieces = ((0, (own,)), (3, (left_a, left_b)), (1, (right_a, right_b)), (2, (far_a, far_b)))
    for off, parts in pieces:
        q = lax.rem(z_ref[0] + off, NZ)
        row = 0
        for part in parts:
            n = part.shape[0] * CAP
            xs[q, row : row + n, :] = merged(part[:, 0])
            row += n
    g = u = 0.0
    for q in range(NZ):
        rows = slice(q * QF, (q + 1) * QF)
        x_out[0, :, rows] = xs[q]
        g = g + dot(xs[q], wg[0, rows, :], 1, 0)
        u = u + dot(xs[q], wu[0, rows, :], 1, 0)
    sig = jax.nn.sigmoid(g)
    silu = g * sig
    h_out[0] = (silu * u).astype(BF)
    silu_out[0] = silu
    slope_out[0] = u * sig * (1.0 + g * (1.0 - sig))


def middle(
    z_ref, rest, h_in, silu, slope, wg, wu, wd,
    o0, o1t, o1b, o2t, o2b, o3t, o3b, part_out, dg_out, du_out,
):
    z = z_ref[0]
    h = h_in[0]
    dh = dot(merged(rest[:, 0]), wd[0], 1, 1)
    dg = (dh * slope[0]).astype(BF)
    du = (dh * silu[0]).astype(BF)
    dg_out[0] = dg
    du_out[0] = du
    mix = jnp.sum(h.astype(F32) * dh, axis=1, keepdims=True)
    high = mix.astype(BF).astype(F32)
    lane = lax.broadcasted_iota(jnp.int32, (OWN * CAP, 128), 1)
    mix = jnp.where(lane == 0, high, jnp.where(lane == 1, mix - high, 0.0))
    part_out[:, 0, :, NZ * RB :] = parted(mix)
    for off, outs in ((2, (o2t, o2b)), (1, (o1t, o1b)), (3, (o3t, o3b)), (0, (o0,))):
        rows = pl.ds(pl.multiple_of(lax.rem(z + off, NZ) * QF, QF), QF)
        dx = dot(dg, wg[0, rows, :], 1, 1) + dot(du, wu[0, rows, :], 1, 1)
        row = 0
        for out in outs:
            n = out.shape[0] * CAP
            out[:, 0] = parted(dx[row : row + n, :RA])
            row += n
        part_out[:, 0, :, off * RB : (off + 1) * RB] = parted(dx[:, RA:])


def grads(x, rest, h, dg, du, gate_out, up_out, down_out):
    gate_out[0] = dot(x[0], dg[0], 0, 0).astype(BF)
    up_out[0] = dot(x[0], du[0], 0, 0).astype(BF)
    down_out[0] = dot(h[0], merged(rest[:, 0]), 0, 0).astype(BF)


def pick_pairs(dest, back, y0, y1, y2, y3):
    at0, at1 = slots_of(dest, 0, OWN * LOC * CAP)
    one0 = jnp.where(at0, 1.0, 0.0).astype(BF)
    one1 = jnp.where(at1, 1.0, 0.0).astype(BF)
    y = dot(one0 + one1, back[:, : NZ * RB], 0, 0).astype(BF)
    m0 = dot(back[:, NZ * RB :], one0, 0, 0)
    m1 = dot(back[:, NZ * RB :], one1, 0, 0)
    rows = [m[:8, c : c + RB] for m in (m0, m1) for c in range(0, TOK, RB)]
    mix = jnp.concatenate(rows, axis=0).astype(BF)
    for off, out in enumerate((y0, y1, y2, y3)):
        out[:TOK, :] = y[:, off * RB : (off + 1) * RB]
        out[TOK:, :] = mix


def finish(dest, weights, back, y0, y1, y2, y3, grad_out, mix_out):
    at0, at1 = slots_of(dest, 0, OWN * LOC * CAP)
    pick = jnp.where(at0 | at1, 1.0, 0.0).astype(BF)
    grad_out[:, :RA] = dot(pick, back[...], 0, 0).astype(BF)
    y = (y0[...].astype(F32) + y2[...].astype(F32)) + (y1[...].astype(F32) + y3[...].astype(F32))
    grad_out[:, RA:] = y[:TOK].astype(BF)
    for k in range(2):
        for c in range(2):
            row = TOK + 8 * (2 * k + c)
            lanes = slice(c * RB, (c + 1) * RB)
            total = y[row : row + 1] + y[row + 1 : row + 2]
            mix_out[k : k + 1, lanes] = total * SCALE / weights[k : k + 1, lanes]


def shape(dims, dtype=BF):
    return jax.ShapeDtypeStruct(dims, dtype)


def cost(flops, size):
    return pl.CostEstimate(flops=int(flops), bytes_accessed=int(size), transcendentals=0)


def whole(dims):
    return pl.BlockSpec(dims, lambda i: (0,) * len(dims))


def by_expert(n, width):
    return pl.BlockSpec((n, 1, CAP, width), lambda e: (0, e, 0, 0))


def leading(*dims):
    return pl.BlockSpec((1,) + dims, lambda e: (e,) + (0,) * len(dims))


def on_device(tokens, cotangent, zone_ids, gate_weights, gate_proj, up_proj, down_proj):
    z = lax.axis_index("hidden").astype(jnp.int32).reshape(1)
    zones, weights = zone_ids.T, gate_weights.T
    cots = (cotangent, shift(cotangent, -1), shift(cotangent, 2), shift(cotangent, 1))

    smem = pl.BlockSpec(memory_space=pltpu.SMEM)
    pay, dest = pl.pallas_call(
        route_first,
        grid=(4,),
        in_specs=[whole((2, TOK)), whole((TOK, QF))],
        out_specs=[pl.BlockSpec((8, 32, QF), lambda i: (i, 0, 0)), whole((2, TOK))],
        out_shape=[shape((OWN, 32, QF)), shape((2, TOK), jnp.int32)],
        scratch_shapes=[pltpu.VMEM((2, TOK), jnp.int32)],
        compiler_params=params(),
        cost_estimate=cost(5e8, 4e6),
        name="route_first",
    )(zones, tokens)
    got = lax.all_to_all(pay, "expert", split_axis=0, concat_axis=0, tiled=True)

    pay_rest = pl.pallas_call(
        route_rest,
        grid=(4,),
        in_specs=[smem, whole((2, TOK)), whole((2, TOK))] + [whole((TOK, QF))] * 4,
        out_specs=pl.BlockSpec((8, 32, D), lambda i: (i, 0, 0)),
        out_shape=shape((OWN, 32, D)),
        compiler_params=params(),
        cost_estimate=cost(8e8, 6e6),
        name="route_rest",
    )(z, dest, weights, *cots)
    rest = lax.all_to_all(pay_rest, "expert", split_axis=0, concat_axis=0, tiled=True)
    rest = rest.reshape(OWN, LOC, CAP, D)

    half = OWN // 2
    got = got.reshape(OWN, LOC, CAP, QF)
    top, bot = got[:half], got[half:]
    left_t = shift(top, 1)
    right_b = shift(bot, -1)
    left_b = shift(bot, 1)
    right_t = shift(top, -1)
    far_t = shift(left_t, 1)
    far_b = shift(right_b, -1)

    rows = OWN * CAP
    hid, hid_f = shape((LOC, rows, QH)), shape((LOC, rows, QH), F32)
    hid_spec = leading(rows, QH)
    x_slots, h, silu, slope = pl.pallas_call(
        gates,
        grid=(LOC,),
        in_specs=[smem, by_expert(OWN, QF)] + [by_expert(half, QF)] * 6 + [leading(D, QH)] * 2,
        out_specs=[leading(rows, D), hid_spec, hid_spec, hid_spec],
        out_shape=[shape((LOC, rows, D)), hid, hid_f, hid_f],
        scratch_shapes=[pltpu.VMEM((NZ, rows, QF), BF)],
        compiler_params=params(),
        cost_estimate=cost(2.2e9, 19e6),
        name="gates",
    )(z, got, left_t, left_b, right_t, right_b, far_t, far_b, gate_proj, up_proj)

    whole_part = shape((OWN, LOC, CAP, RA))
    half_part = shape((half, LOC, CAP, RA))
    o0, o1t, o1b, o2t, o2b, o3t, o3b, part, dg, du = pl.pallas_call(
        middle,
        grid=(LOC,),
        in_specs=[smem, by_expert(OWN, D)] + [hid_spec] * 3
        + [leading(D, QH), leading(D, QH), leading(QH, D)],
        out_specs=[by_expert(OWN, RA)] + [by_expert(half, RA)] * 6 + [by_expert(OWN, WR)]
        + [hid_spec] * 2,
        out_shape=[whole_part] + [half_part] * 6 + [shape((OWN, LOC, CAP, WR)), hid, hid],
        compiler_params=params(),
        cost_estimate=cost(3.3e9, 27e6),
        name="middle",
    )(z, rest, h, silu, slope, gate_proj, up_proj, down_proj)

    relay_t = shift(o2t, 1)
    relay_b = shift(o2b, -1)
    from_l_b = shift(o1b, 1)
    from_r_t = shift(o3t, -1)
    gate_grad, up_grad, down_grad = pl.pallas_call(
        grads,
        grid=(LOC,),
        in_specs=[leading(rows, D), by_expert(OWN, D)] + [hid_spec] * 3,
        out_specs=[leading(D, QH), leading(D, QH), leading(QH, D)],
        out_shape=[shape((LOC, D, QH)), shape((LOC, D, QH)), shape((LOC, QH, D))],
        compiler_params=params(),
        cost_estimate=cost(3.3e9, 30e6),
        name="grads",
    )(x_slots, rest, h, dg, du)
    relay_t, relay_b, down_grad = lax.optimization_barrier((relay_t, relay_b, down_grad))
    from_l_t = shift((o1t.astype(F32) + relay_t.astype(F32)).astype(BF), 1)
    from_r_b = shift((o3b.astype(F32) + relay_b.astype(F32)).astype(BF), -1)

    part_back = lax.all_to_all(
        part.reshape(OWN, 32, WR), "expert", split_axis=0, concat_axis=0, tiled=True
    ).reshape(OWN * 32, WR)

    sum_t = o0[:half].astype(F32) + from_l_t.astype(F32) + from_r_t.astype(F32)
    sum_b = o0[half:].astype(F32) + from_l_b.astype(F32) + from_r_b.astype(F32)
    sums = jnp.concatenate([sum_t.astype(BF), sum_b.astype(BF)], axis=0)
    back = lax.all_to_all(
        sums.reshape(OWN, 32, RA), "expert", split_axis=0, concat_axis=0, tiled=True
    ).reshape(OWN * 32, RA)

    y_shape = shape((TOK + 32, RB))
    y0, y1, y2, y3 = pl.pallas_call(
        pick_pairs,
        out_shape=[y_shape] * 4,
        compiler_params=params(),
        cost_estimate=cost(4e8, 3e6),
        name="pick_pairs",
    )(dest, part_back)
    ys = (y0, shift(y1, 1), shift(y2, 2), shift(y3, -1))

    input_grad, mix_t = pl.pallas_call(
        finish,
        out_shape=[shape((TOK, QF)), shape((2, TOK), F32)],
        compiler_params=params(),
        cost_estimate=cost(4e8, 3e6),
        name="finish",
    )(dest, weights, back, *ys)
    return (input_grad, mix_t.T, gate_grad, up_grad, down_grad)


def solution(mesh):
    return jax.shard_map(
        on_device,
        mesh=mesh,
        in_specs=(
            P("expert", "hidden"),
            P("expert", "hidden"),
            P("expert", None),
            P("expert", None),
            P("expert", None, "hidden"),
            P("expert", None, "hidden"),
            P("expert", "hidden", None),
        ),
        out_specs=(
            P("expert", "hidden"),
            P("expert", None),
            P("expert", None, "hidden"),
            P("expert", None, "hidden"),
            P("expert", "hidden", None),
        ),
        check_vma=False,
    )
```

time: 186 us -> 173 us (0.930); the launches traced: 183 us -> 173 us
  local copies, waits for them, and re-layouts: 26.7 us -> 3.84 us
  Pallas kernels: 31 us -> 42.7 us
  starting transfers between devices: 61.9 us -> 56.9 us
  other arithmetic: 1.48 us -> 4.83 us
  waiting for transfers between devices: 61.6 us -> 63.5 us
    unnamed x78 -> x26, local copies, waits for them, and re-layouts: 23.2 us -> 2.57 us
    pallas_call x4 -> x5, Pallas kernels: 27.2 us -> 36.9 us  [the longest x1 11.3 us: on_device(): pl.pallas_call(middle, grid=(LOC,), in_specs=[smem, by_expert(OWN, D)] +...]
    ppermute x21 -> x18, waiting for transfers between devices: 61.2 us -> 56.6 us  [shift(): return lax.ppermute(x, 'hidden', [(i, (i + d) % NZ) for i in range(NZ)])]
    ppermute x21 -> x18, starting transfers between devices: 27.7 us -> 23.2 us  [shift(): return lax.ppermute(x, 'hidden', [(i, (i + d) % NZ) for i in range(NZ)])]
    all_to_all x1, waiting for transfers between devices: 0.01 us -> 4.5 us  [on_device(): lax.all_to_all(sums.reshape(OWN, 32, RA), 'expert', split_axis=0, concat_...]
    all_to_all x1, waiting for transfers between devices: 0.01 us -> 2.45 us  [on_device(): lax.all_to_all(pay_rest, 'expert', split_axis=0, concat_axis=0, tiled=True)]
    concatenate x2 -> x0, local copies, waits for them, and re-layouts: 2.36 us -> none  [the longest x1 1.18 us: on_device(): right = jnp.concatenate([right_t, right_b], axis=0)]
  transfers between devices with their start and end apart: 25 -> 22, of which waited for: 11 -> 11; matrix products, arithmetic and copies ran while one was open for 4% -> 4% of each run, Pallas kernels for 8% -> 15%
where the time goes in v2:
time: 173 us
  waiting for transfers between devices  63.5 us (37%)
  starting transfers between devices  56.9 us (33%)
  Pallas kernels  42.7 us (25%)
  other arithmetic  4.83 us (3%)
  local copies, waits for them, and re-layouts  3.84 us (2%)
    ppermute x18, waiting for transfers between devices, shift(): return lax.ppermute(x, 'hidden', [(i, (i + d) % NZ) for i in range(NZ)])  56.6 us
    ppermute x18, starting transfers between devices, shift(): return lax.ppermute(x, 'hidden', [(i, (i + d) % NZ) for i in range(NZ)])  23.2 us
    pallas_call x1, Pallas kernels, on_device(): pl.pallas_call(middle, grid=(LOC,), in_specs=[smem, by_expert(OWN, D)] +...  11.3 us
    pallas_call x1, Pallas kernels, on_device(): pl.pallas_call(grads, grid=(LOC,), in_specs=[leading(rows, D), by_expert(...  9.66 us
    all_to_all x1, starting transfers between devices, on_device(): lax.all_to_all(sums.reshape(OWN, 32, RA), 'expert', split_axis=0, concat_...  9.09 us
    all_to_all x1, starting transfers between devices, on_device(): got = lax.all_to_all(pay, 'expert', split_axis=0, concat_axis=0, tiled=True)  8.64 us
    pallas_call x1, Pallas kernels, on_device(): pl.pallas_call(gates, grid=(LOC,), in_specs=[smem, by_expert(OWN, QF)] +...  8.52 us
    all_to_all x1, starting transfers between devices, on_device(): lax.all_to_all(pay_rest, 'expert', split_axis=0, concat_axis=0, tiled=True)  8.21 us
  transfers between devices with their start and end apart: 22, of which 11 were waited for; matrix products, arithmetic and copies ran while one was open for 4% of the time, Pallas kernels for 15%

profile of v2, /device:TPU:1, one launch (start us, length us, event | category | flops | bytes accessed | tf_op | source)
XLA Modules:
  0.0 172.6 jit_solution(6904695091382670639)
XLA Ops:
  0.6 3.4 %route_first.1 = (bf16[32,32,512]{2,1,0:T(8,128)(2,1)}, s32[2,256]{1,0:T(2,128)}) custom-call(s32[2,256]{1,0:T(2,128)} %bitcast.19, bf16[256,512]{1,0:T(8,128)(2,1)} %tokens.1), custom_call_target="tpu_custom_call" | custom-call | flops 500000000 | bytes 4000000 | tf_op jit(solution)/shard_map/route_first/pallas_call | solution.py:201
  4.1 8.6 %all-to-all-start.1 = ((bf16[32,32,512]{2,1,0:T(8,128)(2,1)}), bf16[32,32,512]{2,1,0:T(8,128)(2,1)}, u32[]{:S(2)}, u32[]{:S(2)}) async-start(bf16[32,32,512]{2,1,0:T(8,128)(2,1)} %get-tuple-element.34), calls=%async_computation.1 | async-start | bytes 2097152 | tf_op jit(solution)/shard_map/all_to_all | solution.py:212
  12.7 3.7 %collective-permute-start.1 = (bf16[256,512]{1,0:T(8,128)(2,1)}, bf16[256,512]{1,0:T(8,128)(2,1)S(1)}, u32[]{:S(2)}, u32[]{:S(2)}) collective-permute-start(bf16[256,512]{1,0:T(8,128)(2,1)} %c0.1), channel_id=1, source_target_pairs={{0,2},{1,3},{2,0},{3,1},{4,6},{5,7},{6,4},{7,5},{8,10},{9,11},{10,... | collective-permute-start | bytes 786440 | tf_op jit(solution)/shard_map/ppermute | solution.py:30
  17.8 5.3 %collective-permute-done.1.c2 = bf16[256,512]{1,0:T(8,128)(2,1)S(1)} collective-permute-done((bf16[256,512]{1,0:T(8,128)(2,1)}, bf16[256,512]{1,0:T(8,128)(2,1)S(1)}, u32[]{:S(2)}, u32[]{:S(2)}) %collective-permute-start.1) | collective-permute-done | bytes 262176 | tf_op jit(solution)/shard_map/ppermute | solution.py:30
  23.2 5.9 %collective-permute-done.c1 = bf16[256,512]{1,0:T(8,128)(2,1)S(1)} collective-permute-done((bf16[256,512]{1,0:T(8,128)(2,1)}, bf16[256,512]{1,0:T(8,128)(2,1)S(1)}, u32[]{:S(2)}, u32[]{:S(2)}) %collective-permute-start) | collective-permute-done | bytes 262176 | tf_op jit(solution)/shard_map/ppermute | solution.py:30
  29.9 4.5 %route_rest.1 = bf16[32,32,2048]{2,1,0:T(8,128)(2,1)} custom-call(s32[1]{0:T(128)} %bitcast.2.z_ref, s32[2,256]{1,0:T(2,128)} %get-tuple-element.33.dest, f32[2,256]{1,0:T(2,128)} %bitcast.17, bf16[256,512]{1,0:T(8,128)(2,1)} %c0.1, bf16[256,512]{1,0:T(8,128)(2,1)} %copy-done.9, bf16[256,512]{1,0:T(8,128)(2,1)} %copy-done.8, bf16[256,512]{1,0:T(8,128)(2,1)} %copy-done.10), custom_call_target="tpu_custom_call" | custom-call | flops 800000000 | bytes 6000000 | tf_op jit(solution)/shard_map/route_rest/pallas_call | solution.py:214
  34.5 8.2 %all-to-all-start = ((bf16[32,32,2048]{2,1,0:T(8,128)(2,1)}), bf16[32,32,2048]{2,1,0:T(8,128)(2,1)}, u32[]{:S(2)}, u32[]{:S(2)}) async-start(bf16[32,32,2048]{2,1,0:T(8,128)(2,1)} %route_rest.1), calls=%async_computation | async-start | bytes 8388608 | tf_op jit(solution)/shard_map/all_to_all | solution.py:224
  46.4 2.7 %collective-permute-start.5 = (bf16[16,4,8,512]{3,2,1,0:T(8,128)(2,1)S(1)}, bf16[16,4,8,512]{3,2,1,0:T(8,128)(2,1)S(1)}, u32[]{:S(2)}, u32[]{:S(2)}) collective-permute-start(bf16[16,4,8,512]{3,2,1,0:T(8,128)(2,1)S(1)} %get-tuple-element.62), channel_id=1, source_target_pairs={{0,3},{1,0},{2,1},{3,2},{4,7},{5,4},{6,5},{7,6},{8,11},{9,8},{10,9... | collective-permute-start | bytes 1572872 | tf_op jit(solution)/shard_map/ppermute | solution.py:30
  49.1 8.3 %collective-permute-done.6.right_b = bf16[16,4,8,512]{3,2,1,0:T(8,128)(2,1)S(1)} collective-permute-done((bf16[16,4,8,512]{3,2,1,0:T(8,128)(2,1)S(1)}, bf16[16,4,8,512]{3,2,1,0:T(8,128)(2,1)S(1)}, u32[]{:S(2)}, u32[]{:S(2)}) %collective-permute-start.6) | collective-permute-done | bytes 524320 | tf_op jit(solution)/shard_map/ppermute | solution.py:30
  57.4 3.5 %collective-permute-start.8 = (bf16[16,4,8,512]{3,2,1,0:T(8,128)(2,1)S(1)}, bf16[16,4,8,512]{3,2,1,0:T(8,128)(2,1)S(1)}, u32[]{:S(2)}, u32[]{:S(2)}) collective-permute-start(bf16[16,4,8,512]{3,2,1,0:T(8,128)(2,1)S(1)} %collective-permute-done.6.right_b), channel_id=1, source_target_pairs={{0,3},{1,0},{2,1},{3,2},{4,7},{5,4},{6,5},{7,6},{8,11},{9,8},{10,9... | collective-permute-start | bytes 1572872 | tf_op jit(solution)/shard_map/ppermute | solution.py:30
  60.9 10.9 %collective-permute-done.4.left_b = bf16[16,4,8,512]{3,2,1,0:T(8,128)(2,1)S(1)} collective-permute-done((bf16[16,4,8,512]{3,2,1,0:T(8,128)(2,1)S(1)}, bf16[16,4,8,512]{3,2,1,0:T(8,128)(2,1)S(1)}, u32[]{:S(2)}, u32[]{:S(2)}) %collective-permute-start.4) | collective-permute-done | bytes 524320 | tf_op jit(solution)/shard_map/ppermute | solution.py:30
  71.8 8.0 %collective-permute-done.8.far_b = bf16[16,4,8,512]{3,2,1,0:T(8,128)(2,1)S(1)} collective-permute-done((bf16[16,4,8,512]{3,2,1,0:T(8,128)(2,1)S(1)}, bf16[16,4,8,512]{3,2,1,0:T(8,128)(2,1)S(1)}, u32[]{:S(2)}, u32[]{:S(2)}) %collective-permute-start.8) | collective-permute-done | bytes 524320 | tf_op jit(solution)/shard_map/ppermute | solution.py:30
  79.8 3.2 %collective-permute-done.7.far_a = bf16[16,4,8,512]{3,2,1,0:T(8,128)(2,1)S(1)} collective-permute-done((bf16[16,4,8,512]{3,2,1,0:T(8,128)(2,1)S(1)}, bf16[16,4,8,512]{3,2,1,0:T(8,128)(2,1)S(1)}, u32[]{:S(2)}, u32[]{:S(2)}) %collective-permute-start.7) | collective-permute-done | bytes 524320 | tf_op jit(solution)/shard_map/ppermute | solution.py:30
  83.9 8.5 %gates.1 = (bf16[4,256,2048]{2,1,0:T(8,128)(2,1)}, bf16[4,256,256]{2,1,0:T(8,128)(2,1)}, f32[4,256,256]{2,1,0:T(8,128)}, f32[4,256,256]{2,1,0:T(8,128)}) custom-call(s32[1]{0:T(128)} %bitcast.2.z_ref, bf16[32,4,8,512]{3,2,1,0:T(8,128)(2,1)} %bitcast.4.own, bf16[16,4,8,512]{3,2,1,0:T(8,128)(2,1)} %copy-done.3, bf16[16,4,8,512]{3,2,1,0:T(8,128)(2,1)} %copy-done.4, ...), custom_call_target="tpu_custom_call" | custom-call | flops 2200000000 | bytes 19000000 | tf_op jit(solution)/shard_map/gates/pallas_call | solution.py:240
  92.4 2.5 %all-to-all-done = bf16[32,32,2048]{2,1,0:T(8,128)(2,1)} async-done(((bf16[32,32,2048]{2,1,0:T(8,128)(2,1)}), bf16[32,32,2048]{2,1,0:T(8,128)(2,1)}, u32[]{:S(2)}, u32[]{:S(2)}) %all-to-all-start) | async-done | bytes 4194336 | tf_op jit(solution)/shard_map/all_to_all | solution.py:224
  94.9 11.3 %middle.1 = (bf16[32,4,8,384]{3,2,1,0:T(8,128)(2,1)}, bf16[16,4,8,384]{3,2,1,0:T(8,128)(2,1)}, bf16[16,4,8,384]{3,2,1,0:T(8,128)(2,1)}, bf16[16,4,8,384]{3,2,1,0...) custom-call(s32[1]{0:T(128)} %bitcast.2.z_ref, ...), custom_call_target="tpu_custom_call" | custom-call | flops 3300000000 | bytes 27000000 | tf_op jit(solution)/shard_map/middle/pallas_call | solution.py:254
  109.0 7.7 %all-to-all-start.3 = ((bf16[32,32,640]{2,1,0:T(8,128)(2,1)}), bf16[32,32,640]{2,1,0:T(8,128)(2,1)}, u32[]{:S(2)}, u32[]{:S(2)}) async-start(bf16[32,32,640]{2,1,0:T(8,128)(2,1)} %bitcast.15), calls=%async_computation.3 | async-start | bytes 2621440 | tf_op jit(solution)/shard_map/all_to_all | solution.py:285
  118.3 9.7 %grads.1 = (bf16[4,2048,256]{2,1,0:T(8,128)(2,1)}, bf16[4,2048,256]{2,1,0:T(8,128)(2,1)}, bf16[4,256,2048]{2,1,0:T(8,128)(2,1)}) custom-call(bf16[4,256,2048]{2,1,0:T(8,128)(2,1)} %get-tuple-element.42.x, bf16[32,4,8,2048]{3,2,1,0:T(8,128)(2,1)} %bitcast.3.rest, bf16[4,256,256]{2,1,0:T(8,128)(2,1)} %get-tuple-element.35.h_in.h, ...), custom_call_target="tpu_custom_call" | custom-call | flops 3300000000 | bytes 30000000 | tf_op jit(solution)/shard_map/grads/pallas_call | solution.py:271
  132.9 6.2 %collective-permute-done.14 = bf16[16,4,8,384]{3,2,1,0:T(8,128)(2,1)S(1)} collective-permute-done((bf16[16,4,8,384]{3,2,1,0:T(8,128)(2,1)S(1)}, bf16[16,4,8,384]{3,2,1,0:T(8,128)(2,1)S(1)}, u32[]{:S(2)}, u32[]{:S(2)}) %collective-permute-start.14) | collective-permute-done | bytes 393248 | tf_op jit(solution)/shard_map/ppermute | solution.py:30
  139.1 4.4 %collective-permute-done.11 = bf16[16,4,8,384]{3,2,1,0:T(8,128)(2,1)S(1)} collective-permute-done((bf16[16,4,8,384]{3,2,1,0:T(8,128)(2,1)S(1)}, bf16[16,4,8,384]{3,2,1,0:T(8,128)(2,1)S(1)}, u32[]{:S(2)}, u32[]{:S(2)}) %collective-permute-start.11) | collective-permute-done | bytes 393248 | tf_op jit(solution)/shard_map/ppermute | solution.py:30
  145.9 9.1 %all-to-all-start.2 = ((bf16[32,32,384]{2,1,0:T(8,128)(2,1)}), bf16[32,32,384]{2,1,0:T(8,128)(2,1)S(1)}, u32[]{:S(2)}, u32[]{:S(2)}) async-start(bf16[32,32,384]{2,1,0:T(8,128)(2,1)} %maximum_bitcast_fusion), calls=%async_computation.2 | async-start | bytes 1572864 | tf_op jit(solution)/shard_map/all_to_all | solution.py:292
  155.0 2.8 %pick_pairs.1 = (bf16[288,128]{1,0:T(8,128)(2,1)}, bf16[288,128]{1,0:T(8,128)(2,1)}, bf16[288,128]{1,0:T(8,128)(2,1)}, bf16[288,128]{1,0:T(8,128)(2,1)}) custom-call(s32[2,256]{1,0:T(2,128)} %get-tuple-element.33.dest, bf16[1024,640]{1,0:T(8,128)(2,1)} %bitcast.10.back), custom_call_target="tpu_custom_call" | custom-call | flops 400000000 | bytes 3000000 | tf_op jit(solution)/shard_map/pick_pairs/pallas_call | solution.py:297
  160.5 4.3 %collective-permute-done.15.y1 = bf16[288,128]{1,0:T(8,128)(2,1)S(1)} collective-permute-done((bf16[288,128]{1,0:T(8,128)(2,1)}, bf16[288,128]{1,0:T(8,128)(2,1)S(1)}, u32[]{:S(2)}, u32[]{:S(2)}) %collective-permute-start.15) | collective-permute-done | bytes 73760 | tf_op jit(solution)/shard_map/ppermute | solution.py:30
  164.8 4.5 %all-to-all-done.2 = bf16[32,32,384]{2,1,0:T(8,128)(2,1)S(1)} async-done(((bf16[32,32,384]{2,1,0:T(8,128)(2,1)}), bf16[32,32,384]{2,1,0:T(8,128)(2,1)S(1)}, u32[]{:S(2)}, u32[]{:S(2)}) %all-to-all-start.2) | async-done | bytes 786464 | tf_op jit(solution)/shard_map/all_to_all | solution.py:292
  (58 shorter events, 24.4 us)
Async XLA Ops:
  4.1 30.4 %all-to-all-start.1 = ((bf16[32,32,512]{2,1,0:T(8,128)(2,1)}), bf16[32,32,512]{2,1,0:T(8,128)(2,1)}, u32[]{:S(2)}, u32[]{:S(2)}) async-start(bf16[32,32,512]{2,1,0:T(8,128)(2,1)} %get-tuple-element.34), calls=%async_computation.1 | async-start | bytes 2097152 | tf_op jit(solution)/shard_map/all_to_all | solution.py:212
  12.7 10.5 %collective-permute-start.1 = (bf16[256,512]{1,0:T(8,128)(2,1)}, bf16[256,512]{1,0:T(8,128)(2,1)S(1)}, u32[]{:S(2)}, u32[]{:S(2)}) collective-permute-start(bf16[256,512]{1,0:T(8,128)(2,1)} %c0.1), channel_id=1, source_target_pairs={{0,2},{1,3},{2,0},{3,1},{4,6},{5,7},{6,4},{7,5},{8,10},{9,11},{10,... | collective-permute-start | bytes 786440 | tf_op jit(solution)/shard_map/ppermute | solution.py:30
  16.4 12.7 %collective-permute-start = (bf16[256,512]{1,0:T(8,128)(2,1)}, bf16[256,512]{1,0:T(8,128)(2,1)S(1)}, u32[]{:S(2)}, u32[]{:S(2)}) collective-permute-start(bf16[256,512]{1,0:T(8,128)(2,1)} %c0.1), channel_id=1, source_target_pairs={{0,3},{1,0},{2,1},{3,2},{4,7},{5,4},{6,5},{7,6},{8,11},{9,8},{10,9... | collective-permute-start | bytes 786440 | tf_op jit(solution)/shard_map/ppermute | solution.py:30
  16.8 12.3 %collective-permute-start.2 = (bf16[256,512]{1,0:T(8,128)(2,1)}, bf16[256,512]{1,0:T(8,128)(2,1)S(1)}, u32[]{:S(2)}, u32[]{:S(2)}) collective-permute-start(bf16[256,512]{1,0:T(8,128)(2,1)} %c0.1), channel_id=1, source_target_pairs={{0,1},{1,2},{2,3},{3,0},{4,5},{5,6},{6,7},{7,4},{8,9},{9,10},{10,1... | collective-permute-start | bytes 786440 | tf_op jit(solution)/shard_map/ppermute | solution.py:30
  34.5 60.4 %all-to-all-start = ((bf16[32,32,2048]{2,1,0:T(8,128)(2,1)}), bf16[32,32,2048]{2,1,0:T(8,128)(2,1)}, u32[]{:S(2)}, u32[]{:S(2)}) async-start(bf16[32,32,2048]{2,1,0:T(8,128)(2,1)} %route_rest.1), calls=%async_computation | async-start | bytes 8388608 | tf_op jit(solution)/shard_map/all_to_all | solution.py:224
  44.0 13.4 %collective-permute-start.6 = (bf16[16,4,8,512]{3,2,1,0:T(8,128)(2,1)S(1)}, bf16[16,4,8,512]{3,2,1,0:T(8,128)(2,1)S(1)}, u32[]{:S(2)}, u32[]{:S(2)}) collective-permute-start(bf16[16,4,8,512]{3,2,1,0:T(8,128)(2,1)S(1)} %get-tuple-element.61), channel_id=1, source_target_pairs={{0,3},{1,0},{2,1},{3,2},{4,7},{5,4},{6,5},{7,6},{8,11},{9,8},{10,9... | collective-permute-start | bytes 1572872 | tf_op jit(solution)/shard_map/ppermute | solution.py:30
  46.4 14.5 %collective-permute-start.3 = (bf16[16,4,8,512]{3,2,1,0:T(8,128)(2,1)S(1)}, bf16[16,4,8,512]{3,2,1,0:T(8,128)(2,1)S(1)}, u32[]{:S(2)}, u32[]{:S(2)}) collective-permute-start(bf16[16,4,8,512]{3,2,1,0:T(8,128)(2,1)S(1)} %get-tuple-element.62), channel_id=1, source_target_pairs={{0,1},{1,2},{2,3},{3,0},{4,5},{5,6},{6,7},{7,4},{8,9},{9,10},{10,1... | collective-permute-start | bytes 1572872 | tf_op jit(solution)/shard_map/ppermute | solution.py:30
  46.4 25.4 %collective-permute-start.4 = (bf16[16,4,8,512]{3,2,1,0:T(8,128)(2,1)S(1)}, bf16[16,4,8,512]{3,2,1,0:T(8,128)(2,1)S(1)}, u32[]{:S(2)}, u32[]{:S(2)}) collective-permute-start(bf16[16,4,8,512]{3,2,1,0:T(8,128)(2,1)S(1)} %get-tuple-element.61), channel_id=1, source_target_pairs={{0,1},{1,2},{2,3},{3,0},{4,5},{5,6},{6,7},{7,4},{8,9},{9,10},{10,1... | collective-permute-start | bytes 1572872 | tf_op jit(solution)/shard_map/ppermute | solution.py:30
  46.4 25.4 %collective-permute-start.5 = (bf16[16,4,8,512]{3,2,1,0:T(8,128)(2,1)S(1)}, bf16[16,4,8,512]{3,2,1,0:T(8,128)(2,1)S(1)}, u32[]{:S(2)}, u32[]{:S(2)}) collective-permute-start(bf16[16,4,8,512]{3,2,1,0:T(8,128)(2,1)S(1)} %get-tuple-element.62), channel_id=1, source_target_pairs={{0,3},{1,0},{2,1},{3,2},{4,7},{5,4},{6,5},{7,6},{8,11},{9,8},{10,9... | collective-permute-start | bytes 1572872 | tf_op jit(solution)/shard_map/ppermute | solution.py:30
  57.4 26.5 %copy-start.2 = (bf16[16,4,8,512]{3,2,1,0:T(8,128)(2,1)}, bf16[16,4,8,512]{3,2,1,0:T(8,128)(2,1)S(1)}, u32[]{:S(2)}) copy-start(bf16[16,4,8,512]{3,2,1,0:T(8,128)(2,1)S(1)} %collective-permute-done.6.right_b) | copy-start | bytes 1572868
  57.4 22.5 %collective-permute-start.8 = (bf16[16,4,8,512]{3,2,1,0:T(8,128)(2,1)S(1)}, bf16[16,4,8,512]{3,2,1,0:T(8,128)(2,1)S(1)}, u32[]{:S(2)}, u32[]{:S(2)}) collective-permute-start(bf16[16,4,8,512]{3,2,1,0:T(8,128)(2,1)S(1)} %collective-permute-done.6.right_b), channel_id=1, source_target_pairs={{0,3},{1,0},{2,1},{3,2},{4,7},{5,4},{6,5},{7,6},{8,11},{9,8},{10,9... | collective-permute-start | bytes 1572872 | tf_op jit(solution)/shard_map/ppermute | solution.py:30
  60.9 22.1 %collective-permute-start.7 = (bf16[16,4,8,512]{3,2,1,0:T(8,128)(2,1)S(1)}, bf16[16,4,8,512]{3,2,1,0:T(8,128)(2,1)S(1)}, u32[]{:S(2)}, u32[]{:S(2)}) collective-permute-start(bf16[16,4,8,512]{3,2,1,0:T(8,128)(2,1)S(1)} %collective-permute-done.3.left_a), channel_id=1, source_target_pairs={{0,1},{1,2},{2,3},{3,0},{4,5},{5,6},{6,7},{7,4},{8,9},{9,10},{10,1... | collective-permute-start | bytes 1572872 | tf_op jit(solution)/shard_map/ppermute | solution.py:30
  106.2 21.7 %collective-permute-start.9 = (bf16[16,4,8,384]{3,2,1,0:T(8,128)(2,1)}, bf16[16,4,8,384]{3,2,1,0:T(8,128)(2,1)}, u32[]{:S(2)}, u32[]{:S(2)}) collective-permute-start(bf16[16,4,8,384]{3,2,1,0:T(8,128)(2,1)} %get-tuple-element.40), channel_id=1, source_target_pairs={{0,1},{1,2},{2,3},{3,0},{4,5},{5,6},{6,7},{7,4},{8,9},{9,10},{10,1... | collective-permute-start | bytes 1179656 | tf_op jit(solution)/shard_map/ppermute | solution.py:30
  107.0 21.0 %collective-permute-start.10 = (bf16[16,4,8,384]{3,2,1,0:T(8,128)(2,1)}, bf16[16,4,8,384]{3,2,1,0:T(8,128)(2,1)}, u32[]{:S(2)}, u32[]{:S(2)}) collective-permute-start(bf16[16,4,8,384]{3,2,1,0:T(8,128)(2,1)} %get-tuple-element.41), channel_id=1, source_target_pairs={{0,3},{1,0},{2,1},{3,2},{4,7},{5,4},{6,5},{7,6},{8,11},{9,8},{10,9... | collective-permute-start | bytes 1179656 | tf_op jit(solution)/shard_map/ppermute | solution.py:30
  109.0 36.9 %all-to-all-start.3 = ((bf16[32,32,640]{2,1,0:T(8,128)(2,1)}), bf16[32,32,640]{2,1,0:T(8,128)(2,1)}, u32[]{:S(2)}, u32[]{:S(2)}) async-start(bf16[32,32,640]{2,1,0:T(8,128)(2,1)} %bitcast.15), calls=%async_computation.3 | async-start | bytes 2621440 | tf_op jit(solution)/shard_map/all_to_all | solution.py:285
  116.7 16.1 %collective-permute-start.12 = (bf16[16,4,8,384]{3,2,1,0:T(8,128)(2,1)}, bf16[16,4,8,384]{3,2,1,0:T(8,128)(2,1)}, u32[]{:S(2)}, u32[]{:S(2)}) collective-permute-start(bf16[16,4,8,384]{3,2,1,0:T(8,128)(2,1)} %get-tuple-element.47), channel_id=1, source_target_pairs={{0,3},{1,0},{2,1},{3,2},{4,7},{5,4},{6,5},{7,6},{8,11},{9,8},{10,9... | collective-permute-start | bytes 1179656 | tf_op jit(solution)/shard_map/ppermute | solution.py:30
  117.9 14.9 %collective-permute-start.13 = (bf16[16,4,8,384]{3,2,1,0:T(8,128)(2,1)}, bf16[16,4,8,384]{3,2,1,0:T(8,128)(2,1)}, u32[]{:S(2)}, u32[]{:S(2)}) collective-permute-start(bf16[16,4,8,384]{3,2,1,0:T(8,128)(2,1)} %get-tuple-element.48), channel_id=1, source_target_pairs={{0,1},{1,2},{2,3},{3,0},{4,5},{5,6},{6,7},{7,4},{8,9},{9,10},{10,1... | collective-permute-start | bytes 1179656 | tf_op jit(solution)/shard_map/ppermute | solution.py:30
  118.3 25.3 %copy-start.1 = (bf16[32,4,8,384]{3,2,1,0:T(8,128)(2,1)S(1)}, bf16[32,4,8,384]{3,2,1,0:T(8,128)(2,1)}, u32[]{:S(2)}) copy-start(bf16[32,4,8,384]{3,2,1,0:T(8,128)(2,1)} %get-tuple-element.38) | copy-start | bytes 2359300
  129.2 10.0 %collective-permute-start.14 = (bf16[16,4,8,384]{3,2,1,0:T(8,128)(2,1)S(1)}, bf16[16,4,8,384]{3,2,1,0:T(8,128)(2,1)S(1)}, u32[]{:S(2)}, u32[]{:S(2)}) collective-permute-start(bf16[16,4,8,384]{3,2,1,0:T(8,128)(2,1)S(1)} %add_convert_fusion.1), channel_id=1, source_target_pairs={{0,3},{1,0},{2,1},{3,2},{4,7},{5,4},{6,5},{7,6},{8,11},{9,8},{10,9... | collective-permute-start | bytes 1179656 | tf_op jit(solution)/shard_map/ppermute | solution.py:30
  132.8 10.7 %collective-permute-start.11 = (bf16[16,4,8,384]{3,2,1,0:T(8,128)(2,1)S(1)}, bf16[16,4,8,384]{3,2,1,0:T(8,128)(2,1)S(1)}, u32[]{:S(2)}, u32[]{:S(2)}) collective-permute-start(bf16[16,4,8,384]{3,2,1,0:T(8,128)(2,1)S(1)} %add_convert_fusion.3), channel_id=1, source_target_pairs={{0,1},{1,2},{2,3},{3,0},{4,5},{5,6},{6,7},{7,4},{8,9},{9,10},{10,1... | collective-permute-start | bytes 1179656 | tf_op jit(solution)/shard_map/ppermute | solution.py:30
  145.9 23.3 %all-to-all-start.2 = ((bf16[32,32,384]{2,1,0:T(8,128)(2,1)}), bf16[32,32,384]{2,1,0:T(8,128)(2,1)S(1)}, u32[]{:S(2)}, u32[]{:S(2)}) async-start(bf16[32,32,384]{2,1,0:T(8,128)(2,1)} %maximum_bitcast_fusion), calls=%async_computation.2 | async-start | bytes 1572864 | tf_op jit(solution)/shard_map/all_to_all | solution.py:292
  157.8 6.9 %collective-permute-start.15 = (bf16[288,128]{1,0:T(8,128)(2,1)}, bf16[288,128]{1,0:T(8,128)(2,1)S(1)}, u32[]{:S(2)}, u32[]{:S(2)}) collective-permute-start(bf16[288,128]{1,0:T(8,128)(2,1)} %get-tuple-element.53), channel_id=1, source_target_pairs={{0,1},{1,2},{2,3},{3,0},{4,5},{5,6},{6,7},{7,4},{8,9},{9,10},{10,1... | collective-permute-start | bytes 221192 | tf_op jit(solution)/shard_map/ppermute | solution.py:30
  157.8 6.9 %collective-permute-start.16 = (bf16[288,128]{1,0:T(8,128)(2,1)}, bf16[288,128]{1,0:T(8,128)(2,1)S(1)}, u32[]{:S(2)}, u32[]{:S(2)}) collective-permute-start(bf16[288,128]{1,0:T(8,128)(2,1)} %get-tuple-element.54), channel_id=1, source_target_pairs={{0,2},{1,3},{2,0},{3,1},{4,6},{5,7},{6,4},{7,5},{8,10},{9,11},{10,... | collective-permute-start | bytes 221192 | tf_op jit(solution)/shard_map/ppermute | solution.py:30
  158.3 6.5 %collective-permute-start.17 = (bf16[288,128]{1,0:T(8,128)(2,1)}, bf16[288,128]{1,0:T(8,128)(2,1)}, u32[]{:S(2)}, u32[]{:S(2)}) collective-permute-start(bf16[288,128]{1,0:T(8,128)(2,1)} %get-tuple-element.55), channel_id=1, source_target_pairs={{0,3},{1,0},{2,1},{3,2},{4,7},{5,4},{6,5},{7,6},{8,11},{9,8},{10,9... | collective-permute-start | bytes 221192 | tf_op jit(solution)/shard_map/ppermute | solution.py:30
  (11 other events, 62.8 us)

commit v3 on v2

--- a/solution.py
+++ b/solution.py
@@ -113,7 +113,7 @@
 
 def middle(
     z_ref, rest, h_in, silu, slope, wg, wu, wd,
-    o0, o1t, o1b, o2t, o2b, o3t, o3b, part_out, dg_out, du_out,
+    o0t, o0b, o1t, o1b, o2t, o2b, o3t, o3b, part_out, dg_out, du_out,
 ):
     z = z_ref[0]
     h = h_in[0]
@@ -127,41 +127,52 @@
     lane = lax.broadcasted_iota(jnp.int32, (OWN * CAP, 128), 1)
     mix = jnp.where(lane == 0, high, jnp.where(lane == 1, mix - high, 0.0))
     part_out[:, 0, :, NZ * RB :] = parted(mix)
-    for off, outs in ((2, (o2t, o2b)), (1, (o1t, o1b)), (3, (o3t, o3b)), (0, (o0,))):
+    half = OWN * CAP // 2
+    for off, top, bot in ((2, o2t, o2b), (1, o1t, o1b), (3, o3t, o3b), (0, o0t, o0b)):
         rows = pl.ds(pl.multiple_of(lax.rem(z + off, NZ) * QF, QF), QF)
         dx = dot(dg, wg[0, rows, :], 1, 1) + dot(du, wu[0, rows, :], 1, 1)
-        row = 0
-        for out in outs:
-            n = out.shape[0] * CAP
-            out[:, 0] = parted(dx[row : row + n, :RA])
-            row += n
+        top[:, 0] = parted(dx[:half, :RA])
+        bot[:, 0] = parted(dx[half:, :RA])
         part_out[:, 0, :, off * RB : (off + 1) * RB] = parted(dx[:, RA:])
 
 
-def grads(x, rest, h, dg, du, gate_out, up_out, down_out):
+def relay_sums(a0, a1, b0, b1, a_out, b_out):
+    a_out[...] = (a0[...].astype(F32) + a1[...].astype(F32)).astype(BF)
+    b_out[...] = (b0[...].astype(F32) + b1[...].astype(F32)).astype(BF)
+
+
+def last_sums(a0, a1, a2, b0, b1, b2, out):
+    out[0] = (a0[...].astype(F32) + a1[...].astype(F32) + a2[...].astype(F32)).astype(BF)
+    out[1] = (b0[...].astype(F32) + b1[...].astype(F32) + b2[...].astype(F32)).astype(BF)
+
+
+def grads_down(dest, rest, h, down_out, pick_out):
+    at0, at1 = slots_of(dest, pl.program_id(0) * 256, 256)
+    pick_out[...] = jnp.where(at0 | at1, 1.0, 0.0).T.astype(BF)
+    down_out[0] = dot(h[0], merged(rest[:, 0]), 0, 0).astype(BF)
+
+
+def grads_up(x, dg, du, gate_out, up_out):
     gate_out[0] = dot(x[0], dg[0], 0, 0).astype(BF)
     up_out[0] = dot(x[0], du[0], 0, 0).astype(BF)
-    down_out[0] = dot(h[0], merged(rest[:, 0]), 0, 0).astype(BF)
-
-
-def pick_pairs(dest, back, y0, y1, y2, y3):
+
+
+def pick_pairs(dest, back, y0, y1, y2, y3, ys):
     at0, at1 = slots_of(dest, 0, OWN * LOC * CAP)
     one0 = jnp.where(at0, 1.0, 0.0).astype(BF)
     one1 = jnp.where(at1, 1.0, 0.0).astype(BF)
-    y = dot(one0 + one1, back[:, : NZ * RB], 0, 0).astype(BF)
+    ys[...] = dot(one0 + one1, back[:, : NZ * RB], 0, 0)
     m0 = dot(back[:, NZ * RB :], one0, 0, 0)
     m1 = dot(back[:, NZ * RB :], one1, 0, 0)
     rows = [m[:8, c : c + RB] for m in (m0, m1) for c in range(0, TOK, RB)]
     mix = jnp.concatenate(rows, axis=0).astype(BF)
     for off, out in enumerate((y0, y1, y2, y3)):
-        out[:TOK, :] = y[:, off * RB : (off + 1) * RB]
+        out[:TOK, :] = ys[:, off * RB : (off + 1) * RB].astype(BF)
         out[TOK:, :] = mix
 
 
-def finish(dest, weights, back, y0, y1, y2, y3, grad_out, mix_out):
-    at0, at1 = slots_of(dest, 0, OWN * LOC * CAP)
-    pick = jnp.where(at0 | at1, 1.0, 0.0).astype(BF)
-    grad_out[:, :RA] = dot(pick, back[...], 0, 0).astype(BF)
+def finish(pick, weights, back, y0, y1, y2, y3, grad_out, mix_out):
+    grad_out[:, :RA] = dot(pick[...], back[...], 1, 0).astype(BF)
     y = (y0[...].astype(F32) + y2[...].astype(F32)) + (y1[...].astype(F32) + y3[...].astype(F32))
     grad_out[:, RA:] = y[:TOK].astype(BF)
     for k in range(2):
@@ -249,18 +260,16 @@
         name="gates",
     )(z, got, left_t, left_b, right_t, right_b, far_t, far_b, gate_proj, up_proj)
 
-    whole_part = shape((OWN, LOC, CAP, RA))
     half_part = shape((half, LOC, CAP, RA))
-    o0, o1t, o1b, o2t, o2b, o3t, o3b, part, dg, du = pl.pallas_call(
+    o0t, o0b, o1t, o1b, o2t, o2b, o3t, o3b, part, dg, du = pl.pallas_call(
         middle,
         grid=(LOC,),
         in_specs=[smem, by_expert(OWN, D)] + [hid_spec] * 3
         + [leading(D, QH), leading(D, QH), leading(QH, D)],
-        out_specs=[by_expert(OWN, RA)] + [by_expert(half, RA)] * 6 + [by_expert(OWN, WR)]
-        + [hid_spec] * 2,
-        out_shape=[whole_part] + [half_part] * 6 + [shape((OWN, LOC, CAP, WR)), hid, hid],
-        compiler_params=params(),
-        cost_estimate=cost(3.3e9, 27e6),
+        out_specs=[by_expert(half, RA)] * 8 + [by_expert(OWN, WR)] + [hid_spec] * 2,
+        out_shape=[half_part] * 8 + [shape((OWN, LOC, CAP, WR)), hid, hid],
+        compiler_params=params(),
+        cost_estimate=cost(2.7e9, 27e6),
         name="middle",
     )(z, rest, h, silu, slope, gate_proj, up_proj, down_proj)
 
@@ -268,27 +277,59 @@
     relay_b = shift(o2b, -1)
     from_l_b = shift(o1b, 1)
     from_r_t = shift(o3t, -1)
-    gate_grad, up_grad, down_grad = pl.pallas_call(
-        grads,
-        grid=(LOC,),
-        in_specs=[leading(rows, D), by_expert(OWN, D)] + [hid_spec] * 3,
-        out_specs=[leading(D, QH), leading(D, QH), leading(QH, D)],
-        out_shape=[shape((LOC, D, QH)), shape((LOC, D, QH)), shape((LOC, QH, D))],
-        compiler_params=params(),
-        cost_estimate=cost(3.3e9, 30e6),
-        name="grads",
-    )(x_slots, rest, h, dg, du)
-    relay_t, relay_b, down_grad = lax.optimization_barrier((relay_t, relay_b, down_grad))
-    from_l_t = shift((o1t.astype(F32) + relay_t.astype(F32)).astype(BF), 1)
-    from_r_b = shift((o3b.astype(F32) + relay_b.astype(F32)).astype(BF), -1)
 
     part_back = lax.all_to_all(
         part.reshape(OWN, 32, WR), "expert", split_axis=0, concat_axis=0, tiled=True
     ).reshape(OWN * 32, WR)
 
-    sum_t = o0[:half].astype(F32) + from_l_t.astype(F32) + from_r_t.astype(F32)
-    sum_b = o0[half:].astype(F32) + from_l_b.astype(F32) + from_r_b.astype(F32)
-    sums = jnp.concatenate([sum_t.astype(BF), sum_b.astype(BF)], axis=0)
+    down_grad, pick = pl.pallas_call(
+        grads_down,
+        grid=(LOC,),
+        in_specs=[whole((2, TOK)), by_expert(OWN, D), hid_spec],
+        out_specs=[leading(QH, D), pl.BlockSpec((TOK, 256), lambda e: (0, e))],
+        out_shape=[shape((LOC, QH, D)), shape((TOK, OWN * LOC * CAP))],
+        compiler_params=params(),
+        cost_estimate=cost(1.1e9, 10e6),
+        name="grads_down",
+    )(dest, rest, h)
+    relay_t, relay_b, pick = lax.optimization_barrier((relay_t, relay_b, pick))
+
+    quarter = pl.BlockSpec((half // 4, LOC, CAP, RA), lambda i: (i, 0, 0, 0))
+    sum_t, sum_b = pl.pallas_call(
+        relay_sums,
+        grid=(4,),
+        in_specs=[quarter] * 4,
+        out_specs=[quarter] * 2,
+        out_shape=[half_part] * 2,
+        compiler_params=params(),
+        cost_estimate=cost(1e6, 2.4e6),
+        name="relay_sums",
+    )(o1t, relay_t, o3b, relay_b)
+    from_l_t = shift(sum_t, 1)
+    from_r_b = shift(sum_b, -1)
+
+    sum_t, sum_b, dg, du = lax.optimization_barrier((sum_t, sum_b, dg, du))
+    gate_grad, up_grad = pl.pallas_call(
+        grads_up,
+        grid=(LOC,),
+        in_specs=[leading(rows, D)] + [hid_spec] * 2,
+        out_specs=[leading(D, QH), leading(D, QH)],
+        out_shape=[shape((LOC, D, QH)), shape((LOC, D, QH))],
+        compiler_params=params(),
+        cost_estimate=cost(1.2e10, 20e6),
+        name="grads_up",
+    )(x_slots, dg, du)
+    from_l_b, from_r_t, up_grad = lax.optimization_barrier((from_l_b, from_r_t, up_grad))
+    sums = pl.pallas_call(
+        last_sums,
+        grid=(4,),
+        in_specs=[quarter] * 6,
+        out_specs=pl.BlockSpec((2, half // 4, LOC, CAP, RA), lambda i: (0, i, 0, 0, 0)),
+        out_shape=shape((2, half, LOC, CAP, RA)),
+        compiler_params=params(),
+        cost_estimate=cost(2e6, 3.2e6),
+        name="last_sums",
+    )(o0t, from_l_t, from_r_t, o0b, from_l_b, from_r_b)
     back = lax.all_to_all(
         sums.reshape(OWN, 32, RA), "expert", split_axis=0, concat_axis=0, tiled=True
     ).reshape(OWN * 32, RA)
@@ -296,7 +337,9 @@
     y_shape = shape((TOK + 32, RB))
     y0, y1, y2, y3 = pl.pallas_call(
         pick_pairs,
+        in_specs=[pl.BlockSpec(memory_space=pltpu.VMEM)] * 2,
         out_shape=[y_shape] * 4,
+        scratch_shapes=[pltpu.VMEM((TOK, NZ * RB), F32)],
         compiler_params=params(),
         cost_estimate=cost(4e8, 3e6),
         name="pick_pairs",
@@ -309,7 +352,7 @@
         compiler_params=params(),
         cost_estimate=cost(4e8, 3e6),
         name="finish",
-    )(dest, weights, back, *ys)
+    )(pick, weights, back, *ys)
     return (input_grad, mix_t.T, gate_grad, up_grad, down_grad)
 
 

time: 173 us -> 171 us (0.988)
  Pallas kernels: 42.7 us -> 53.6 us
  waiting for transfers between devices: 63.5 us -> 52.9 us
  other arithmetic: 4.83 us -> 0 us
  starting transfers between devices: 56.9 us -> 59.1 us
    pallas_call x2 -> x5, Pallas kernels: 12.4 us -> 23.2 us  [the longest x1 7.43 us: on_device(): pl.pallas_call(grads_up, grid=(LOC,), in_specs=[leading(rows, D)] + [hid_...]
    ppermute x18, waiting for transfers between devices: 56.6 us -> 46.8 us  [shift(): return lax.ppermute(x, 'hidden', [(i, (i + d) % NZ) for i in range(NZ)])]
    convert_element_type x3 -> x0, other arithmetic: 3.85 us -> none  [the longest x1 1.42 us: on_device(): sums = jnp.concatenate([sum_t.astype(BF), sum_b.astype(BF)], axis=0)]
    ppermute x18, starting transfers between devices: 23.2 us -> 25.8 us  [shift(): return lax.ppermute(x, 'hidden', [(i, (i + d) % NZ) for i in range(NZ)])]
  transfers between devices with their start and end apart: 22 -> 22, of which waited for: 11 -> 11; matrix products, arithmetic and copies ran while one was open for 4% -> 1% of each run, Pallas kernels for 15% -> 21%
where the time goes in v3:
time: 171 us; the launch traced here: 170 us
  starting transfers between devices  59.1 us (35%)
  Pallas kernels  53.6 us (31%)
  waiting for transfers between devices  52.9 us (31%)
  local copies, waits for them, and re-layouts  3.82 us (2%)
    ppermute x18, waiting for transfers between devices, shift(): return lax.ppermute(x, 'hidden', [(i, (i + d) % NZ) for i in range(NZ)])  46.8 us
    ppermute x18, starting transfers between devices, shift(): return lax.ppermute(x, 'hidden', [(i, (i + d) % NZ) for i in range(NZ)])  25.8 us
    pallas_call x1, Pallas kernels, on_device(): pl.pallas_call(middle, grid=(LOC,), in_specs=[smem, by_expert(OWN, D)] +...  11.4 us
    all_to_all x1, starting transfers between devices, on_device(): lax.all_to_all(sums.reshape(OWN, 32, RA), 'expert', split_axis=0, concat_...  8.79 us
    all_to_all x1, starting transfers between devices, on_device(): got = lax.all_to_all(pay, 'expert', split_axis=0, concat_axis=0, tiled=True)  8.64 us
    pallas_call x1, Pallas kernels, on_device(): pl.pallas_call(gates, grid=(LOC,), in_specs=[smem, by_expert(OWN, QF)] +...  8.52 us
    all_to_all x1, starting transfers between devices, on_device(): lax.all_to_all(pay_rest, 'expert', split_axis=0, concat_axis=0, tiled=True)  8.2 us
    all_to_all x1, starting transfers between devices, on_device(): lax.all_to_all(part.reshape(OWN, 32, WR), 'expert', split_axis=0, concat_...  7.73 us
  transfers between devices with their start and end apart: 22, of which 11 were waited for; matrix products, arithmetic and copies ran while one was open for 1% of the time, Pallas kernels for 21%

profile of v3, /device:TPU:1, one launch (start us, length us, event | category | flops | bytes accessed | tf_op | source)
XLA Modules:
  0.0 170.3 jit_solution(13117868705551977098)
XLA Ops:
  0.6 3.4 %route_first.1 = (bf16[32,32,512]{2,1,0:T(8,128)(2,1)}, s32[2,256]{1,0:T(2,128)}) custom-call(s32[2,256]{1,0:T(2,128)} %bitcast.19, bf16[256,512]{1,0:T(8,128)(2,1)} %tokens.1), custom_call_target="tpu_custom_call" | custom-call | flops 500000000 | bytes 4000000 | tf_op jit(solution)/shard_map/route_first/pallas_call | solution.py:212
  4.1 8.6 %all-to-all-start.1 = ((bf16[32,32,512]{2,1,0:T(8,128)(2,1)}), bf16[32,32,512]{2,1,0:T(8,128)(2,1)}, u32[]{:S(2)}, u32[]{:S(2)}) async-start(bf16[32,32,512]{2,1,0:T(8,128)(2,1)} %get-tuple-element.43), calls=%async_computation.1 | async-start | bytes 2097152 | tf_op jit(solution)/shard_map/all_to_all | solution.py:223
  12.7 3.7 %collective-permute-start.1 = (bf16[256,512]{1,0:T(8,128)(2,1)}, bf16[256,512]{1,0:T(8,128)(2,1)S(1)}, u32[]{:S(2)}, u32[]{:S(2)}) collective-permute-start(bf16[256,512]{1,0:T(8,128)(2,1)} %c0.1), channel_id=1, source_target_pairs={{0,2},{1,3},{2,0},{3,1},{4,6},{5,7},{6,4},{7,5},{8,10},{9,11},{10,... | collective-permute-start | bytes 786440 | tf_op jit(solution)/shard_map/ppermute | solution.py:30
  17.8 5.3 %collective-permute-done.1.c2 = bf16[256,512]{1,0:T(8,128)(2,1)S(1)} collective-permute-done((bf16[256,512]{1,0:T(8,128)(2,1)}, bf16[256,512]{1,0:T(8,128)(2,1)S(1)}, u32[]{:S(2)}, u32[]{:S(2)}) %collective-permute-start.1) | collective-permute-done | bytes 262176 | tf_op jit(solution)/shard_map/ppermute | solution.py:30
  23.2 5.9 %collective-permute-done.c1 = bf16[256,512]{1,0:T(8,128)(2,1)S(1)} collective-permute-done((bf16[256,512]{1,0:T(8,128)(2,1)}, bf16[256,512]{1,0:T(8,128)(2,1)S(1)}, u32[]{:S(2)}, u32[]{:S(2)}) %collective-permute-start) | collective-permute-done | bytes 262176 | tf_op jit(solution)/shard_map/ppermute | solution.py:30
  29.9 4.6 %route_rest.1 = bf16[32,32,2048]{2,1,0:T(8,128)(2,1)} custom-call(s32[1]{0:T(128)} %bitcast.z_ref, s32[2,256]{1,0:T(2,128)} %get-tuple-element.42.dest, f32[2,256]{1,0:T(2,128)} %bitcast.17, bf16[256,512]{1,0:T(8,128)(2,1)} %c0.1, bf16[256,512]{1,0:T(8,128)(2,1)} %copy-done.10, bf16[256,512]{1,0:T(8,128)(2,1)} %copy-done.9, bf16[256,512]{1,0:T(8,128)(2,1)} %copy-done.11), custom_call_target="tpu_custom_call" | custom-call | flops 800000000 | bytes 6000000 | tf_op jit(solution)/shard_map/route_rest/pallas_call | solution.py:225
  34.5 8.2 %all-to-all-start = ((bf16[32,32,2048]{2,1,0:T(8,128)(2,1)}), bf16[32,32,2048]{2,1,0:T(8,128)(2,1)}, u32[]{:S(2)}, u32[]{:S(2)}) async-start(bf16[32,32,2048]{2,1,0:T(8,128)(2,1)} %route_rest.1), calls=%async_computation | async-start | bytes 8388608 | tf_op jit(solution)/shard_map/all_to_all | solution.py:235
  49.1 8.3 %collective-permute-done.6.right_b = bf16[16,4,8,512]{3,2,1,0:T(8,128)(2,1)S(1)} collective-permute-done((bf16[16,4,8,512]{3,2,1,0:T(8,128)(2,1)S(1)}, bf16[16,4,8,512]{3,2,1,0:T(8,128)(2,1)S(1)}, u32[]{:S(2)}, u32[]{:S(2)}) %collective-permute-start.6) | collective-permute-done | bytes 524320 | tf_op jit(solution)/shard_map/ppermute | solution.py:30
  57.4 3.5 %collective-permute-start.8 = (bf16[16,4,8,512]{3,2,1,0:T(8,128)(2,1)S(1)}, bf16[16,4,8,512]{3,2,1,0:T(8,128)(2,1)S(1)}, u32[]{:S(2)}, u32[]{:S(2)}) collective-permute-start(bf16[16,4,8,512]{3,2,1,0:T(8,128)(2,1)S(1)} %collective-permute-done.6.right_b), channel_id=1, source_target_pairs={{0,3},{1,0},{2,1},{3,2},{4,7},{5,4},{6,5},{7,6},{8,11},{9,8},{10,9... | collective-permute-start | bytes 1572872 | tf_op jit(solution)/shard_map/ppermute | solution.py:30
  60.9 10.9 %collective-permute-done.4.left_b = bf16[16,4,8,512]{3,2,1,0:T(8,128)(2,1)S(1)} collective-permute-done((bf16[16,4,8,512]{3,2,1,0:T(8,128)(2,1)S(1)}, bf16[16,4,8,512]{3,2,1,0:T(8,128)(2,1)S(1)}, u32[]{:S(2)}, u32[]{:S(2)}) %collective-permute-start.4) | collective-permute-done | bytes 524320 | tf_op jit(solution)/shard_map/ppermute | solution.py:30
  71.8 8.0 %collective-permute-done.8.far_b = bf16[16,4,8,512]{3,2,1,0:T(8,128)(2,1)S(1)} collective-permute-done((bf16[16,4,8,512]{3,2,1,0:T(8,128)(2,1)S(1)}, bf16[16,4,8,512]{3,2,1,0:T(8,128)(2,1)S(1)}, u32[]{:S(2)}, u32[]{:S(2)}) %collective-permute-start.8) | collective-permute-done | bytes 524320 | tf_op jit(solution)/shard_map/ppermute | solution.py:30
  79.8 3.2 %collective-permute-done.7.far_a = bf16[16,4,8,512]{3,2,1,0:T(8,128)(2,1)S(1)} collective-permute-done((bf16[16,4,8,512]{3,2,1,0:T(8,128)(2,1)S(1)}, bf16[16,4,8,512]{3,2,1,0:T(8,128)(2,1)S(1)}, u32[]{:S(2)}, u32[]{:S(2)}) %collective-permute-start.7) | collective-permute-done | bytes 524320 | tf_op jit(solution)/shard_map/ppermute | solution.py:30
  83.9 8.5 %gates.1 = (bf16[4,256,2048]{2,1,0:T(8,128)(2,1)}, bf16[4,256,256]{2,1,0:T(8,128)(2,1)}, f32[4,256,256]{2,1,0:T(8,128)}, f32[4,256,256]{2,1,0:T(8,128)}) custom-call(s32[1]{0:T(128)} %bitcast.z_ref, bf16[32,4,8,512]{3,2,1,0:T(8,128)(2,1)} %bitcast.4.own, bf16[16,4,8,512]{3,2,1,0:T(8,128)(2,1)} %copy-done.2, bf16[16,4,8,512]{3,2,1,0:T(8,128)(2,1)} %copy-done.3, ...), custom_call_target="tpu_custom_call" | custom-call | flops 2200000000 | bytes 19000000 | tf_op jit(solution)/shard_map/gates/pallas_call | solution.py:251
  94.9 11.4 %middle.1 = (bf16[16,4,8,384]{3,2,1,0:T(8,128)(2,1)}, bf16[16,4,8,384]{3,2,1,0:T(8,128)(2,1)}, bf16[16,4,8,384]{3,2,1,0:T(8,128)(2,1)}, bf16[16,4,8,384]{3,2,1,0...) custom-call(s32[1]{0:T(128)} %bitcast.z_ref, ...), custom_call_target="tpu_custom_call" | custom-call | flops 2700000000 | bytes 27000000 | tf_op jit(solution)/shard_map/middle/pallas_call | solution.py:264
  109.0 7.7 %all-to-all-start.3 = ((bf16[32,32,640]{2,1,0:T(8,128)(2,1)}), bf16[32,32,640]{2,1,0:T(8,128)(2,1)}, u32[]{:S(2)}, u32[]{:S(2)}) async-start(bf16[32,32,640]{2,1,0:T(8,128)(2,1)} %bitcast.16), calls=%async_computation.3 | async-start | bytes 2621440 | tf_op jit(solution)/shard_map/all_to_all | solution.py:281
  119.5 5.7 %grads_down.1 = (bf16[4,256,2048]{2,1,0:T(8,128)(2,1)}, bf16[256,1024]{1,0:T(8,128)(2,1)}) custom-call(s32[2,256]{1,0:T(2,128)} %get-tuple-element.42.dest, bf16[32,4,8,2048]{3,2,1,0:T(8,128)(2,1)} %bitcast.3.rest, bf16[4,256,256]{2,1,0:T(8,128)(2,1)} %get-tuple-element.44.h_in.h), custom_call_target="tpu_custom_call" | custom-call | flops 1100000000 | bytes 10000000 | tf_op jit(solution)/shard_map/grads_down/pallas_call | solution.py:285
  125.2 3.5 %relay_sums.1 = (bf16[16,4,8,384]{3,2,1,0:T(8,128)(2,1)}, bf16[16,4,8,384]{3,2,1,0:T(8,128)(2,1)}) custom-call(bf16[16,4,8,384]{3,2,1,0:T(8,128)(2,1)} %get-tuple-element.52.a0, bf16[16,4,8,384]{3,2,1,0:T(8,128)(2,1)} %collective-permute-done.9.a1, bf16[16,4,8,384]{3,2,1,0:T(8,128)(2,1)} %get-tuple-element.54.b0, ...), custom_call_target="tpu_custom_call" | custom-call | flops 1000000 | bytes 2400000 | tf_op jit(solution)/shard_map/relay_sums/pallas_call | solution.py:298
  131.4 7.4 %grads_up.1 = (bf16[4,2048,256]{2,1,0:T(8,128)(2,1)}, bf16[4,2048,256]{2,1,0:T(8,128)(2,1)}) custom-call(bf16[4,256,2048]{2,1,0:T(8,128)(2,1)} %get-tuple-element.59.x, bf16[4,256,256]{2,1,0:T(8,128)(2,1)} %get-tuple-element.63.dg, bf16[4,256,256]{2,1,0:T(8,128)(2,1)} %get-tuple-element.64.du), custom_call_target="tpu_custom_call" | custom-call | flops 12000000000 | bytes 20000000 | tf_op jit(solution)/shard_map/grads_up/pallas_call | solution.py:312
  140.0 3.8 %last_sums.1 = bf16[2,16,4,8,384]{4,3,2,1,0:T(8,128)(2,1)} custom-call(bf16[16,4,8,384]{3,2,1,0:T(8,128)(2,1)} %get-tuple-element.51.a0, bf16[16,4,8,384]{3,2,1,0:T(8,128)(2,1)} %collective-permute-done.11.a1, bf16[16,4,8,384]{3,2,1,0:T(8,128)(2,1)} %copy-done.8, bf16[16,4,8,384]{3,2,1,0:T(8,128)(2,1)} %get-tuple-element.67.b0, ...), custom_call_target="tpu_custom_call" | custom-call | flops 2000000 | bytes 3200000 | tf_op jit(solution)/shard_map/last_sums/pallas_call | solution.py:323
  143.8 8.8 %all-to-all-start.2 = ((bf16[32,32,384]{2,1,0:T(8,128)(2,1)}), bf16[32,32,384]{2,1,0:T(8,128)(2,1)S(1)}, u32[]{:S(2)}, u32[]{:S(2)}) async-start(bf16[32,32,384]{2,1,0:T(8,128)(2,1)} %bitcast.15), calls=%async_computation.2 | async-start | bytes 1572864 | tf_op jit(solution)/shard_map/all_to_all | solution.py:333
  152.6 2.8 %pick_pairs.1 = (bf16[288,128]{1,0:T(8,128)(2,1)}, bf16[288,128]{1,0:T(8,128)(2,1)}, bf16[288,128]{1,0:T(8,128)(2,1)}, bf16[288,128]{1,0:T(8,128)(2,1)}) custom-call(s32[2,256]{1,0:T(2,128)} %get-tuple-element.42.dest, bf16[1024,640]{1,0:T(8,128)(2,1)} %bitcast.10.back), custom_call_target="tpu_custom_call" | custom-call | flops 400000000 | bytes 3000000 | tf_op jit(solution)/shard_map/pick_pairs/pallas_call | solution.py:338
  155.4 3.8 %collective-permute-start.16 = (bf16[288,128]{1,0:T(8,128)(2,1)}, bf16[288,128]{1,0:T(8,128)(2,1)S(1)}, u32[]{:S(2)}, u32[]{:S(2)}) collective-permute-start(bf16[288,128]{1,0:T(8,128)(2,1)} %get-tuple-element.72), channel_id=1, source_target_pairs={{0,2},{1,3},{2,0},{3,1},{4,6},{5,7},{6,4},{7,5},{8,10},{9,11},{10,... | collective-permute-start | bytes 221192 | tf_op jit(solution)/shard_map/ppermute | solution.py:30
  160.5 2.8 %collective-permute-done.16.y2 = bf16[288,128]{1,0:T(8,128)(2,1)S(1)} collective-permute-done((bf16[288,128]{1,0:T(8,128)(2,1)}, bf16[288,128]{1,0:T(8,128)(2,1)S(1)}, u32[]{:S(2)}, u32[]{:S(2)}) %collective-permute-start.16) | collective-permute-done | bytes 73760 | tf_op jit(solution)/shard_map/ppermute | solution.py:30
  163.2 3.6 %all-to-all-done.2 = bf16[32,32,384]{2,1,0:T(8,128)(2,1)S(1)} async-done(((bf16[32,32,384]{2,1,0:T(8,128)(2,1)}), bf16[32,32,384]{2,1,0:T(8,128)(2,1)S(1)}, u32[]{:S(2)}, u32[]{:S(2)}) %all-to-all-start.2) | async-done | bytes 786464 | tf_op jit(solution)/shard_map/all_to_all | solution.py:333
  (59 shorter events, 26.0 us)
Async XLA Ops:
  4.1 30.4 %all-to-all-start.1 = ((bf16[32,32,512]{2,1,0:T(8,128)(2,1)}), bf16[32,32,512]{2,1,0:T(8,128)(2,1)}, u32[]{:S(2)}, u32[]{:S(2)}) async-start(bf16[32,32,512]{2,1,0:T(8,128)(2,1)} %get-tuple-element.43), calls=%async_computation.1 | async-start | bytes 2097152 | tf_op jit(solution)/shard_map/all_to_all | solution.py:223
  12.7 10.5 %collective-permute-start.1 = (bf16[256,512]{1,0:T(8,128)(2,1)}, bf16[256,512]{1,0:T(8,128)(2,1)S(1)}, u32[]{:S(2)}, u32[]{:S(2)}) collective-permute-start(bf16[256,512]{1,0:T(8,128)(2,1)} %c0.1), channel_id=1, source_target_pairs={{0,2},{1,3},{2,0},{3,1},{4,6},{5,7},{6,4},{7,5},{8,10},{9,11},{10,... | collective-permute-start | bytes 786440 | tf_op jit(solution)/shard_map/ppermute | solution.py:30
  16.4 12.7 %collective-permute-start = (bf16[256,512]{1,0:T(8,128)(2,1)}, bf16[256,512]{1,0:T(8,128)(2,1)S(1)}, u32[]{:S(2)}, u32[]{:S(2)}) collective-permute-start(bf16[256,512]{1,0:T(8,128)(2,1)} %c0.1), channel_id=1, source_target_pairs={{0,3},{1,0},{2,1},{3,2},{4,7},{5,4},{6,5},{7,6},{8,11},{9,8},{10,9... | collective-permute-start | bytes 786440 | tf_op jit(solution)/shard_map/ppermute | solution.py:30
  16.8 12.3 %collective-permute-start.2 = (bf16[256,512]{1,0:T(8,128)(2,1)}, bf16[256,512]{1,0:T(8,128)(2,1)S(1)}, u32[]{:S(2)}, u32[]{:S(2)}) collective-permute-start(bf16[256,512]{1,0:T(8,128)(2,1)} %c0.1), channel_id=1, source_target_pairs={{0,1},{1,2},{2,3},{3,0},{4,5},{5,6},{6,7},{7,4},{8,9},{9,10},{10,1... | collective-permute-start | bytes 786440 | tf_op jit(solution)/shard_map/ppermute | solution.py:30
  34.5 60.4 %all-to-all-start = ((bf16[32,32,2048]{2,1,0:T(8,128)(2,1)}), bf16[32,32,2048]{2,1,0:T(8,128)(2,1)}, u32[]{:S(2)}, u32[]{:S(2)}) async-start(bf16[32,32,2048]{2,1,0:T(8,128)(2,1)} %route_rest.1), calls=%async_computation | async-start | bytes 8388608 | tf_op jit(solution)/shard_map/all_to_all | solution.py:235
  44.0 13.4 %collective-permute-start.6 = (bf16[16,4,8,512]{3,2,1,0:T(8,128)(2,1)S(1)}, bf16[16,4,8,512]{3,2,1,0:T(8,128)(2,1)S(1)}, u32[]{:S(2)}, u32[]{:S(2)}) collective-permute-start(bf16[16,4,8,512]{3,2,1,0:T(8,128)(2,1)S(1)} %get-tuple-element.79), channel_id=1, source_target_pairs={{0,3},{1,0},{2,1},{3,2},{4,7},{5,4},{6,5},{7,6},{8,11},{9,8},{10,9... | collective-permute-start | bytes 1572872 | tf_op jit(solution)/shard_map/ppermute | solution.py:30
  46.4 14.5 %collective-permute-start.3 = (bf16[16,4,8,512]{3,2,1,0:T(8,128)(2,1)S(1)}, bf16[16,4,8,512]{3,2,1,0:T(8,128)(2,1)S(1)}, u32[]{:S(2)}, u32[]{:S(2)}) collective-permute-start(bf16[16,4,8,512]{3,2,1,0:T(8,128)(2,1)S(1)} %get-tuple-element.80), channel_id=1, source_target_pairs={{0,1},{1,2},{2,3},{3,0},{4,5},{5,6},{6,7},{7,4},{8,9},{9,10},{10,1... | collective-permute-start | bytes 1572872 | tf_op jit(solution)/shard_map/ppermute | solution.py:30
  46.4 25.4 %collective-permute-start.4 = (bf16[16,4,8,512]{3,2,1,0:T(8,128)(2,1)S(1)}, bf16[16,4,8,512]{3,2,1,0:T(8,128)(2,1)S(1)}, u32[]{:S(2)}, u32[]{:S(2)}) collective-permute-start(bf16[16,4,8,512]{3,2,1,0:T(8,128)(2,1)S(1)} %get-tuple-element.79), channel_id=1, source_target_pairs={{0,1},{1,2},{2,3},{3,0},{4,5},{5,6},{6,7},{7,4},{8,9},{9,10},{10,1... | collective-permute-start | bytes 1572872 | tf_op jit(solution)/shard_map/ppermute | solution.py:30
  46.4 25.4 %collective-permute-start.5 = (bf16[16,4,8,512]{3,2,1,0:T(8,128)(2,1)S(1)}, bf16[16,4,8,512]{3,2,1,0:T(8,128)(2,1)S(1)}, u32[]{:S(2)}, u32[]{:S(2)}) collective-permute-start(bf16[16,4,8,512]{3,2,1,0:T(8,128)(2,1)S(1)} %get-tuple-element.80), channel_id=1, source_target_pairs={{0,3},{1,0},{2,1},{3,2},{4,7},{5,4},{6,5},{7,6},{8,11},{9,8},{10,9... | collective-permute-start | bytes 1572872 | tf_op jit(solution)/shard_map/ppermute | solution.py:30
  57.4 26.5 %copy-start.1 = (bf16[16,4,8,512]{3,2,1,0:T(8,128)(2,1)}, bf16[16,4,8,512]{3,2,1,0:T(8,128)(2,1)S(1)}, u32[]{:S(2)}) copy-start(bf16[16,4,8,512]{3,2,1,0:T(8,128)(2,1)S(1)} %collective-permute-done.6.right_b) | copy-start | bytes 1572868
  57.4 22.5 %collective-permute-start.8 = (bf16[16,4,8,512]{3,2,1,0:T(8,128)(2,1)S(1)}, bf16[16,4,8,512]{3,2,1,0:T(8,128)(2,1)S(1)}, u32[]{:S(2)}, u32[]{:S(2)}) collective-permute-start(bf16[16,4,8,512]{3,2,1,0:T(8,128)(2,1)S(1)} %collective-permute-done.6.right_b), channel_id=1, source_target_pairs={{0,3},{1,0},{2,1},{3,2},{4,7},{5,4},{6,5},{7,6},{8,11},{9,8},{10,9... | collective-permute-start | bytes 1572872 | tf_op jit(solution)/shard_map/ppermute | solution.py:30
  60.9 19.0 %copy-start.2 = (bf16[16,4,8,512]{3,2,1,0:T(8,128)(2,1)}, bf16[16,4,8,512]{3,2,1,0:T(8,128)(2,1)S(1)}, u32[]{:S(2)}) copy-start(bf16[16,4,8,512]{3,2,1,0:T(8,128)(2,1)S(1)} %collective-permute-done.3.left_a) | copy-start | bytes 1572868
  60.9 22.1 %collective-permute-start.7 = (bf16[16,4,8,512]{3,2,1,0:T(8,128)(2,1)S(1)}, bf16[16,4,8,512]{3,2,1,0:T(8,128)(2,1)S(1)}, u32[]{:S(2)}, u32[]{:S(2)}) collective-permute-start(bf16[16,4,8,512]{3,2,1,0:T(8,128)(2,1)S(1)} %collective-permute-done.3.left_a), channel_id=1, source_target_pairs={{0,1},{1,2},{2,3},{3,0},{4,5},{5,6},{6,7},{7,4},{8,9},{9,10},{10,1... | collective-permute-start | bytes 1572872 | tf_op jit(solution)/shard_map/ppermute | solution.py:30
  106.3 18.9 %collective-permute-start.9 = (bf16[16,4,8,384]{3,2,1,0:T(8,128)(2,1)}, bf16[16,4,8,384]{3,2,1,0:T(8,128)(2,1)}, u32[]{:S(2)}, u32[]{:S(2)}) collective-permute-start(bf16[16,4,8,384]{3,2,1,0:T(8,128)(2,1)} %get-tuple-element.47), channel_id=1, source_target_pairs={{0,1},{1,2},{2,3},{3,0},{4,5},{5,6},{6,7},{7,4},{8,9},{9,10},{10,1... | collective-permute-start | bytes 1179656 | tf_op jit(solution)/shard_map/ppermute | solution.py:30
  107.0 18.2 %collective-permute-start.10 = (bf16[16,4,8,384]{3,2,1,0:T(8,128)(2,1)}, bf16[16,4,8,384]{3,2,1,0:T(8,128)(2,1)}, u32[]{:S(2)}, u32[]{:S(2)}) collective-permute-start(bf16[16,4,8,384]{3,2,1,0:T(8,128)(2,1)} %get-tuple-element.48), channel_id=1, source_target_pairs={{0,3},{1,0},{2,1},{3,2},{4,7},{5,4},{6,5},{7,6},{8,11},{9,8},{10,9... | collective-permute-start | bytes 1179656 | tf_op jit(solution)/shard_map/ppermute | solution.py:30
  109.0 34.8 %all-to-all-start.3 = ((bf16[32,32,640]{2,1,0:T(8,128)(2,1)}), bf16[32,32,640]{2,1,0:T(8,128)(2,1)}, u32[]{:S(2)}, u32[]{:S(2)}) async-start(bf16[32,32,640]{2,1,0:T(8,128)(2,1)} %bitcast.16), calls=%async_computation.3 | async-start | bytes 2621440 | tf_op jit(solution)/shard_map/all_to_all | solution.py:281
  116.7 22.1 %collective-permute-start.12 = (bf16[16,4,8,384]{3,2,1,0:T(8,128)(2,1)}, bf16[16,4,8,384]{3,2,1,0:T(8,128)(2,1)S(1)}, u32[]{:S(2)}, u32[]{:S(2)}) collective-permute-start(bf16[16,4,8,384]{3,2,1,0:T(8,128)(2,1)} %get-tuple-element.57), channel_id=1, source_target_pairs={{0,1},{1,2},{2,3},{3,0},{4,5},{5,6},{6,7},{7,4},{8,9},{9,10},{10,1... | collective-permute-start | bytes 1179656 | tf_op jit(solution)/shard_map/ppermute | solution.py:30
  116.8 22.0 %collective-permute-start.13 = (bf16[16,4,8,384]{3,2,1,0:T(8,128)(2,1)}, bf16[16,4,8,384]{3,2,1,0:T(8,128)(2,1)S(1)}, u32[]{:S(2)}, u32[]{:S(2)}) collective-permute-start(bf16[16,4,8,384]{3,2,1,0:T(8,128)(2,1)} %get-tuple-element.58), channel_id=1, source_target_pairs={{0,3},{1,0},{2,1},{3,2},{4,7},{5,4},{6,5},{7,6},{8,11},{9,8},{10,9... | collective-permute-start | bytes 1179656 | tf_op jit(solution)/shard_map/ppermute | solution.py:30
  128.7 11.3 %collective-permute-start.11 = (bf16[16,4,8,384]{3,2,1,0:T(8,128)(2,1)}, bf16[16,4,8,384]{3,2,1,0:T(8,128)(2,1)}, u32[]{:S(2)}, u32[]{:S(2)}) collective-permute-start(bf16[16,4,8,384]{3,2,1,0:T(8,128)(2,1)} %get-tuple-element.56), channel_id=1, source_target_pairs={{0,1},{1,2},{2,3},{3,0},{4,5},{5,6},{6,7},{7,4},{8,9},{9,10},{10,1... | collective-permute-start | bytes 1179656 | tf_op jit(solution)/shard_map/ppermute | solution.py:30
  128.7 11.3 %collective-permute-start.14 = (bf16[16,4,8,384]{3,2,1,0:T(8,128)(2,1)}, bf16[16,4,8,384]{3,2,1,0:T(8,128)(2,1)}, u32[]{:S(2)}, u32[]{:S(2)}) collective-permute-start(bf16[16,4,8,384]{3,2,1,0:T(8,128)(2,1)} %get-tuple-element.60), channel_id=1, source_target_pairs={{0,3},{1,0},{2,1},{3,2},{4,7},{5,4},{6,5},{7,6},{8,11},{9,8},{10,9... | collective-permute-start | bytes 1179656 | tf_op jit(solution)/shard_map/ppermute | solution.py:30
  143.8 23.0 %all-to-all-start.2 = ((bf16[32,32,384]{2,1,0:T(8,128)(2,1)}), bf16[32,32,384]{2,1,0:T(8,128)(2,1)S(1)}, u32[]{:S(2)}, u32[]{:S(2)}) async-start(bf16[32,32,384]{2,1,0:T(8,128)(2,1)} %bitcast.15), calls=%async_computation.2 | async-start | bytes 1572864 | tf_op jit(solution)/shard_map/all_to_all | solution.py:333
  155.4 5.1 %collective-permute-start.15 = (bf16[288,128]{1,0:T(8,128)(2,1)}, bf16[288,128]{1,0:T(8,128)(2,1)S(1)}, u32[]{:S(2)}, u32[]{:S(2)}) collective-permute-start(bf16[288,128]{1,0:T(8,128)(2,1)} %get-tuple-element.71), channel_id=1, source_target_pairs={{0,1},{1,2},{2,3},{3,0},{4,5},{5,6},{6,7},{7,4},{8,9},{9,10},{10,1... | collective-permute-start | bytes 221192 | tf_op jit(solution)/shard_map/ppermute | solution.py:30
  155.4 7.8 %collective-permute-start.16 = (bf16[288,128]{1,0:T(8,128)(2,1)}, bf16[288,128]{1,0:T(8,128)(2,1)S(1)}, u32[]{:S(2)}, u32[]{:S(2)}) collective-permute-start(bf16[288,128]{1,0:T(8,128)(2,1)} %get-tuple-element.72), channel_id=1, source_target_pairs={{0,2},{1,3},{2,0},{3,1},{4,6},{5,7},{6,4},{7,5},{8,10},{9,11},{10,... | collective-permute-start | bytes 221192 | tf_op jit(solution)/shard_map/ppermute | solution.py:30
  159.3 4.0 %collective-permute-start.17 = (bf16[288,128]{1,0:T(8,128)(2,1)}, bf16[288,128]{1,0:T(8,128)(2,1)}, u32[]{:S(2)}, u32[]{:S(2)}) collective-permute-start(bf16[288,128]{1,0:T(8,128)(2,1)} %get-tuple-element.73), channel_id=1, source_target_pairs={{0,3},{1,0},{2,1},{3,2},{4,7},{5,4},{6,5},{7,6},{8,11},{9,8},{10,9... | collective-permute-start | bytes 221192 | tf_op jit(solution)/shard_map/ppermute | solution.py:30
  (12 other events, 47.2 us)

commit v4 on v3

--- a/solution.py
+++ b/solution.py
@@ -19,7 +19,9 @@
 WR = NZ * RB + 128
 BF = jnp.bfloat16
 F32 = jnp.float32
-VMEM = 63 * 1024 * 1024
+MIB = 1024 * 1024
+ROUTE = 56
+LAST = 56
 
 
 def dot(a, b, ca, cb):
@@ -30,8 +32,8 @@
     return lax.ppermute(x, "hidden", [(i, (i + d) % NZ) for i in range(NZ)])
 
 
-def params(**kw):
-    return pltpu.CompilerParams(vmem_limit_bytes=VMEM, **kw)
+def params(mib=63):
+    return pltpu.CompilerParams(vmem_limit_bytes=mib * MIB)
 
 
 def slots_of(dest, base, rows):
@@ -63,7 +65,7 @@
     pay[...] = dot(pick, tokens[...], 1, 0).astype(BF).reshape(8, 32, QF)
 
 
-def route_rest(z_ref, dest, weights, c0, c1, c2, c3, pay):
+def picked(dest, weights):
     at0, at1 = slots_of(dest, pl.program_id(0) * 256, 256)
     pick = jnp.where(at0 | at1, 1.0, 0.0).astype(BF)
     w = jnp.sum(
@@ -71,10 +73,20 @@
         axis=1,
         keepdims=True,
     )
-    for off, c in enumerate((c0, c1, c2, c3)):
+    return pick, w
+
+
+def route_near(z_ref, dest, weights, c0, c1, c3, pay):
+    pick, w = picked(dest, weights)
+    for off, c in ((0, c0), (1, c1), (3, c3)):
         dy = (dot(pick, c[...], 1, 0) * w).astype(BF)
         q = lax.rem(z_ref[0] + off, NZ)
         pay[:, :, pl.ds(pl.multiple_of(q * QF, QF), QF)] = dy.reshape(8, 32, QF)
+
+
+def route_far(z_ref, dest, weights, c2, near, pay):
+    pick, w = picked(dest, weights)
+    pay[...] = (dot(pick, c2[...], 1, 0) * w).astype(BF).reshape(8, 32, QF)
 
 
 def merged(v):
@@ -136,16 +148,6 @@
         part_out[:, 0, :, off * RB : (off + 1) * RB] = parted(dx[:, RA:])
 
 
-def relay_sums(a0, a1, b0, b1, a_out, b_out):
-    a_out[...] = (a0[...].astype(F32) + a1[...].astype(F32)).astype(BF)
-    b_out[...] = (b0[...].astype(F32) + b1[...].astype(F32)).astype(BF)
-
-
-def last_sums(a0, a1, a2, b0, b1, b2, out):
-    out[0] = (a0[...].astype(F32) + a1[...].astype(F32) + a2[...].astype(F32)).astype(BF)
-    out[1] = (b0[...].astype(F32) + b1[...].astype(F32) + b2[...].astype(F32)).astype(BF)
-
-
 def grads_down(dest, rest, h, down_out, pick_out):
     at0, at1 = slots_of(dest, pl.program_id(0) * 256, 256)
     pick_out[...] = jnp.where(at0 | at1, 1.0, 0.0).T.astype(BF)
@@ -184,7 +186,7 @@
 
 
 def shape(dims, dtype=BF):
-    return jax.ShapeDtypeStruct(dims, dtype)
+    return pltpu.HBM(dims, dtype)
 
 
 def cost(flops, size):
@@ -206,8 +208,6 @@
 def on_device(tokens, cotangent, zone_ids, gate_weights, gate_proj, up_proj, down_proj):
     z = lax.axis_index("hidden").astype(jnp.int32).reshape(1)
     zones, weights = zone_ids.T, gate_weights.T
-    cots = (cotangent, shift(cotangent, -1), shift(cotangent, 2), shift(cotangent, 1))
-
     smem = pl.BlockSpec(memory_space=pltpu.SMEM)
     pay, dest = pl.pallas_call(
         route_first,
@@ -222,16 +222,38 @@
     )(zones, tokens)
     got = lax.all_to_all(pay, "expert", split_axis=0, concat_axis=0, tiled=True)
 
+    c1, c2, c3 = shift(cotangent, -1), shift(cotangent, 2), shift(cotangent, 1)
+    c1, c2, c3 = (pltpu.with_memory_space_constraint(c, pltpu.VMEM) for c in (c1, c2, c3))
     pay_rest = pl.pallas_call(
-        route_rest,
+        route_near,
         grid=(4,),
-        in_specs=[smem, whole((2, TOK)), whole((2, TOK))] + [whole((TOK, QF))] * 4,
+        in_specs=[smem, whole((2, TOK)), whole((2, TOK))] + [whole((TOK, QF))] * 3,
         out_specs=pl.BlockSpec((8, 32, D), lambda i: (i, 0, 0)),
         out_shape=shape((OWN, 32, D)),
-        compiler_params=params(),
-        cost_estimate=cost(8e8, 6e6),
-        name="route_rest",
-    )(z, dest, weights, *cots)
+        compiler_params=params(ROUTE),
+        cost_estimate=cost(6e8, 5e6),
+        name="route_near",
+    )(z, dest, weights, cotangent, c1, c3)
+    fixed = pl.BlockSpec((2, TOK), lambda i, z: (0, 0))
+    pay_rest = pl.pallas_call(
+        route_far,
+        grid_spec=pltpu.PrefetchScalarGridSpec(
+            num_scalar_prefetch=1,
+            grid=(4,),
+            in_specs=[
+                fixed,
+                fixed,
+                pl.BlockSpec((TOK, QF), lambda i, z: (0, 0)),
+                pl.BlockSpec(memory_space=pl.ANY),
+            ],
+            out_specs=pl.BlockSpec((8, 32, QF), lambda i, z: (i, 0, lax.rem(z[0] + 2, NZ))),
+        ),
+        out_shape=shape((OWN, 32, D)),
+        input_output_aliases={4: 0},
+        compiler_params=params(ROUTE),
+        cost_estimate=cost(2e8, 2e6),
+        name="route_far",
+    )(z, dest, weights, c2, pay_rest)
     rest = lax.all_to_all(pay_rest, "expert", split_axis=0, concat_axis=0, tiled=True)
     rest = rest.reshape(OWN, LOC, CAP, D)
 
@@ -245,6 +267,9 @@
     far_t = shift(left_t, 1)
     far_b = shift(right_b, -1)
 
+    left_b, right_t, far_t, far_b = (
+        pltpu.with_memory_space_constraint(v, pltpu.VMEM) for v in (left_b, right_t, far_t, far_b)
+    )
     rows = OWN * CAP
     hid, hid_f = shape((LOC, rows, QH)), shape((LOC, rows, QH), F32)
     hid_spec = leading(rows, QH)
@@ -255,7 +280,7 @@
         out_specs=[leading(rows, D), hid_spec, hid_spec, hid_spec],
         out_shape=[shape((LOC, rows, D)), hid, hid_f, hid_f],
         scratch_shapes=[pltpu.VMEM((NZ, rows, QF), BF)],
-        compiler_params=params(),
+        compiler_params=params(56),
         cost_estimate=cost(2.2e9, 19e6),
         name="gates",
     )(z, got, left_t, left_b, right_t, right_b, far_t, far_b, gate_proj, up_proj)
@@ -294,17 +319,8 @@
     )(dest, rest, h)
     relay_t, relay_b, pick = lax.optimization_barrier((relay_t, relay_b, pick))
 
-    quarter = pl.BlockSpec((half // 4, LOC, CAP, RA), lambda i: (i, 0, 0, 0))
-    sum_t, sum_b = pl.pallas_call(
-        relay_sums,
-        grid=(4,),
-        in_specs=[quarter] * 4,
-        out_specs=[quarter] * 2,
-        out_shape=[half_part] * 2,
-        compiler_params=params(),
-        cost_estimate=cost(1e6, 2.4e6),
-        name="relay_sums",
-    )(o1t, relay_t, o3b, relay_b)
+    sum_t = (o1t.astype(F32) + relay_t.astype(F32)).astype(BF)
+    sum_b = (o3b.astype(F32) + relay_b.astype(F32)).astype(BF)
     from_l_t = shift(sum_t, 1)
     from_r_b = shift(sum_b, -1)
 
@@ -320,16 +336,9 @@
         name="grads_up",
     )(x_slots, dg, du)
     from_l_b, from_r_t, up_grad = lax.optimization_barrier((from_l_b, from_r_t, up_grad))
-    sums = pl.pallas_call(
-        last_sums,
-        grid=(4,),
-        in_specs=[quarter] * 6,
-        out_specs=pl.BlockSpec((2, half // 4, LOC, CAP, RA), lambda i: (0, i, 0, 0, 0)),
-        out_shape=shape((2, half, LOC, CAP, RA)),
-        compiler_params=params(),
-        cost_estimate=cost(2e6, 3.2e6),
-        name="last_sums",
-    )(o0t, from_l_t, from_r_t, o0b, from_l_b, from_r_b)
+    sum_t = o0t.astype(F32) + from_l_t.astype(F32) + from_r_t.astype(F32)
+    sum_b = o0b.astype(F32) + from_l_b.astype(F32) + from_r_b.astype(F32)
+    sums = jnp.concatenate([sum_t.astype(BF), sum_b.astype(BF)], axis=0)
     back = lax.all_to_all(
         sums.reshape(OWN, 32, RA), "expert", split_axis=0, concat_axis=0, tiled=True
     ).reshape(OWN * 32, RA)
@@ -346,10 +355,12 @@
     )(dest, part_back)
     ys = (y0, shift(y1, 1), shift(y2, 2), shift(y3, -1))
 
+    back = pltpu.with_memory_space_constraint(back, pltpu.VMEM)
     input_grad, mix_t = pl.pallas_call(
         finish,
-        out_shape=[shape((TOK, QF)), shape((2, TOK), F32)],
-        compiler_params=params(),
+        out_specs=[pl.BlockSpec(memory_space=pltpu.VMEM)] * 2,
+        out_shape=[jax.ShapeDtypeStruct((TOK, QF), BF), jax.ShapeDtypeStruct((2, TOK), F32)],
+        compiler_params=params(LAST),
         cost_estimate=cost(4e8, 3e6),
         name="finish",
     )(pick, weights, back, *ys)

time: 171 us -> 173 us (1.012)
  other arithmetic: 0 us -> 7.23 us
  Pallas kernels: 53.6 us -> 48.1 us
  waiting for transfers between devices: 52.9 us -> 58.4 us
  local copies, waits for them, and re-layouts: 3.82 us -> 0.11 us
    convert_element_type x0 -> x4, other arithmetic: none -> 6.24 us  [the longest x2 2.53 us: on_device(): sums = jnp.concatenate([sum_t.astype(BF), sum_b.astype(BF)], axis=0)]
    pallas_call x4 -> x3, Pallas kernels: 14.4 us -> 9.28 us  [the longest x1 4.11 us: on_device(): pl.pallas_call(route_near, grid=(4,), in_specs=[smem, whole((2, TOK)), wh...]
    all_to_all x1, waiting for transfers between devices: 2.49 us -> 7.09 us  [on_device(): lax.all_to_all(pay_rest, 'expert', split_axis=0, concat_axis=0, tiled=True)]
    unnamed x28 -> x20, local copies, waits for them, and re-layouts: 2.55 us -> 0.04 us
    ppermute x18, starting transfers between devices: 25.8 us -> 23.6 us  [shift(): return lax.ppermute(x, 'hidden', [(i, (i + d) % NZ) for i in range(NZ)])]
  transfers between devices with their start and end apart: 22 -> 22, of which waited for: 11 -> 11; matrix products, arithmetic and copies ran while one was open for 1% -> 4% of each run, Pallas kernels for 21% -> 18%
where the time goes in v4:
time: 173 us; the launch traced here: 172 us
  waiting for transfers between devices  58.4 us (34%)
  starting transfers between devices  57.7 us (33%)
  Pallas kernels  48.1 us (28%)
  other arithmetic  7.23 us (4%)
    ppermute x18, waiting for transfers between devices, shift(): return lax.ppermute(x, 'hidden', [(i, (i + d) % NZ) for i in range(NZ)])  48.4 us
    ppermute x18, starting transfers between devices, shift(): return lax.ppermute(x, 'hidden', [(i, (i + d) % NZ) for i in range(NZ)])  23.6 us
    pallas_call x1, Pallas kernels, on_device(): pl.pallas_call(middle, grid=(LOC,), in_specs=[smem, by_expert(OWN, D)] +...  11.4 us
    all_to_all x1, starting transfers between devices, on_device(): lax.all_to_all(sums.reshape(OWN, 32, RA), 'expert', split_axis=0, concat_...  9.26 us
    all_to_all x1, starting transfers between devices, on_device(): got = lax.all_to_all(pay, 'expert', split_axis=0, concat_axis=0, tiled=True)  8.59 us
    all_to_all x1, starting transfers between devices, on_device(): lax.all_to_all(pay_rest, 'expert', split_axis=0, concat_axis=0, tiled=True)  8.45 us
    pallas_call x1, Pallas kernels, on_device(): pl.pallas_call(gates, grid=(LOC,), in_specs=[smem, by_expert(OWN, QF)] +...  8.09 us
    all_to_all x1, starting transfers between devices, on_device(): lax.all_to_all(part.reshape(OWN, 32, WR), 'expert', split_axis=0, concat_...  7.85 us
  transfers between devices with their start and end apart: 22, of which 11 were waited for; matrix products, arithmetic and copies ran while one was open for 4% of the time, Pallas kernels for 18%

profile of v4, /device:TPU:1, one launch (start us, length us, event | category | flops | bytes accessed | tf_op | source)
XLA Modules:
  0.0 172.3 jit_solution(15049810545647872676)
XLA Ops:
  0.6 3.4 %route_first.1 = (bf16[32,32,512]{2,1,0:T(8,128)(2,1)}, s32[2,256]{1,0:T(2,128)}) custom-call(s32[2,256]{1,0:T(2,128)} %bitcast.21, bf16[256,512]{1,0:T(8,128)(2,1)} %tokens.1), custom_call_target="tpu_custom_call" | custom-call | flops 500000000 | bytes 4000000 | tf_op jit(solution)/shard_map/route_first/pallas_call | solution.py:212
  4.1 8.6 %all-to-all-start.1 = ((bf16[32,32,512]{2,1,0:T(8,128)(2,1)}), bf16[32,32,512]{2,1,0:T(8,128)(2,1)S(1)}, u32[]{:S(2)}, u32[]{:S(2)}) async-start(bf16[32,32,512]{2,1,0:T(8,128)(2,1)} %get-tuple-element.41), calls=%async_computation.1 | async-start | bytes 2097152 | tf_op jit(solution)/shard_map/all_to_all | solution.py:223
  12.7 3.8 %collective-permute-start.1 = (bf16[256,512]{1,0:T(8,128)(2,1)}, bf16[256,512]{1,0:T(8,128)(2,1)S(1)}, u32[]{:S(2)}, u32[]{:S(2)}) collective-permute-start(bf16[256,512]{1,0:T(8,128)(2,1)} %c0.1), channel_id=1, source_target_pairs={{0,3},{1,0},{2,1},{3,2},{4,7},{5,4},{6,5},{7,6},{8,11},{9,8},{10,9... | collective-permute-start | bytes 786440 | tf_op jit(solution)/shard_map/ppermute | solution.py:32
  17.8 10.1 %collective-permute-done.1.c1 = bf16[256,512]{1,0:T(8,128)(2,1)S(1)} collective-permute-done((bf16[256,512]{1,0:T(8,128)(2,1)}, bf16[256,512]{1,0:T(8,128)(2,1)S(1)}, u32[]{:S(2)}, u32[]{:S(2)}) %collective-permute-start.1) | collective-permute-done | bytes 262176 | tf_op jit(solution)/shard_map/ppermute | solution.py:32
  27.9 3.0 %collective-permute-done.2.c3 = bf16[256,512]{1,0:T(8,128)(2,1)S(1)} collective-permute-done((bf16[256,512]{1,0:T(8,128)(2,1)}, bf16[256,512]{1,0:T(8,128)(2,1)S(1)}, u32[]{:S(2)}, u32[]{:S(2)}) %collective-permute-start.2) | collective-permute-done | bytes 262176 | tf_op jit(solution)/shard_map/ppermute | solution.py:32
  30.9 4.1 %route_near.1.near = bf16[32,32,2048]{2,1,0:T(8,128)(2,1)} custom-call(s32[1]{0:T(128)} %bitcast.z_ref, s32[2,256]{1,0:T(2,128)} %get-tuple-element.40.dest, f32[2,256]{1,0:T(2,128)} %bitcast.18, bf16[256,512]{1,0:T(8,128)(2,1)} %c0.1, bf16[256,512]{1,0:T(8,128)(2,1)S(1)} %collective-permute-done.1.c1, bf16[256,512]{1,0:T(8,128)(2,1)S(1)} %collective-permute-done.2.c3), custom_call_target="tpu_custom_call" | custom-call | flops 600000000 | bytes 5000000 | tf_op jit(solution)/shard_map/route_near/pallas_call | solution.py:227
  35.0 2.9 %route_far.1 = bf16[32,32,2048]{2,1,0:T(8,128)(2,1)} custom-call(s32[1]{0:T(128)} %bitcast.z_ref, s32[2,256]{1,0:T(2,128)} %get-tuple-element.40.dest, f32[2,256]{1,0:T(2,128)} %bitcast.19, bf16[256,512]{1,0:T(8,128)(2,1)S(1)} %collective-permute-done.c2, bf16[32,32,2048]{2,1,0:T(8,128)(2,1)} %route_near.1.near), custom_call_target="tpu_custom_call", output_to_operand_aliasing={{}: (4, {})} | custom-call | flops 200000000 | bytes 2000000 | tf_op jit(solution)/shard_map/route_far/pallas_call | solution.py:238
  37.9 8.5 %all-to-all-start = ((bf16[32,32,2048]{2,1,0:T(8,128)(2,1)}), bf16[32,32,2048]{2,1,0:T(8,128)(2,1)}, u32[]{:S(2)}, u32[]{:S(2)}) async-start(bf16[32,32,2048]{2,1,0:T(8,128)(2,1)} %route_far.1), calls=%async_computation | async-start | bytes 8388608 | tf_op jit(solution)/shard_map/all_to_all | solution.py:257
  50.6 9.2 %collective-permute-done.6.right_b = bf16[16,4,8,512]{3,2,1,0:T(8,128)(2,1)S(1)} collective-permute-done((bf16[16,4,8,512]{3,2,1,0:T(8,128)(2,1)S(1)}, bf16[16,4,8,512]{3,2,1,0:T(8,128)(2,1)S(1)}, u32[]{:S(2)}, u32[]{:S(2)}) %collective-permute-start.6) | collective-permute-done | bytes 524320 | tf_op jit(solution)/shard_map/ppermute | solution.py:32
  61.3 10.8 %collective-permute-done.4.left_b = bf16[16,4,8,512]{3,2,1,0:T(8,128)(2,1)S(1)} collective-permute-done((bf16[16,4,8,512]{3,2,1,0:T(8,128)(2,1)S(1)}, bf16[16,4,8,512]{3,2,1,0:T(8,128)(2,1)S(1)}, u32[]{:S(2)}, u32[]{:S(2)}) %collective-permute-start.4) | collective-permute-done | bytes 524320 | tf_op jit(solution)/shard_map/ppermute | solution.py:32
  72.1 10.1 %collective-permute-done.8.far_b = bf16[16,4,8,512]{3,2,1,0:T(8,128)(2,1)S(1)} collective-permute-done((bf16[16,4,8,512]{3,2,1,0:T(8,128)(2,1)S(1)}, bf16[16,4,8,512]{3,2,1,0:T(8,128)(2,1)S(1)}, u32[]{:S(2)}, u32[]{:S(2)}) %collective-permute-start.8) | collective-permute-done | bytes 524320 | tf_op jit(solution)/shard_map/ppermute | solution.py:32
  83.4 8.1 %gates.1 = (bf16[4,256,2048]{2,1,0:T(8,128)(2,1)}, bf16[4,256,256]{2,1,0:T(8,128)(2,1)}, f32[4,256,256]{2,1,0:T(8,128)}, f32[4,256,256]{2,1,0:T(8,128)}) custom-call(s32[1]{0:T(128)} %bitcast.z_ref, bf16[32,4,8,512]{3,2,1,0:T(8,128)(2,1)} %bitcast.16, bf16[16,4,8,512]{3,2,1,0:T(8,128)(2,1)} %copy-done.2, ...), custom_call_target="tpu_custom_call" | custom-call | flops 2200000000 | bytes 19000000 | tf_op jit(solution)/shard_map/gates/pallas_call | solution.py:276
  91.5 7.1 %all-to-all-done = bf16[32,32,2048]{2,1,0:T(8,128)(2,1)} async-done(((bf16[32,32,2048]{2,1,0:T(8,128)(2,1)}), bf16[32,32,2048]{2,1,0:T(8,128)(2,1)}, u32[]{:S(2)}, u32[]{:S(2)}) %all-to-all-start) | async-done | bytes 4194336 | tf_op jit(solution)/shard_map/all_to_all | solution.py:257
  98.6 11.4 %middle.1 = (bf16[16,4,8,384]{3,2,1,0:T(8,128)(2,1)}, bf16[16,4,8,384]{3,2,1,0:T(8,128)(2,1)}, bf16[16,4,8,384]{3,2,1,0:T(8,128)(2,1)}, bf16[16,4,8,384]{3,2,1,0...) custom-call(s32[1]{0:T(128)} %bitcast.z_ref, ...), custom_call_target="tpu_custom_call" | custom-call | flops 2700000000 | bytes 27000000 | tf_op jit(solution)/shard_map/middle/pallas_call | solution.py:289
  110.0 2.7 %collective-permute-start.10 = (bf16[16,4,8,384]{3,2,1,0:T(8,128)(2,1)}, bf16[16,4,8,384]{3,2,1,0:T(8,128)(2,1)}, u32[]{:S(2)}, u32[]{:S(2)}) collective-permute-start(bf16[16,4,8,384]{3,2,1,0:T(8,128)(2,1)} %get-tuple-element.46), channel_id=1, source_target_pairs={{0,3},{1,0},{2,1},{3,2},{4,7},{5,4},{6,5},{7,6},{8,11},{9,8},{10,9... | collective-permute-start | bytes 1179656 | tf_op jit(solution)/shard_map/ppermute | solution.py:32
  112.7 7.9 %all-to-all-start.3 = ((bf16[32,32,640]{2,1,0:T(8,128)(2,1)}), bf16[32,32,640]{2,1,0:T(8,128)(2,1)}, u32[]{:S(2)}, u32[]{:S(2)}) async-start(bf16[32,32,640]{2,1,0:T(8,128)(2,1)} %bitcast.17), calls=%async_computation.3 | async-start | bytes 2621440 | tf_op jit(solution)/shard_map/all_to_all | solution.py:306
  120.6 2.7 %collective-permute-start.13 = (bf16[16,4,8,384]{3,2,1,0:T(8,128)(2,1)}, bf16[16,4,8,384]{3,2,1,0:T(8,128)(2,1)}, u32[]{:S(2)}, u32[]{:S(2)}) collective-permute-start(bf16[16,4,8,384]{3,2,1,0:T(8,128)(2,1)} %get-tuple-element.53), channel_id=1, source_target_pairs={{0,3},{1,0},{2,1},{3,2},{4,7},{5,4},{6,5},{7,6},{8,11},{9,8},{10,9... | collective-permute-start | bytes 1179656 | tf_op jit(solution)/shard_map/ppermute | solution.py:32
  123.3 5.7 %grads_down.1 = (bf16[4,256,2048]{2,1,0:T(8,128)(2,1)}, bf16[256,1024]{1,0:T(8,128)(2,1)}) custom-call(s32[2,256]{1,0:T(2,128)} %get-tuple-element.40.dest, bf16[32,4,8,2048]{3,2,1,0:T(8,128)(2,1)} %bitcast.3.rest, bf16[4,256,256]{2,1,0:T(8,128)(2,1)} %get-tuple-element.42.h_in.h), custom_call_target="tpu_custom_call" | custom-call | flops 1100000000 | bytes 10000000 | tf_op jit(solution)/shard_map/grads_down/pallas_call | solution.py:310
  132.7 2.7 %collective-permute-start.14 = (bf16[16,4,8,384]{3,2,1,0:T(8,128)(2,1)}, bf16[16,4,8,384]{3,2,1,0:T(8,128)(2,1)}, u32[]{:S(2)}, u32[]{:S(2)}) collective-permute-start(bf16[16,4,8,384]{3,2,1,0:T(8,128)(2,1)} %add_convert_fusion.2), channel_id=1, source_target_pairs={{0,3},{1,0},{2,1},{3,2},{4,7},{5,4},{6,5},{7,6},{8,11},{9,8},{10,9... | collective-permute-start | bytes 1179656 | tf_op jit(solution)/shard_map/ppermute | solution.py:32
  135.4 7.5 %grads_up.1 = (bf16[4,2048,256]{2,1,0:T(8,128)(2,1)}, bf16[4,2048,256]{2,1,0:T(8,128)(2,1)}) custom-call(bf16[4,256,2048]{2,1,0:T(8,128)(2,1)} %get-tuple-element.54.x, bf16[4,256,256]{2,1,0:T(8,128)(2,1)} %get-tuple-element.59.dg, bf16[4,256,256]{2,1,0:T(8,128)(2,1)} %get-tuple-element.60.du), custom_call_target="tpu_custom_call" | custom-call | flops 12000000000 | bytes 20000000 | tf_op jit(solution)/shard_map/grads_up/pallas_call | solution.py:328
  146.5 9.3 %all-to-all-start.2 = ((bf16[32,32,384]{2,1,0:T(8,128)(2,1)}), bf16[32,32,384]{2,1,0:T(8,128)(2,1)S(1)}, u32[]{:S(2)}, u32[]{:S(2)}) async-start(bf16[32,32,384]{2,1,0:T(8,128)(2,1)} %maximum_bitcast_fusion), calls=%async_computation.2 | async-start | bytes 1572864 | tf_op jit(solution)/shard_map/all_to_all | solution.py:342
  155.8 2.8 %pick_pairs.1 = (bf16[288,128]{1,0:T(8,128)(2,1)}, bf16[288,128]{1,0:T(8,128)(2,1)}, bf16[288,128]{1,0:T(8,128)(2,1)}, bf16[288,128]{1,0:T(8,128)(2,1)}) custom-call(s32[2,256]{1,0:T(2,128)} %get-tuple-element.40.dest, bf16[1024,640]{1,0:T(8,128)(2,1)} %bitcast.10.back), custom_call_target="tpu_custom_call" | custom-call | flops 400000000 | bytes 3000000 | tf_op jit(solution)/shard_map/pick_pairs/pallas_call | solution.py:347
  158.6 4.6 %collective-permute-start.16 = (bf16[288,128]{1,0:T(8,128)(2,1)}, bf16[288,128]{1,0:T(8,128)(2,1)S(1)}, u32[]{:S(2)}, u32[]{:S(2)}) collective-permute-start(bf16[288,128]{1,0:T(8,128)(2,1)} %get-tuple-element.68), channel_id=1, source_target_pairs={{0,2},{1,3},{2,0},{3,1},{4,6},{5,7},{6,4},{7,5},{8,10},{9,11},{10,... | collective-permute-start | bytes 221192 | tf_op jit(solution)/shard_map/ppermute | solution.py:32
  167.2 2.9 %all-to-all-done.2 = bf16[32,32,384]{2,1,0:T(8,128)(2,1)S(1)} async-done(((bf16[32,32,384]{2,1,0:T(8,128)(2,1)}), bf16[32,32,384]{2,1,0:T(8,128)(2,1)S(1)}, u32[]{:S(2)}, u32[]{:S(2)}) %all-to-all-start.2) | async-done | bytes 786464 | tf_op jit(solution)/shard_map/all_to_all | solution.py:342
  (55 shorter events, 21.9 us)
Async XLA Ops:
  4.1 33.8 %all-to-all-start.1 = ((bf16[32,32,512]{2,1,0:T(8,128)(2,1)}), bf16[32,32,512]{2,1,0:T(8,128)(2,1)S(1)}, u32[]{:S(2)}, u32[]{:S(2)}) async-start(bf16[32,32,512]{2,1,0:T(8,128)(2,1)} %get-tuple-element.41), calls=%async_computation.1 | async-start | bytes 2097152 | tf_op jit(solution)/shard_map/all_to_all | solution.py:223
  12.7 15.2 %collective-permute-start.1 = (bf16[256,512]{1,0:T(8,128)(2,1)}, bf16[256,512]{1,0:T(8,128)(2,1)S(1)}, u32[]{:S(2)}, u32[]{:S(2)}) collective-permute-start(bf16[256,512]{1,0:T(8,128)(2,1)} %c0.1), channel_id=1, source_target_pairs={{0,3},{1,0},{2,1},{3,2},{4,7},{5,4},{6,5},{7,6},{8,11},{9,8},{10,9... | collective-permute-start | bytes 786440 | tf_op jit(solution)/shard_map/ppermute | solution.py:32
  16.5 14.4 %collective-permute-start.2 = (bf16[256,512]{1,0:T(8,128)(2,1)}, bf16[256,512]{1,0:T(8,128)(2,1)S(1)}, u32[]{:S(2)}, u32[]{:S(2)}) collective-permute-start(bf16[256,512]{1,0:T(8,128)(2,1)} %c0.1), channel_id=1, source_target_pairs={{0,1},{1,2},{2,3},{3,0},{4,5},{5,6},{6,7},{7,4},{8,9},{9,10},{10,1... | collective-permute-start | bytes 786440 | tf_op jit(solution)/shard_map/ppermute | solution.py:32
  16.5 18.5 %collective-permute-start = (bf16[256,512]{1,0:T(8,128)(2,1)}, bf16[256,512]{1,0:T(8,128)(2,1)S(1)}, u32[]{:S(2)}, u32[]{:S(2)}) collective-permute-start(bf16[256,512]{1,0:T(8,128)(2,1)} %c0.1), channel_id=1, source_target_pairs={{0,2},{1,3},{2,0},{3,1},{4,6},{5,7},{6,4},{7,5},{8,10},{9,11},{10,... | collective-permute-start | bytes 786440 | tf_op jit(solution)/shard_map/ppermute | solution.py:32
  37.9 60.7 %all-to-all-start = ((bf16[32,32,2048]{2,1,0:T(8,128)(2,1)}), bf16[32,32,2048]{2,1,0:T(8,128)(2,1)}, u32[]{:S(2)}, u32[]{:S(2)}) async-start(bf16[32,32,2048]{2,1,0:T(8,128)(2,1)} %route_far.1), calls=%async_computation | async-start | bytes 8388608 | tf_op jit(solution)/shard_map/all_to_all | solution.py:257
  46.4 13.4 %collective-permute-start.6 = (bf16[16,4,8,512]{3,2,1,0:T(8,128)(2,1)S(1)}, bf16[16,4,8,512]{3,2,1,0:T(8,128)(2,1)S(1)}, u32[]{:S(2)}, u32[]{:S(2)}) collective-permute-start(bf16[16,4,8,512]{3,2,1,0:T(8,128)(2,1)S(1)} %get-tuple-element.75), channel_id=1, source_target_pairs={{0,3},{1,0},{2,1},{3,2},{4,7},{5,4},{6,5},{7,6},{8,11},{9,8},{10,9... | collective-permute-start | bytes 1572872 | tf_op jit(solution)/shard_map/ppermute | solution.py:32
  46.5 14.5 %collective-permute-start.3 = (bf16[16,4,8,512]{3,2,1,0:T(8,128)(2,1)S(1)}, bf16[16,4,8,512]{3,2,1,0:T(8,128)(2,1)S(1)}, u32[]{:S(2)}, u32[]{:S(2)}) collective-permute-start(bf16[16,4,8,512]{3,2,1,0:T(8,128)(2,1)S(1)} %get-tuple-element.76), channel_id=1, source_target_pairs={{0,1},{1,2},{2,3},{3,0},{4,5},{5,6},{6,7},{7,4},{8,9},{9,10},{10,1... | collective-permute-start | bytes 1572872 | tf_op jit(solution)/shard_map/ppermute | solution.py:32
  48.0 24.2 %collective-permute-start.4 = (bf16[16,4,8,512]{3,2,1,0:T(8,128)(2,1)S(1)}, bf16[16,4,8,512]{3,2,1,0:T(8,128)(2,1)S(1)}, u32[]{:S(2)}, u32[]{:S(2)}) collective-permute-start(bf16[16,4,8,512]{3,2,1,0:T(8,128)(2,1)S(1)} %get-tuple-element.75), channel_id=1, source_target_pairs={{0,1},{1,2},{2,3},{3,0},{4,5},{5,6},{6,7},{7,4},{8,9},{9,10},{10,1... | collective-permute-start | bytes 1572872 | tf_op jit(solution)/shard_map/ppermute | solution.py:32
  48.0 24.1 %collective-permute-start.5 = (bf16[16,4,8,512]{3,2,1,0:T(8,128)(2,1)S(1)}, bf16[16,4,8,512]{3,2,1,0:T(8,128)(2,1)S(1)}, u32[]{:S(2)}, u32[]{:S(2)}) collective-permute-start(bf16[16,4,8,512]{3,2,1,0:T(8,128)(2,1)S(1)} %get-tuple-element.76), channel_id=1, source_target_pairs={{0,3},{1,0},{2,1},{3,2},{4,7},{5,4},{6,5},{7,6},{8,11},{9,8},{10,9... | collective-permute-start | bytes 1572872 | tf_op jit(solution)/shard_map/ppermute | solution.py:32
  59.8 23.6 %copy-start.1 = (bf16[16,4,8,512]{3,2,1,0:T(8,128)(2,1)}, bf16[16,4,8,512]{3,2,1,0:T(8,128)(2,1)S(1)}, u32[]{:S(2)}) copy-start(bf16[16,4,8,512]{3,2,1,0:T(8,128)(2,1)S(1)} %collective-permute-done.6.right_b) | copy-start | bytes 1572868
  59.8 22.5 %collective-permute-start.8 = (bf16[16,4,8,512]{3,2,1,0:T(8,128)(2,1)S(1)}, bf16[16,4,8,512]{3,2,1,0:T(8,128)(2,1)S(1)}, u32[]{:S(2)}, u32[]{:S(2)}) collective-permute-start(bf16[16,4,8,512]{3,2,1,0:T(8,128)(2,1)S(1)} %collective-permute-done.6.right_b), channel_id=1, source_target_pairs={{0,3},{1,0},{2,1},{3,2},{4,7},{5,4},{6,5},{7,6},{8,11},{9,8},{10,9... | collective-permute-start | bytes 1572872 | tf_op jit(solution)/shard_map/ppermute | solution.py:32
  61.1 22.3 %copy-start.2 = (bf16[16,4,8,512]{3,2,1,0:T(8,128)(2,1)}, bf16[16,4,8,512]{3,2,1,0:T(8,128)(2,1)S(1)}, u32[]{:S(2)}) copy-start(bf16[16,4,8,512]{3,2,1,0:T(8,128)(2,1)S(1)} %collective-permute-done.3.left_a) | copy-start | bytes 1572868
  61.1 22.3 %collective-permute-start.7 = (bf16[16,4,8,512]{3,2,1,0:T(8,128)(2,1)S(1)}, bf16[16,4,8,512]{3,2,1,0:T(8,128)(2,1)S(1)}, u32[]{:S(2)}, u32[]{:S(2)}) collective-permute-start(bf16[16,4,8,512]{3,2,1,0:T(8,128)(2,1)S(1)} %collective-permute-done.3.left_a), channel_id=1, source_target_pairs={{0,1},{1,2},{2,3},{3,0},{4,5},{5,6},{6,7},{7,4},{8,9},{9,10},{10,1... | collective-permute-start | bytes 1572872 | tf_op jit(solution)/shard_map/ppermute | solution.py:32
  109.9 19.1 %collective-permute-start.9 = (bf16[16,4,8,384]{3,2,1,0:T(8,128)(2,1)}, bf16[16,4,8,384]{3,2,1,0:T(8,128)(2,1)}, u32[]{:S(2)}, u32[]{:S(2)}) collective-permute-start(bf16[16,4,8,384]{3,2,1,0:T(8,128)(2,1)} %get-tuple-element.45), channel_id=1, source_target_pairs={{0,1},{1,2},{2,3},{3,0},{4,5},{5,6},{6,7},{7,4},{8,9},{9,10},{10,1... | collective-permute-start | bytes 1179656 | tf_op jit(solution)/shard_map/ppermute | solution.py:32
  110.0 19.0 %collective-permute-start.10 = (bf16[16,4,8,384]{3,2,1,0:T(8,128)(2,1)}, bf16[16,4,8,384]{3,2,1,0:T(8,128)(2,1)}, u32[]{:S(2)}, u32[]{:S(2)}) collective-permute-start(bf16[16,4,8,384]{3,2,1,0:T(8,128)(2,1)} %get-tuple-element.46), channel_id=1, source_target_pairs={{0,3},{1,0},{2,1},{3,2},{4,7},{5,4},{6,5},{7,6},{8,11},{9,8},{10,9... | collective-permute-start | bytes 1179656 | tf_op jit(solution)/shard_map/ppermute | solution.py:32
  112.7 33.9 %all-to-all-start.3 = ((bf16[32,32,640]{2,1,0:T(8,128)(2,1)}), bf16[32,32,640]{2,1,0:T(8,128)(2,1)}, u32[]{:S(2)}, u32[]{:S(2)}) async-start(bf16[32,32,640]{2,1,0:T(8,128)(2,1)} %bitcast.17), calls=%async_computation.3 | async-start | bytes 2621440 | tf_op jit(solution)/shard_map/all_to_all | solution.py:306
  120.5 22.4 %collective-permute-start.12 = (bf16[16,4,8,384]{3,2,1,0:T(8,128)(2,1)}, bf16[16,4,8,384]{3,2,1,0:T(8,128)(2,1)}, u32[]{:S(2)}, u32[]{:S(2)}) collective-permute-start(bf16[16,4,8,384]{3,2,1,0:T(8,128)(2,1)} %get-tuple-element.52), channel_id=1, source_target_pairs={{0,1},{1,2},{2,3},{3,0},{4,5},{5,6},{6,7},{7,4},{8,9},{9,10},{10,1... | collective-permute-start | bytes 1179656 | tf_op jit(solution)/shard_map/ppermute | solution.py:32
  120.6 22.3 %collective-permute-start.13 = (bf16[16,4,8,384]{3,2,1,0:T(8,128)(2,1)}, bf16[16,4,8,384]{3,2,1,0:T(8,128)(2,1)}, u32[]{:S(2)}, u32[]{:S(2)}) collective-permute-start(bf16[16,4,8,384]{3,2,1,0:T(8,128)(2,1)} %get-tuple-element.53), channel_id=1, source_target_pairs={{0,3},{1,0},{2,1},{3,2},{4,7},{5,4},{6,5},{7,6},{8,11},{9,8},{10,9... | collective-permute-start | bytes 1179656 | tf_op jit(solution)/shard_map/ppermute | solution.py:32
  130.9 13.4 %collective-permute-start.11 = (bf16[16,4,8,384]{3,2,1,0:T(8,128)(2,1)}, bf16[16,4,8,384]{3,2,1,0:T(8,128)(2,1)}, u32[]{:S(2)}, u32[]{:S(2)}) collective-permute-start(bf16[16,4,8,384]{3,2,1,0:T(8,128)(2,1)} %add_convert_fusion.3), channel_id=1, source_target_pairs={{0,1},{1,2},{2,3},{3,0},{4,5},{5,6},{6,7},{7,4},{8,9},{9,10},{10,1... | collective-permute-start | bytes 1179656 | tf_op jit(solution)/shard_map/ppermute | solution.py:32
  132.7 10.3 %collective-permute-start.14 = (bf16[16,4,8,384]{3,2,1,0:T(8,128)(2,1)}, bf16[16,4,8,384]{3,2,1,0:T(8,128)(2,1)}, u32[]{:S(2)}, u32[]{:S(2)}) collective-permute-start(bf16[16,4,8,384]{3,2,1,0:T(8,128)(2,1)} %add_convert_fusion.2), channel_id=1, source_target_pairs={{0,3},{1,0},{2,1},{3,2},{4,7},{5,4},{6,5},{7,6},{8,11},{9,8},{10,9... | collective-permute-start | bytes 1179656 | tf_op jit(solution)/shard_map/ppermute | solution.py:32
  146.5 23.5 %all-to-all-start.2 = ((bf16[32,32,384]{2,1,0:T(8,128)(2,1)}), bf16[32,32,384]{2,1,0:T(8,128)(2,1)S(1)}, u32[]{:S(2)}, u32[]{:S(2)}) async-start(bf16[32,32,384]{2,1,0:T(8,128)(2,1)} %maximum_bitcast_fusion), calls=%async_computation.2 | async-start | bytes 1572864 | tf_op jit(solution)/shard_map/all_to_all | solution.py:342
  158.6 6.1 %collective-permute-start.15 = (bf16[288,128]{1,0:T(8,128)(2,1)}, bf16[288,128]{1,0:T(8,128)(2,1)S(1)}, u32[]{:S(2)}, u32[]{:S(2)}) collective-permute-start(bf16[288,128]{1,0:T(8,128)(2,1)} %get-tuple-element.67), channel_id=1, source_target_pairs={{0,1},{1,2},{2,3},{3,0},{4,5},{5,6},{6,7},{7,4},{8,9},{9,10},{10,1... | collective-permute-start | bytes 221192 | tf_op jit(solution)/shard_map/ppermute | solution.py:32
  158.6 8.6 %collective-permute-start.16 = (bf16[288,128]{1,0:T(8,128)(2,1)}, bf16[288,128]{1,0:T(8,128)(2,1)S(1)}, u32[]{:S(2)}, u32[]{:S(2)}) collective-permute-start(bf16[288,128]{1,0:T(8,128)(2,1)} %get-tuple-element.68), channel_id=1, source_target_pairs={{0,2},{1,3},{2,0},{3,1},{4,6},{5,7},{6,4},{7,5},{8,10},{9,11},{10,... | collective-permute-start | bytes 221192 | tf_op jit(solution)/shard_map/ppermute | solution.py:32
  163.2 4.0 %collective-permute-start.17 = (bf16[288,128]{1,0:T(8,128)(2,1)}, bf16[288,128]{1,0:T(8,128)(2,1)S(1)}, u32[]{:S(2)}, u32[]{:S(2)}) collective-permute-start(bf16[288,128]{1,0:T(8,128)(2,1)} %get-tuple-element.69), channel_id=1, source_target_pairs={{0,3},{1,0},{2,1},{3,2},{4,7},{5,4},{6,5},{7,6},{8,11},{9,8},{10,9... | collective-permute-start | bytes 221192 | tf_op jit(solution)/shard_map/ppermute | solution.py:32
  (8 other events, 73.4 us)

commit v5 on v4

--- a/solution.py
+++ b/solution.py
@@ -76,17 +76,12 @@
     return pick, w
 
 
-def route_near(z_ref, dest, weights, c0, c1, c3, pay):
+def route_rest(z_ref, dest, weights, c0, c1, c2, c3, pay):
     pick, w = picked(dest, weights)
-    for off, c in ((0, c0), (1, c1), (3, c3)):
+    for off, c in enumerate((c0, c1, c2, c3)):
         dy = (dot(pick, c[...], 1, 0) * w).astype(BF)
         q = lax.rem(z_ref[0] + off, NZ)
         pay[:, :, pl.ds(pl.multiple_of(q * QF, QF), QF)] = dy.reshape(8, 32, QF)
-
-
-def route_far(z_ref, dest, weights, c2, near, pay):
-    pick, w = picked(dest, weights)
-    pay[...] = (dot(pick, c2[...], 1, 0) * w).astype(BF).reshape(8, 32, QF)
 
 
 def merged(v):
@@ -225,35 +220,15 @@
     c1, c2, c3 = shift(cotangent, -1), shift(cotangent, 2), shift(cotangent, 1)
     c1, c2, c3 = (pltpu.with_memory_space_constraint(c, pltpu.VMEM) for c in (c1, c2, c3))
     pay_rest = pl.pallas_call(
-        route_near,
+        route_rest,
         grid=(4,),
-        in_specs=[smem, whole((2, TOK)), whole((2, TOK))] + [whole((TOK, QF))] * 3,
+        in_specs=[smem, whole((2, TOK)), whole((2, TOK))] + [whole((TOK, QF))] * 4,
         out_specs=pl.BlockSpec((8, 32, D), lambda i: (i, 0, 0)),
         out_shape=shape((OWN, 32, D)),
         compiler_params=params(ROUTE),
-        cost_estimate=cost(6e8, 5e6),
-        name="route_near",
-    )(z, dest, weights, cotangent, c1, c3)
-    fixed = pl.BlockSpec((2, TOK), lambda i, z: (0, 0))
-    pay_rest = pl.pallas_call(
-        route_far,
-        grid_spec=pltpu.PrefetchScalarGridSpec(
-            num_scalar_prefetch=1,
-            grid=(4,),
-            in_specs=[
-                fixed,
-                fixed,
-                pl.BlockSpec((TOK, QF), lambda i, z: (0, 0)),
-                pl.BlockSpec(memory_space=pl.ANY),
-            ],
-            out_specs=pl.BlockSpec((8, 32, QF), lambda i, z: (i, 0, lax.rem(z[0] + 2, NZ))),
-        ),
-        out_shape=shape((OWN, 32, D)),
-        input_output_aliases={4: 0},
-        compiler_params=params(ROUTE),
-        cost_estimate=cost(2e8, 2e6),
-        name="route_far",
-    )(z, dest, weights, c2, pay_rest)
+        cost_estimate=cost(8e8, 6e6),
+        name="route_rest",
+    )(z, dest, weights, cotangent, c1, c2, c3)
     rest = lax.all_to_all(pay_rest, "expert", split_axis=0, concat_axis=0, tiled=True)
     rest = rest.reshape(OWN, LOC, CAP, D)
 
@@ -307,17 +282,6 @@
         part.reshape(OWN, 32, WR), "expert", split_axis=0, concat_axis=0, tiled=True
     ).reshape(OWN * 32, WR)
 
-    down_grad, pick = pl.pallas_call(
-        grads_down,
-        grid=(LOC,),
-        in_specs=[whole((2, TOK)), by_expert(OWN, D), hid_spec],
-        out_specs=[leading(QH, D), pl.BlockSpec((TOK, 256), lambda e: (0, e))],
-        out_shape=[shape((LOC, QH, D)), shape((TOK, OWN * LOC * CAP))],
-        compiler_params=params(),
-        cost_estimate=cost(1.1e9, 10e6),
-        name="grads_down",
-    )(dest, rest, h)
-    relay_t, relay_b, pick = lax.optimization_barrier((relay_t, relay_b, pick))
 
     sum_t = (o1t.astype(F32) + relay_t.astype(F32)).astype(BF)
     sum_b = (o3b.astype(F32) + relay_b.astype(F32)).astype(BF)
@@ -339,6 +303,17 @@
     sum_t = o0t.astype(F32) + from_l_t.astype(F32) + from_r_t.astype(F32)
     sum_b = o0b.astype(F32) + from_l_b.astype(F32) + from_r_b.astype(F32)
     sums = jnp.concatenate([sum_t.astype(BF), sum_b.astype(BF)], axis=0)
+    sums, h = lax.optimization_barrier((sums, h))
+    down_grad, pick = pl.pallas_call(
+        grads_down,
+        grid=(LOC,),
+        in_specs=[whole((2, TOK)), by_expert(OWN, D), hid_spec],
+        out_specs=[leading(QH, D), pl.BlockSpec((TOK, 256), lambda e: (0, e))],
+        out_shape=[shape((LOC, QH, D)), shape((TOK, OWN * LOC * CAP))],
+        compiler_params=params(),
+        cost_estimate=cost(1.1e9, 10e6),
+        name="grads_down",
+    )(dest, rest, h)
     back = lax.all_to_all(
         sums.reshape(OWN, 32, RA), "expert", split_axis=0, concat_axis=0, tiled=True
     ).reshape(OWN * 32, RA)

time: 173 us -> 164 us (0.948)
  waiting for transfers between devices: 58.4 us -> 50.6 us
  Pallas kernels: 48.1 us -> 45.4 us
    ppermute x18, waiting for transfers between devices: 48.4 us -> 44.5 us  [shift(): return lax.ppermute(x, 'hidden', [(i, (i + d) % NZ) for i in range(NZ)])]
    ppermute x18, starting transfers between devices: 23.6 us -> 26.5 us  [shift(): return lax.ppermute(x, 'hidden', [(i, (i + d) % NZ) for i in range(NZ)])]
    pallas_call x2 -> x1, Pallas kernels: 6.99 us -> 4.31 us  [on_device(): pl.pallas_call(route_rest, grid=(4,), in_specs=[smem, whole((2, TOK)), wh...]
    all_to_all x1, waiting for transfers between devices: 7.09 us -> 4.95 us  [on_device(): lax.all_to_all(pay_rest, 'expert', split_axis=0, concat_axis=0, tiled=True)]
    all_to_all x1, waiting for transfers between devices: 2.87 us -> 1.07 us  [on_device(): lax.all_to_all(sums.reshape(OWN, 32, RA), 'expert', split_axis=0, concat_...]
  transfers between devices with their start and end apart: 22 -> 22, of which waited for: 11 -> 9; matrix products, arithmetic and copies ran while one was open for 4% -> 5% of each run, Pallas kernels for 18% -> 17%
where the time goes in v5:
time: 164 us
  starting transfers between devices  59.4 us (36%)
  waiting for transfers between devices  50.6 us (31%)
  Pallas kernels  45.4 us (28%)
  other arithmetic  7.29 us (4%)
    ppermute x18, waiting for transfers between devices, shift(): return lax.ppermute(x, 'hidden', [(i, (i + d) % NZ) for i in range(NZ)])  44.5 us
    ppermute x18, starting transfers between devices, shift(): return lax.ppermute(x, 'hidden', [(i, (i + d) % NZ) for i in range(NZ)])  26.5 us
    pallas_call x1, Pallas kernels, on_device(): pl.pallas_call(middle, grid=(LOC,), in_specs=[smem, by_expert(OWN, D)] +...  11.3 us
    all_to_all x1, starting transfers between devices, on_device(): got = lax.all_to_all(pay, 'expert', split_axis=0, concat_axis=0, tiled=True)  8.59 us
    all_to_all x1, starting transfers between devices, on_device(): lax.all_to_all(sums.reshape(OWN, 32, RA), 'expert', split_axis=0, concat_...  8.47 us
    all_to_all x1, starting transfers between devices, on_device(): lax.all_to_all(pay_rest, 'expert', split_axis=0, concat_axis=0, tiled=True)  8.12 us
    pallas_call x1, Pallas kernels, on_device(): pl.pallas_call(gates, grid=(LOC,), in_specs=[smem, by_expert(OWN, QF)] +...  8.1 us
    all_to_all x1, starting transfers between devices, on_device(): lax.all_to_all(part.reshape(OWN, 32, WR), 'expert', split_axis=0, concat_...  7.72 us
  transfers between devices with their start and end apart: 22, of which 9 were waited for; matrix products, arithmetic and copies ran while one was open for 5% of the time, Pallas kernels for 17%

profile of v5, /device:TPU:1, one launch (start us, length us, event | category | flops | bytes accessed | tf_op | source)
XLA Modules:
  0.0 163.6 jit_solution(1629487882303251426)
XLA Ops:
  0.6 3.4 %route_first.1 = (bf16[32,32,512]{2,1,0:T(8,128)(2,1)}, s32[2,256]{1,0:T(2,128)}) custom-call(s32[2,256]{1,0:T(2,128)} %bitcast.19, bf16[256,512]{1,0:T(8,128)(2,1)} %tokens.1), custom_call_target="tpu_custom_call" | custom-call | flops 500000000 | bytes 4000000 | tf_op jit(solution)/shard_map/route_first/pallas_call | solution.py:207
  4.1 8.6 %all-to-all-start.1 = ((bf16[32,32,512]{2,1,0:T(8,128)(2,1)}), bf16[32,32,512]{2,1,0:T(8,128)(2,1)S(1)}, u32[]{:S(2)}, u32[]{:S(2)}) async-start(bf16[32,32,512]{2,1,0:T(8,128)(2,1)} %get-tuple-element.40), calls=%async_computation.1 | async-start | bytes 2097152 | tf_op jit(solution)/shard_map/all_to_all | solution.py:218
  12.7 3.7 %collective-permute-start.1 = (bf16[256,512]{1,0:T(8,128)(2,1)}, bf16[256,512]{1,0:T(8,128)(2,1)S(1)}, u32[]{:S(2)}, u32[]{:S(2)}) collective-permute-start(bf16[256,512]{1,0:T(8,128)(2,1)} %c0.1), channel_id=1, source_target_pairs={{0,2},{1,3},{2,0},{3,1},{4,6},{5,7},{6,4},{7,5},{8,10},{9,11},{10,... | collective-permute-start | bytes 786440 | tf_op jit(solution)/shard_map/ppermute | solution.py:32
  17.8 5.3 %collective-permute-done.1.c2 = bf16[256,512]{1,0:T(8,128)(2,1)S(1)} collective-permute-done((bf16[256,512]{1,0:T(8,128)(2,1)}, bf16[256,512]{1,0:T(8,128)(2,1)S(1)}, u32[]{:S(2)}, u32[]{:S(2)}) %collective-permute-start.1) | collective-permute-done | bytes 262176 | tf_op jit(solution)/shard_map/ppermute | solution.py:32
  23.1 6.0 %collective-permute-done.c1 = bf16[256,512]{1,0:T(8,128)(2,1)S(1)} collective-permute-done((bf16[256,512]{1,0:T(8,128)(2,1)}, bf16[256,512]{1,0:T(8,128)(2,1)S(1)}, u32[]{:S(2)}, u32[]{:S(2)}) %collective-permute-start) | collective-permute-done | bytes 262176 | tf_op jit(solution)/shard_map/ppermute | solution.py:32
  29.2 4.3 %route_rest.1 = bf16[32,32,2048]{2,1,0:T(8,128)(2,1)} custom-call(s32[1]{0:T(128)} %bitcast.1.z_ref, s32[2,256]{1,0:T(2,128)} %get-tuple-element.39.dest, f32[2,256]{1,0:T(2,128)} %bitcast.17, bf16[256,512]{1,0:T(8,128)(2,1)} %c0.1, bf16[256,512]{1,0:T(8,128)(2,1)S(1)} %collective-permute-done.c1, bf16[256,512]{1,0:T(8,128)(2,1)S(1)} %collective-permute-done.1.c2, ...), custom_call_target="tpu_custom_call" | custom-call | flops 800000000 | bytes 6000000 | tf_op jit(solution)/shard_map/route_rest/pallas_call | solution.py:222
  33.5 8.1 %all-to-all-start = ((bf16[32,32,2048]{2,1,0:T(8,128)(2,1)}), bf16[32,32,2048]{2,1,0:T(8,128)(2,1)}, u32[]{:S(2)}, u32[]{:S(2)}) async-start(bf16[32,32,2048]{2,1,0:T(8,128)(2,1)} %route_rest.1), calls=%async_computation | async-start | bytes 8388608 | tf_op jit(solution)/shard_map/all_to_all | solution.py:232
  44.1 2.7 %collective-permute-start.5 = (bf16[16,4,8,512]{3,2,1,0:T(8,128)(2,1)S(1)}, bf16[16,4,8,512]{3,2,1,0:T(8,128)(2,1)S(1)}, u32[]{:S(2)}, u32[]{:S(2)}) collective-permute-start(bf16[16,4,8,512]{3,2,1,0:T(8,128)(2,1)S(1)} %get-tuple-element.74), channel_id=1, source_target_pairs={{0,3},{1,0},{2,1},{3,2},{4,7},{5,4},{6,5},{7,6},{8,11},{9,8},{10,9... | collective-permute-start | bytes 1572872 | tf_op jit(solution)/shard_map/ppermute | solution.py:32
  46.8 8.3 %collective-permute-done.6.right_b = bf16[16,4,8,512]{3,2,1,0:T(8,128)(2,1)S(1)} collective-permute-done((bf16[16,4,8,512]{3,2,1,0:T(8,128)(2,1)S(1)}, bf16[16,4,8,512]{3,2,1,0:T(8,128)(2,1)S(1)}, u32[]{:S(2)}, u32[]{:S(2)}) %collective-permute-start.6) | collective-permute-done | bytes 524320 | tf_op jit(solution)/shard_map/ppermute | solution.py:32
  55.1 3.5 %collective-permute-start.8 = (bf16[16,4,8,512]{3,2,1,0:T(8,128)(2,1)S(1)}, bf16[16,4,8,512]{3,2,1,0:T(8,128)(2,1)S(1)}, u32[]{:S(2)}, u32[]{:S(2)}) collective-permute-start(bf16[16,4,8,512]{3,2,1,0:T(8,128)(2,1)S(1)} %collective-permute-done.6.right_b), channel_id=1, source_target_pairs={{0,3},{1,0},{2,1},{3,2},{4,7},{5,4},{6,5},{7,6},{8,11},{9,8},{10,9... | collective-permute-start | bytes 1572872 | tf_op jit(solution)/shard_map/ppermute | solution.py:32
  58.6 10.9 %collective-permute-done.4.left_b = bf16[16,4,8,512]{3,2,1,0:T(8,128)(2,1)S(1)} collective-permute-done((bf16[16,4,8,512]{3,2,1,0:T(8,128)(2,1)S(1)}, bf16[16,4,8,512]{3,2,1,0:T(8,128)(2,1)S(1)}, u32[]{:S(2)}, u32[]{:S(2)}) %collective-permute-start.4) | collective-permute-done | bytes 524320 | tf_op jit(solution)/shard_map/ppermute | solution.py:32
  69.5 8.0 %collective-permute-done.8.far_b = bf16[16,4,8,512]{3,2,1,0:T(8,128)(2,1)S(1)} collective-permute-done((bf16[16,4,8,512]{3,2,1,0:T(8,128)(2,1)S(1)}, bf16[16,4,8,512]{3,2,1,0:T(8,128)(2,1)S(1)}, u32[]{:S(2)}, u32[]{:S(2)}) %collective-permute-start.8) | collective-permute-done | bytes 524320 | tf_op jit(solution)/shard_map/ppermute | solution.py:32
  77.6 3.2 %collective-permute-done.7.far_a = bf16[16,4,8,512]{3,2,1,0:T(8,128)(2,1)S(1)} collective-permute-done((bf16[16,4,8,512]{3,2,1,0:T(8,128)(2,1)S(1)}, bf16[16,4,8,512]{3,2,1,0:T(8,128)(2,1)S(1)}, u32[]{:S(2)}, u32[]{:S(2)}) %collective-permute-start.7) | collective-permute-done | bytes 524320 | tf_op jit(solution)/shard_map/ppermute | solution.py:32
  80.8 8.1 %gates.1 = (bf16[4,256,2048]{2,1,0:T(8,128)(2,1)}, bf16[4,256,256]{2,1,0:T(8,128)(2,1)}, f32[4,256,256]{2,1,0:T(8,128)}, f32[4,256,256]{2,1,0:T(8,128)}) custom-call(s32[1]{0:T(128)} %bitcast.1.z_ref, bf16[32,4,8,512]{3,2,1,0:T(8,128)(2,1)} %bitcast.15, bf16[16,4,8,512]{3,2,1,0:T(8,128)(2,1)} %copy-done.2, ...), custom_call_target="tpu_custom_call" | custom-call | flops 2200000000 | bytes 19000000 | tf_op jit(solution)/shard_map/gates/pallas_call | solution.py:251
  88.9 5.0 %all-to-all-done = bf16[32,32,2048]{2,1,0:T(8,128)(2,1)} async-done(((bf16[32,32,2048]{2,1,0:T(8,128)(2,1)}), bf16[32,32,2048]{2,1,0:T(8,128)(2,1)}, u32[]{:S(2)}, u32[]{:S(2)}) %all-to-all-start) | async-done | bytes 4194336 | tf_op jit(solution)/shard_map/all_to_all | solution.py:232
  93.8 11.3 %middle.1 = (bf16[16,4,8,384]{3,2,1,0:T(8,128)(2,1)}, bf16[16,4,8,384]{3,2,1,0:T(8,128)(2,1)}, bf16[16,4,8,384]{3,2,1,0:T(8,128)(2,1)}, bf16[16,4,8,384]{3,2,1,0...) custom-call(s32[1]{0:T(128)} %bitcast.1.z_ref, ...), custom_call_target="tpu_custom_call" | custom-call | flops 2700000000 | bytes 27000000 | tf_op jit(solution)/shard_map/middle/pallas_call | solution.py:264
  107.9 7.7 %all-to-all-start.3 = ((bf16[32,32,640]{2,1,0:T(8,128)(2,1)}), bf16[32,32,640]{2,1,0:T(8,128)(2,1)}, u32[]{:S(2)}, u32[]{:S(2)}) async-start(bf16[32,32,640]{2,1,0:T(8,128)(2,1)} %bitcast.16), calls=%async_computation.3 | async-start | bytes 2621440 | tf_op jit(solution)/shard_map/all_to_all | solution.py:281
  122.1 2.7 %collective-permute-start.14 = (bf16[16,4,8,384]{3,2,1,0:T(8,128)(2,1)}, bf16[16,4,8,384]{3,2,1,0:T(8,128)(2,1)}, u32[]{:S(2)}, u32[]{:S(2)}) collective-permute-start(bf16[16,4,8,384]{3,2,1,0:T(8,128)(2,1)} %add_convert_fusion.2), channel_id=1, source_target_pairs={{0,3},{1,0},{2,1},{3,2},{4,7},{5,4},{6,5},{7,6},{8,11},{9,8},{10,9... | collective-permute-start | bytes 1179656 | tf_op jit(solution)/shard_map/ppermute | solution.py:32
  124.8 7.5 %grads_up.1 = (bf16[4,2048,256]{2,1,0:T(8,128)(2,1)}, bf16[4,2048,256]{2,1,0:T(8,128)(2,1)}) custom-call(bf16[4,256,2048]{2,1,0:T(8,128)(2,1)} %get-tuple-element.49.x, bf16[4,256,256]{2,1,0:T(8,128)(2,1)} %get-tuple-element.54.dg, bf16[4,256,256]{2,1,0:T(8,128)(2,1)} %get-tuple-element.55.du), custom_call_target="tpu_custom_call" | custom-call | flops 12000000000 | bytes 20000000 | tf_op jit(solution)/shard_map/grads_up/pallas_call | solution.py:292
  132.3 2.7 %collective-permute-done.14 = bf16[16,4,8,384]{3,2,1,0:T(8,128)(2,1)} collective-permute-done((bf16[16,4,8,384]{3,2,1,0:T(8,128)(2,1)}, bf16[16,4,8,384]{3,2,1,0:T(8,128)(2,1)}, u32[]{:S(2)}, u32[]{:S(2)}) %collective-permute-start.14) | collective-permute-done | bytes 393248 | tf_op jit(solution)/shard_map/ppermute | solution.py:32
  138.6 8.5 %all-to-all-start.2 = ((bf16[32,32,384]{2,1,0:T(8,128)(2,1)}), bf16[32,32,384]{2,1,0:T(8,128)(2,1)S(1)}, u32[]{:S(2)}, u32[]{:S(2)}) async-start(bf16[32,32,384]{2,1,0:T(8,128)(2,1)} %bitcast.7), calls=%async_computation.2 | async-start | bytes 1572864 | tf_op jit(solution)/shard_map/all_to_all | solution.py:317
  147.1 2.8 %pick_pairs.1 = (bf16[288,128]{1,0:T(8,128)(2,1)}, bf16[288,128]{1,0:T(8,128)(2,1)}, bf16[288,128]{1,0:T(8,128)(2,1)}, bf16[288,128]{1,0:T(8,128)(2,1)}) custom-call(s32[2,256]{1,0:T(2,128)} %get-tuple-element.39.dest, bf16[1024,640]{1,0:T(8,128)(2,1)} %bitcast.10.back), custom_call_target="tpu_custom_call" | custom-call | flops 400000000 | bytes 3000000 | tf_op jit(solution)/shard_map/pick_pairs/pallas_call | solution.py:322
  150.1 4.4 %collective-permute-start.16 = (bf16[288,128]{1,0:T(8,128)(2,1)}, bf16[288,128]{1,0:T(8,128)(2,1)S(1)}, u32[]{:S(2)}, u32[]{:S(2)}) collective-permute-start(bf16[288,128]{1,0:T(8,128)(2,1)} %get-tuple-element.66), channel_id=1, source_target_pairs={{0,2},{1,3},{2,0},{3,1},{4,6},{5,7},{6,4},{7,5},{8,10},{9,11},{10,... | collective-permute-start | bytes 221192 | tf_op jit(solution)/shard_map/ppermute | solution.py:32
  154.5 5.7 %grads_down.1 = (bf16[4,256,2048]{2,1,0:T(8,128)(2,1)}, bf16[256,1024]{1,0:T(8,128)(2,1)}) custom-call(s32[2,256]{1,0:T(2,128)} %get-tuple-element.39.dest, bf16[32,4,8,2048]{3,2,1,0:T(8,128)(2,1)} %bitcast.3.rest, bf16[4,256,256]{2,1,0:T(8,128)(2,1)} %get-tuple-element.60.h_in.h), custom_call_target="tpu_custom_call" | custom-call | flops 1100000000 | bytes 10000000 | tf_op jit(solution)/shard_map/grads_down/pallas_call | solution.py:307
  (48 shorter events, 20.3 us)
Async XLA Ops:
  4.1 29.4 %all-to-all-start.1 = ((bf16[32,32,512]{2,1,0:T(8,128)(2,1)}), bf16[32,32,512]{2,1,0:T(8,128)(2,1)S(1)}, u32[]{:S(2)}, u32[]{:S(2)}) async-start(bf16[32,32,512]{2,1,0:T(8,128)(2,1)} %get-tuple-element.40), calls=%async_computation.1 | async-start | bytes 2097152 | tf_op jit(solution)/shard_map/all_to_all | solution.py:218
  12.7 10.5 %collective-permute-start.1 = (bf16[256,512]{1,0:T(8,128)(2,1)}, bf16[256,512]{1,0:T(8,128)(2,1)S(1)}, u32[]{:S(2)}, u32[]{:S(2)}) collective-permute-start(bf16[256,512]{1,0:T(8,128)(2,1)} %c0.1), channel_id=1, source_target_pairs={{0,2},{1,3},{2,0},{3,1},{4,6},{5,7},{6,4},{7,5},{8,10},{9,11},{10,... | collective-permute-start | bytes 786440 | tf_op jit(solution)/shard_map/ppermute | solution.py:32
  16.3 12.8 %collective-permute-start = (bf16[256,512]{1,0:T(8,128)(2,1)}, bf16[256,512]{1,0:T(8,128)(2,1)S(1)}, u32[]{:S(2)}, u32[]{:S(2)}) collective-permute-start(bf16[256,512]{1,0:T(8,128)(2,1)} %c0.1), channel_id=1, source_target_pairs={{0,3},{1,0},{2,1},{3,2},{4,7},{5,4},{6,5},{7,6},{8,11},{9,8},{10,9... | collective-permute-start | bytes 786440 | tf_op jit(solution)/shard_map/ppermute | solution.py:32
  16.8 12.4 %collective-permute-start.2 = (bf16[256,512]{1,0:T(8,128)(2,1)}, bf16[256,512]{1,0:T(8,128)(2,1)S(1)}, u32[]{:S(2)}, u32[]{:S(2)}) collective-permute-start(bf16[256,512]{1,0:T(8,128)(2,1)} %c0.1), channel_id=1, source_target_pairs={{0,1},{1,2},{2,3},{3,0},{4,5},{5,6},{6,7},{7,4},{8,9},{9,10},{10,1... | collective-permute-start | bytes 786440 | tf_op jit(solution)/shard_map/ppermute | solution.py:32
  33.5 60.3 %all-to-all-start = ((bf16[32,32,2048]{2,1,0:T(8,128)(2,1)}), bf16[32,32,2048]{2,1,0:T(8,128)(2,1)}, u32[]{:S(2)}, u32[]{:S(2)}) async-start(bf16[32,32,2048]{2,1,0:T(8,128)(2,1)} %route_rest.1), calls=%async_computation | async-start | bytes 8388608 | tf_op jit(solution)/shard_map/all_to_all | solution.py:232
  41.7 13.4 %collective-permute-start.6 = (bf16[16,4,8,512]{3,2,1,0:T(8,128)(2,1)S(1)}, bf16[16,4,8,512]{3,2,1,0:T(8,128)(2,1)S(1)}, u32[]{:S(2)}, u32[]{:S(2)}) collective-permute-start(bf16[16,4,8,512]{3,2,1,0:T(8,128)(2,1)S(1)} %get-tuple-element.73), channel_id=1, source_target_pairs={{0,3},{1,0},{2,1},{3,2},{4,7},{5,4},{6,5},{7,6},{8,11},{9,8},{10,9... | collective-permute-start | bytes 1572872 | tf_op jit(solution)/shard_map/ppermute | solution.py:32
  44.1 14.5 %collective-permute-start.3 = (bf16[16,4,8,512]{3,2,1,0:T(8,128)(2,1)S(1)}, bf16[16,4,8,512]{3,2,1,0:T(8,128)(2,1)S(1)}, u32[]{:S(2)}, u32[]{:S(2)}) collective-permute-start(bf16[16,4,8,512]{3,2,1,0:T(8,128)(2,1)S(1)} %get-tuple-element.74), channel_id=1, source_target_pairs={{0,1},{1,2},{2,3},{3,0},{4,5},{5,6},{6,7},{7,4},{8,9},{9,10},{10,1... | collective-permute-start | bytes 1572872 | tf_op jit(solution)/shard_map/ppermute | solution.py:32
  44.1 25.4 %collective-permute-start.4 = (bf16[16,4,8,512]{3,2,1,0:T(8,128)(2,1)S(1)}, bf16[16,4,8,512]{3,2,1,0:T(8,128)(2,1)S(1)}, u32[]{:S(2)}, u32[]{:S(2)}) collective-permute-start(bf16[16,4,8,512]{3,2,1,0:T(8,128)(2,1)S(1)} %get-tuple-element.73), channel_id=1, source_target_pairs={{0,1},{1,2},{2,3},{3,0},{4,5},{5,6},{6,7},{7,4},{8,9},{9,10},{10,1... | collective-permute-start | bytes 1572872 | tf_op jit(solution)/shard_map/ppermute | solution.py:32
  44.1 25.4 %collective-permute-start.5 = (bf16[16,4,8,512]{3,2,1,0:T(8,128)(2,1)S(1)}, bf16[16,4,8,512]{3,2,1,0:T(8,128)(2,1)S(1)}, u32[]{:S(2)}, u32[]{:S(2)}) collective-permute-start(bf16[16,4,8,512]{3,2,1,0:T(8,128)(2,1)S(1)} %get-tuple-element.74), channel_id=1, source_target_pairs={{0,3},{1,0},{2,1},{3,2},{4,7},{5,4},{6,5},{7,6},{8,11},{9,8},{10,9... | collective-permute-start | bytes 1572872 | tf_op jit(solution)/shard_map/ppermute | solution.py:32
  55.1 25.7 %copy-start.1 = (bf16[16,4,8,512]{3,2,1,0:T(8,128)(2,1)}, bf16[16,4,8,512]{3,2,1,0:T(8,128)(2,1)S(1)}, u32[]{:S(2)}) copy-start(bf16[16,4,8,512]{3,2,1,0:T(8,128)(2,1)S(1)} %collective-permute-done.6.right_b) | copy-start | bytes 1572868
  55.1 22.5 %collective-permute-start.8 = (bf16[16,4,8,512]{3,2,1,0:T(8,128)(2,1)S(1)}, bf16[16,4,8,512]{3,2,1,0:T(8,128)(2,1)S(1)}, u32[]{:S(2)}, u32[]{:S(2)}) collective-permute-start(bf16[16,4,8,512]{3,2,1,0:T(8,128)(2,1)S(1)} %collective-permute-done.6.right_b), channel_id=1, source_target_pairs={{0,3},{1,0},{2,1},{3,2},{4,7},{5,4},{6,5},{7,6},{8,11},{9,8},{10,9... | collective-permute-start | bytes 1572872 | tf_op jit(solution)/shard_map/ppermute | solution.py:32
  58.6 22.2 %copy-start.2 = (bf16[16,4,8,512]{3,2,1,0:T(8,128)(2,1)}, bf16[16,4,8,512]{3,2,1,0:T(8,128)(2,1)S(1)}, u32[]{:S(2)}) copy-start(bf16[16,4,8,512]{3,2,1,0:T(8,128)(2,1)S(1)} %collective-permute-done.3.left_a) | copy-start | bytes 1572868
  58.6 22.1 %collective-permute-start.7 = (bf16[16,4,8,512]{3,2,1,0:T(8,128)(2,1)S(1)}, bf16[16,4,8,512]{3,2,1,0:T(8,128)(2,1)S(1)}, u32[]{:S(2)}, u32[]{:S(2)}) collective-permute-start(bf16[16,4,8,512]{3,2,1,0:T(8,128)(2,1)S(1)} %collective-permute-done.3.left_a), channel_id=1, source_target_pairs={{0,1},{1,2},{2,3},{3,0},{4,5},{5,6},{6,7},{7,4},{8,9},{9,10},{10,1... | collective-permute-start | bytes 1572872 | tf_op jit(solution)/shard_map/ppermute | solution.py:32
  105.2 13.2 %collective-permute-start.9 = (bf16[16,4,8,384]{3,2,1,0:T(8,128)(2,1)}, bf16[16,4,8,384]{3,2,1,0:T(8,128)(2,1)S(1)}, u32[]{:S(2)}, u32[]{:S(2)}) collective-permute-start(bf16[16,4,8,384]{3,2,1,0:T(8,128)(2,1)} %get-tuple-element.46), channel_id=1, source_target_pairs={{0,1},{1,2},{2,3},{3,0},{4,5},{5,6},{6,7},{7,4},{8,9},{9,10},{10,1... | collective-permute-start | bytes 1179656 | tf_op jit(solution)/shard_map/ppermute | solution.py:32
  105.9 14.3 %collective-permute-start.13 = (bf16[16,4,8,384]{3,2,1,0:T(8,128)(2,1)}, bf16[16,4,8,384]{3,2,1,0:T(8,128)(2,1)S(1)}, u32[]{:S(2)}, u32[]{:S(2)}) collective-permute-start(bf16[16,4,8,384]{3,2,1,0:T(8,128)(2,1)} %get-tuple-element.51), channel_id=1, source_target_pairs={{0,3},{1,0},{2,1},{3,2},{4,7},{5,4},{6,5},{7,6},{8,11},{9,8},{10,9... | collective-permute-start | bytes 1179656 | tf_op jit(solution)/shard_map/ppermute | solution.py:32
  107.9 30.7 %all-to-all-start.3 = ((bf16[32,32,640]{2,1,0:T(8,128)(2,1)}), bf16[32,32,640]{2,1,0:T(8,128)(2,1)}, u32[]{:S(2)}, u32[]{:S(2)}) async-start(bf16[32,32,640]{2,1,0:T(8,128)(2,1)} %bitcast.16), calls=%async_computation.3 | async-start | bytes 2621440 | tf_op jit(solution)/shard_map/all_to_all | solution.py:281
  115.6 16.6 %collective-permute-start.11 = (bf16[16,4,8,384]{3,2,1,0:T(8,128)(2,1)}, bf16[16,4,8,384]{3,2,1,0:T(8,128)(2,1)}, u32[]{:S(2)}, u32[]{:S(2)}) collective-permute-start(bf16[16,4,8,384]{3,2,1,0:T(8,128)(2,1)} %get-tuple-element.47), channel_id=1, source_target_pairs={{0,1},{1,2},{2,3},{3,0},{4,5},{5,6},{6,7},{7,4},{8,9},{9,10},{10,1... | collective-permute-start | bytes 1179656 | tf_op jit(solution)/shard_map/ppermute | solution.py:32
  115.7 16.5 %collective-permute-start.12 = (bf16[16,4,8,384]{3,2,1,0:T(8,128)(2,1)}, bf16[16,4,8,384]{3,2,1,0:T(8,128)(2,1)}, u32[]{:S(2)}, u32[]{:S(2)}) collective-permute-start(bf16[16,4,8,384]{3,2,1,0:T(8,128)(2,1)} %get-tuple-element.48), channel_id=1, source_target_pairs={{0,3},{1,0},{2,1},{3,2},{4,7},{5,4},{6,5},{7,6},{8,11},{9,8},{10,9... | collective-permute-start | bytes 1179656 | tf_op jit(solution)/shard_map/ppermute | solution.py:32
  120.2 16.0 %collective-permute-start.10 = (bf16[16,4,8,384]{3,2,1,0:T(8,128)(2,1)}, bf16[16,4,8,384]{3,2,1,0:T(8,128)(2,1)}, u32[]{:S(2)}, u32[]{:S(2)}) collective-permute-start(bf16[16,4,8,384]{3,2,1,0:T(8,128)(2,1)} %add_convert_fusion.3), channel_id=1, source_target_pairs={{0,1},{1,2},{2,3},{3,0},{4,5},{5,6},{6,7},{7,4},{8,9},{9,10},{10,1... | collective-permute-start | bytes 1179656 | tf_op jit(solution)/shard_map/ppermute | solution.py:32
  122.1 12.9 %collective-permute-start.14 = (bf16[16,4,8,384]{3,2,1,0:T(8,128)(2,1)}, bf16[16,4,8,384]{3,2,1,0:T(8,128)(2,1)}, u32[]{:S(2)}, u32[]{:S(2)}) collective-permute-start(bf16[16,4,8,384]{3,2,1,0:T(8,128)(2,1)} %add_convert_fusion.2), channel_id=1, source_target_pairs={{0,3},{1,0},{2,1},{3,2},{4,7},{5,4},{6,5},{7,6},{8,11},{9,8},{10,9... | collective-permute-start | bytes 1179656 | tf_op jit(solution)/shard_map/ppermute | solution.py:32
  138.6 22.7 %all-to-all-start.2 = ((bf16[32,32,384]{2,1,0:T(8,128)(2,1)}), bf16[32,32,384]{2,1,0:T(8,128)(2,1)S(1)}, u32[]{:S(2)}, u32[]{:S(2)}) async-start(bf16[32,32,384]{2,1,0:T(8,128)(2,1)} %bitcast.7), calls=%async_computation.2 | async-start | bytes 1572864 | tf_op jit(solution)/shard_map/all_to_all | solution.py:317
  149.9 10.3 %collective-permute-start.15 = (bf16[288,128]{1,0:T(8,128)(2,1)}, bf16[288,128]{1,0:T(8,128)(2,1)S(1)}, u32[]{:S(2)}, u32[]{:S(2)}) collective-permute-start(bf16[288,128]{1,0:T(8,128)(2,1)} %get-tuple-element.65), channel_id=1, source_target_pairs={{0,1},{1,2},{2,3},{3,0},{4,5},{5,6},{6,7},{7,4},{8,9},{9,10},{10,1... | collective-permute-start | bytes 221192 | tf_op jit(solution)/shard_map/ppermute | solution.py:32
  150.1 10.1 %collective-permute-start.16 = (bf16[288,128]{1,0:T(8,128)(2,1)}, bf16[288,128]{1,0:T(8,128)(2,1)S(1)}, u32[]{:S(2)}, u32[]{:S(2)}) collective-permute-start(bf16[288,128]{1,0:T(8,128)(2,1)} %get-tuple-element.66), channel_id=1, source_target_pairs={{0,2},{1,3},{2,0},{3,1},{4,6},{5,7},{6,4},{7,5},{8,10},{9,11},{10,... | collective-permute-start | bytes 221192 | tf_op jit(solution)/shard_map/ppermute | solution.py:32
  154.5 5.7 %collective-permute-start.17 = (bf16[288,128]{1,0:T(8,128)(2,1)}, bf16[288,128]{1,0:T(8,128)(2,1)}, u32[]{:S(2)}, u32[]{:S(2)}) collective-permute-start(bf16[288,128]{1,0:T(8,128)(2,1)} %get-tuple-element.67), channel_id=1, source_target_pairs={{0,3},{1,0},{2,1},{3,2},{4,7},{5,4},{6,5},{7,6},{8,11},{9,8},{10,9... | collective-permute-start | bytes 221192 | tf_op jit(solution)/shard_map/ppermute | solution.py:32
  (5 other events, 32.2 us)

commit v6 on v5

--- a/solution.py
+++ b/solution.py
@@ -94,9 +94,11 @@
 
 
 def gates(
-    z_ref, own, left_a, left_b, right_a, right_b, far_a, far_b, wg, wu,
-    x_out, h_out, silu_out, slope_out, xs,
+    z_ref, dest, own, left_a, left_b, right_a, right_b, far_a, far_b, wg, wu,
+    x_out, h_out, silu_out, slope_out, pick_out, xs,
 ):
+    at0, at1 = slots_of(dest, pl.program_id(0) * 256, 256)
+    pick_out[...] = jnp.where(at0 | at1, 1.0, 0.0).T.astype(BF)
     pieces = ((0, (own,)), (3, (left_a, left_b)), (1, (right_a, right_b)), (2, (far_a, far_b)))
     for off, parts in pieces:
         q = lax.rem(z_ref[0] + off, NZ)
@@ -143,9 +145,12 @@
         part_out[:, 0, :, off * RB : (off + 1) * RB] = parted(dx[:, RA:])
 
 
-def grads_down(dest, rest, h, down_out, pick_out):
-    at0, at1 = slots_of(dest, pl.program_id(0) * 256, 256)
-    pick_out[...] = jnp.where(at0 | at1, 1.0, 0.0).T.astype(BF)
+def last_sums(a0, a1, a2, b0, b1, b2, out):
+    out[0] = (a0[...].astype(F32) + a1[...].astype(F32) + a2[...].astype(F32)).astype(BF)
+    out[1] = (b0[...].astype(F32) + b1[...].astype(F32) + b2[...].astype(F32)).astype(BF)
+
+
+def grads_down(rest, h, down_out):
     down_out[0] = dot(h[0], merged(rest[:, 0]), 0, 0).astype(BF)
 
 
@@ -248,17 +253,19 @@
     rows = OWN * CAP
     hid, hid_f = shape((LOC, rows, QH)), shape((LOC, rows, QH), F32)
     hid_spec = leading(rows, QH)
-    x_slots, h, silu, slope = pl.pallas_call(
+    x_slots, h, silu, slope, pick = pl.pallas_call(
         gates,
         grid=(LOC,),
-        in_specs=[smem, by_expert(OWN, QF)] + [by_expert(half, QF)] * 6 + [leading(D, QH)] * 2,
-        out_specs=[leading(rows, D), hid_spec, hid_spec, hid_spec],
-        out_shape=[shape((LOC, rows, D)), hid, hid_f, hid_f],
+        in_specs=[smem, whole((2, TOK)), by_expert(OWN, QF)]
+        + [by_expert(half, QF)] * 6 + [leading(D, QH)] * 2,
+        out_specs=[leading(rows, D), hid_spec, hid_spec, hid_spec]
+        + [pl.BlockSpec((TOK, 256), lambda e: (0, e))],
+        out_shape=[shape((LOC, rows, D)), hid, hid_f, hid_f, shape((TOK, OWN * LOC * CAP))],
         scratch_shapes=[pltpu.VMEM((NZ, rows, QF), BF)],
         compiler_params=params(56),
         cost_estimate=cost(2.2e9, 19e6),
         name="gates",
-    )(z, got, left_t, left_b, right_t, right_b, far_t, far_b, gate_proj, up_proj)
+    )(z, dest, got, left_t, left_b, right_t, right_b, far_t, far_b, gate_proj, up_proj)
 
     half_part = shape((half, LOC, CAP, RA))
     o0t, o0b, o1t, o1b, o2t, o2b, o3t, o3b, part, dg, du = pl.pallas_call(
@@ -295,25 +302,32 @@
         in_specs=[leading(rows, D)] + [hid_spec] * 2,
         out_specs=[leading(D, QH), leading(D, QH)],
         out_shape=[shape((LOC, D, QH)), shape((LOC, D, QH))],
-        compiler_params=params(),
+        compiler_params=params(56),
         cost_estimate=cost(1.2e10, 20e6),
         name="grads_up",
     )(x_slots, dg, du)
     from_l_b, from_r_t, up_grad = lax.optimization_barrier((from_l_b, from_r_t, up_grad))
-    sum_t = o0t.astype(F32) + from_l_t.astype(F32) + from_r_t.astype(F32)
-    sum_b = o0b.astype(F32) + from_l_b.astype(F32) + from_r_b.astype(F32)
-    sums = jnp.concatenate([sum_t.astype(BF), sum_b.astype(BF)], axis=0)
+    terms = (o0t, from_l_t, from_r_t, o0b, from_l_b, from_r_b)
+    sums = pl.pallas_call(
+        last_sums,
+        in_specs=[pl.BlockSpec(memory_space=pltpu.VMEM)] * 6,
+        out_specs=pl.BlockSpec(memory_space=pltpu.VMEM),
+        out_shape=jax.ShapeDtypeStruct((2, half, LOC, CAP, RA), BF),
+        compiler_params=params(56),
+        cost_estimate=cost(2e6, 3.2e6),
+        name="last_sums",
+    )(*(pltpu.with_memory_space_constraint(v, pltpu.VMEM) for v in terms))
     sums, h = lax.optimization_barrier((sums, h))
-    down_grad, pick = pl.pallas_call(
+    down_grad = pl.pallas_call(
         grads_down,
         grid=(LOC,),
-        in_specs=[whole((2, TOK)), by_expert(OWN, D), hid_spec],
-        out_specs=[leading(QH, D), pl.BlockSpec((TOK, 256), lambda e: (0, e))],
-        out_shape=[shape((LOC, QH, D)), shape((TOK, OWN * LOC * CAP))],
+        in_specs=[by_expert(OWN, D), hid_spec],
+        out_specs=leading(QH, D),
+        out_shape=shape((LOC, QH, D)),
         compiler_params=params(),
         cost_estimate=cost(1.1e9, 10e6),
         name="grads_down",
-    )(dest, rest, h)
+    )(rest, h)
     back = lax.all_to_all(
         sums.reshape(OWN, 32, RA), "expert", split_axis=0, concat_axis=0, tiled=True
     ).reshape(OWN * 32, RA)
@@ -324,10 +338,10 @@
         in_specs=[pl.BlockSpec(memory_space=pltpu.VMEM)] * 2,
         out_shape=[y_shape] * 4,
         scratch_shapes=[pltpu.VMEM((TOK, NZ * RB), F32)],
-        compiler_params=params(),
+        compiler_params=params(56),
         cost_estimate=cost(4e8, 3e6),
         name="pick_pairs",
-    )(dest, part_back)
+    )(dest, pltpu.with_memory_space_constraint(part_back, pltpu.VMEM))
     ys = (y0, shift(y1, 1), shift(y2, 2), shift(y3, -1))
 
     back = pltpu.with_memory_space_constraint(back, pltpu.VMEM)

time: 164 us -> 163 us (level)
  other arithmetic: 7.29 us -> 2.19 us
  waiting for transfers between devices: 50.6 us -> 54.3 us
    convert_element_type x2 -> x0, other arithmetic: 2.53 us -> none  [on_device(): sums = jnp.concatenate([sum_t.astype(BF), sum_b.astype(BF)], axis=0)]
    ppermute x18, waiting for transfers between devices: 44.5 us -> 46.9 us  [shift(): return lax.ppermute(x, 'hidden', [(i, (i + d) % NZ) for i in range(NZ)])]
    pallas_call x2 -> x3, Pallas kernels: 13.8 us -> 15 us  [the longest x1 8.25 us: on_device(): pl.pallas_call(gates, grid=(LOC,), in_specs=[smem, whole((2, TOK)), by_ex...]
  transfers between devices with their start and end apart: 22 -> 22, of which waited for: 9 -> 9; matrix products, arithmetic and copies ran while one was open for 5% -> 1% of each run, Pallas kernels for 17% -> 18%
where the time goes in v6:
time: 163 us; the launch traced here: 162 us
  starting transfers between devices  58.4 us (36%)
  waiting for transfers between devices  54.3 us (33%)
  Pallas kernels  46.1 us (28%)
  other arithmetic  2.19 us (1%)
    ppermute x18, waiting for transfers between devices, shift(): return lax.ppermute(x, 'hidden', [(i, (i + d) % NZ) for i in range(NZ)])  46.9 us
    ppermute x18, starting transfers between devices, shift(): return lax.ppermute(x, 'hidden', [(i, (i + d) % NZ) for i in range(NZ)])  25.9 us
    pallas_call x1, Pallas kernels, on_device(): pl.pallas_call(middle, grid=(LOC,), in_specs=[smem, by_expert(OWN, D)] +...  11.4 us
    all_to_all x1, starting transfers between devices, on_device(): got = lax.all_to_all(pay, 'expert', split_axis=0, concat_axis=0, tiled=True)  8.59 us
    pallas_call x1, Pallas kernels, on_device(): pl.pallas_call(gates, grid=(LOC,), in_specs=[smem, whole((2, TOK)), by_ex...  8.25 us
    all_to_all x1, starting transfers between devices, on_device(): lax.all_to_all(pay_rest, 'expert', split_axis=0, concat_axis=0, tiled=True)  8.12 us
    all_to_all x1, starting transfers between devices, on_device(): lax.all_to_all(sums.reshape(OWN, 32, RA), 'expert', split_axis=0, concat_...  8.07 us
    all_to_all x1, starting transfers between devices, on_device(): lax.all_to_all(part.reshape(OWN, 32, WR), 'expert', split_axis=0, concat_...  7.67 us
  transfers between devices with their start and end apart: 22, of which 9 were waited for; matrix products, arithmetic and copies ran while one was open for 1% of the time, Pallas kernels for 18%

profile of v6, /device:TPU:1, one launch (start us, length us, event | category | flops | bytes accessed | tf_op | source)
XLA Modules:
  0.0 161.8 jit_solution(15588185616869290470)
XLA Ops:
  0.6 3.4 %route_first.1 = (bf16[32,32,512]{2,1,0:T(8,128)(2,1)}, s32[2,256]{1,0:T(2,128)}) custom-call(s32[2,256]{1,0:T(2,128)} %bitcast.21, bf16[256,512]{1,0:T(8,128)(2,1)} %tokens.1), custom_call_target="tpu_custom_call" | custom-call | flops 500000000 | bytes 4000000 | tf_op jit(solution)/shard_map/route_first/pallas_call | solution.py:212
  4.1 8.6 %all-to-all-start = ((bf16[32,32,512]{2,1,0:T(8,128)(2,1)}), bf16[32,32,512]{2,1,0:T(8,128)(2,1)S(1)}, u32[]{:S(2)}, u32[]{:S(2)}) async-start(bf16[32,32,512]{2,1,0:T(8,128)(2,1)} %get-tuple-element.39), calls=%async_computation | async-start | bytes 2097152 | tf_op jit(solution)/shard_map/all_to_all | solution.py:223
  12.7 3.7 %collective-permute-start.7 = (bf16[256,512]{1,0:T(8,128)(2,1)}, bf16[256,512]{1,0:T(8,128)(2,1)S(1)}, u32[]{:S(2)}, u32[]{:S(2)}) collective-permute-start(bf16[256,512]{1,0:T(8,128)(2,1)} %c0.1), channel_id=1, source_target_pairs={{0,2},{1,3},{2,0},{3,1},{4,6},{5,7},{6,4},{7,5},{8,10},{9,11},{10,... | collective-permute-start | bytes 786440 | tf_op jit(solution)/shard_map/ppermute | solution.py:32
  17.8 5.3 %collective-permute-done.7.c2 = bf16[256,512]{1,0:T(8,128)(2,1)S(1)} collective-permute-done((bf16[256,512]{1,0:T(8,128)(2,1)}, bf16[256,512]{1,0:T(8,128)(2,1)S(1)}, u32[]{:S(2)}, u32[]{:S(2)}) %collective-permute-start.7) | collective-permute-done | bytes 262176 | tf_op jit(solution)/shard_map/ppermute | solution.py:32
  23.1 6.0 %collective-permute-done.6.c1 = bf16[256,512]{1,0:T(8,128)(2,1)S(1)} collective-permute-done((bf16[256,512]{1,0:T(8,128)(2,1)}, bf16[256,512]{1,0:T(8,128)(2,1)S(1)}, u32[]{:S(2)}, u32[]{:S(2)}) %collective-permute-start.6) | collective-permute-done | bytes 262176 | tf_op jit(solution)/shard_map/ppermute | solution.py:32
  29.2 4.3 %route_rest.1 = bf16[32,32,2048]{2,1,0:T(8,128)(2,1)} custom-call(s32[1]{0:T(128)} %bitcast.z_ref, s32[2,256]{1,0:T(2,128)} %get-tuple-element.38.dest, f32[2,256]{1,0:T(2,128)} %bitcast.19, bf16[256,512]{1,0:T(8,128)(2,1)} %c0.1, bf16[256,512]{1,0:T(8,128)(2,1)S(1)} %collective-permute-done.6.c1, bf16[256,512]{1,0:T(8,128)(2,1)S(1)} %collective-permute-done.7.c2, ...), custom_call_target="tpu_custom_call" | custom-call | flops 800000000 | bytes 6000000 | tf_op jit(solution)/shard_map/route_rest/pallas_call | solution.py:227
  33.5 8.1 %all-to-all-start.1 = ((bf16[32,32,2048]{2,1,0:T(8,128)(2,1)}), bf16[32,32,2048]{2,1,0:T(8,128)(2,1)}, u32[]{:S(2)}, u32[]{:S(2)}) async-start(bf16[32,32,2048]{2,1,0:T(8,128)(2,1)} %route_rest.1), calls=%async_computation.1 | async-start | bytes 8388608 | tf_op jit(solution)/shard_map/all_to_all | solution.py:237
  44.1 2.7 %collective-permute-start.2 = (bf16[16,4,8,512]{3,2,1,0:T(8,128)(2,1)S(1)}, bf16[16,4,8,512]{3,2,1,0:T(8,128)(2,1)S(1)}, u32[]{:S(2)}, u32[]{:S(2)}) collective-permute-start(bf16[16,4,8,512]{3,2,1,0:T(8,128)(2,1)S(1)} %get-tuple-element.72), channel_id=1, source_target_pairs={{0,3},{1,0},{2,1},{3,2},{4,7},{5,4},{6,5},{7,6},{8,11},{9,8},{10,9... | collective-permute-start | bytes 1572872 | tf_op jit(solution)/shard_map/ppermute | solution.py:32
  46.8 8.3 %collective-permute-done.3.right_b = bf16[16,4,8,512]{3,2,1,0:T(8,128)(2,1)S(1)} collective-permute-done((bf16[16,4,8,512]{3,2,1,0:T(8,128)(2,1)S(1)}, bf16[16,4,8,512]{3,2,1,0:T(8,128)(2,1)S(1)}, u32[]{:S(2)}, u32[]{:S(2)}) %collective-permute-start.3) | collective-permute-done | bytes 524320 | tf_op jit(solution)/shard_map/ppermute | solution.py:32
  55.1 3.5 %collective-permute-start.5 = (bf16[16,4,8,512]{3,2,1,0:T(8,128)(2,1)S(1)}, bf16[16,4,8,512]{3,2,1,0:T(8,128)(2,1)S(1)}, u32[]{:S(2)}, u32[]{:S(2)}) collective-permute-start(bf16[16,4,8,512]{3,2,1,0:T(8,128)(2,1)S(1)} %collective-permute-done.3.right_b), channel_id=1, source_target_pairs={{0,3},{1,0},{2,1},{3,2},{4,7},{5,4},{6,5},{7,6},{8,11},{9,8},{10,9... | collective-permute-start | bytes 1572872 | tf_op jit(solution)/shard_map/ppermute | solution.py:32
  58.6 10.9 %collective-permute-done.1.left_b = bf16[16,4,8,512]{3,2,1,0:T(8,128)(2,1)S(1)} collective-permute-done((bf16[16,4,8,512]{3,2,1,0:T(8,128)(2,1)S(1)}, bf16[16,4,8,512]{3,2,1,0:T(8,128)(2,1)S(1)}, u32[]{:S(2)}, u32[]{:S(2)}) %collective-permute-start.1) | collective-permute-done | bytes 524320 | tf_op jit(solution)/shard_map/ppermute | solution.py:32
  69.5 8.0 %collective-permute-done.5.far_b = bf16[16,4,8,512]{3,2,1,0:T(8,128)(2,1)S(1)} collective-permute-done((bf16[16,4,8,512]{3,2,1,0:T(8,128)(2,1)S(1)}, bf16[16,4,8,512]{3,2,1,0:T(8,128)(2,1)S(1)}, u32[]{:S(2)}, u32[]{:S(2)}) %collective-permute-start.5) | collective-permute-done | bytes 524320 | tf_op jit(solution)/shard_map/ppermute | solution.py:32
  77.6 3.2 %collective-permute-done.4.far_a = bf16[16,4,8,512]{3,2,1,0:T(8,128)(2,1)S(1)} collective-permute-done((bf16[16,4,8,512]{3,2,1,0:T(8,128)(2,1)S(1)}, bf16[16,4,8,512]{3,2,1,0:T(8,128)(2,1)S(1)}, u32[]{:S(2)}, u32[]{:S(2)}) %collective-permute-start.4) | collective-permute-done | bytes 524320 | tf_op jit(solution)/shard_map/ppermute | solution.py:32
  80.8 8.2 %gates.1 = (bf16[4,256,2048]{2,1,0:T(8,128)(2,1)}, bf16[4,256,256]{2,1,0:T(8,128)(2,1)}, f32[4,256,256]{2,1,0:T(8,128)}, f32[4,256,256]{2,1,0:T(8,128)}, bf16[256,1024]{1,0:T(8,128)(2,1)}) custom-call(s32[1]{0:T(128)} %bitcast.z_ref, s32[2,256]{1,0:T(2,128)} %get-tuple-element.38.dest, bf16[32,4,8,512]{3,2,1,0:T(8,128)(2,1)} %bitcast.16, ...), custom_call_target="tpu_custom_call" | custom-call | flops 2200000000 | bytes 19000000 | tf_op jit(solution)/shard_map/gates/pallas_call | solution.py:256
  89.0 4.8 %all-to-all-done.1 = bf16[32,32,2048]{2,1,0:T(8,128)(2,1)} async-done(((bf16[32,32,2048]{2,1,0:T(8,128)(2,1)}), bf16[32,32,2048]{2,1,0:T(8,128)(2,1)}, u32[]{:S(2)}, u32[]{:S(2)}) %all-to-all-start.1) | async-done | bytes 4194336 | tf_op jit(solution)/shard_map/all_to_all | solution.py:237
  93.8 11.4 %middle.1 = (bf16[16,4,8,384]{3,2,1,0:T(8,128)(2,1)}, bf16[16,4,8,384]{3,2,1,0:T(8,128)(2,1)}, bf16[16,4,8,384]{3,2,1,0:T(8,128)(2,1)}, bf16[16,4,8,384]{3,2,1,0...) custom-call(s32[1]{0:T(128)} %bitcast.z_ref, ...), custom_call_target="tpu_custom_call" | custom-call | flops 2700000000 | bytes 27000000 | tf_op jit(solution)/shard_map/middle/pallas_call | solution.py:271
  107.9 7.7 %all-to-all-start.3 = ((bf16[32,32,640]{2,1,0:T(8,128)(2,1)}), bf16[32,32,640]{2,1,0:T(8,128)(2,1)S(1)}, u32[]{:S(2)}, u32[]{:S(2)}) async-start(bf16[32,32,640]{2,1,0:T(8,128)(2,1)} %bitcast.18), calls=%async_computation.3 | async-start | bytes 2621440 | tf_op jit(solution)/shard_map/all_to_all | solution.py:288
  115.7 2.7 %collective-permute-start.12 = (bf16[16,4,8,384]{3,2,1,0:T(8,128)(2,1)}, bf16[16,4,8,384]{3,2,1,0:T(8,128)(2,1)S(1)}, u32[]{:S(2)}, u32[]{:S(2)}) collective-permute-start(bf16[16,4,8,384]{3,2,1,0:T(8,128)(2,1)} %get-tuple-element.48), channel_id=1, source_target_pairs={{0,3},{1,0},{2,1},{3,2},{4,7},{5,4},{6,5},{7,6},{8,11},{9,8},{10,9... | collective-permute-start | bytes 1179656 | tf_op jit(solution)/shard_map/ppermute | solution.py:32
  120.6 2.7 %collective-permute-start.14 = (bf16[16,4,8,384]{3,2,1,0:T(8,128)(2,1)S(1)}, bf16[16,4,8,384]{3,2,1,0:T(8,128)(2,1)S(1)}, u32[]{:S(2)}, u32[]{:S(2)}) collective-permute-start(bf16[16,4,8,384]{3,2,1,0:T(8,128)(2,1)S(1)} %add_convert_fusion), channel_id=1, source_target_pairs={{0,3},{1,0},{2,1},{3,2},{4,7},{5,4},{6,5},{7,6},{8,11},{9,8},{10,9... | collective-permute-start | bytes 1179656 | tf_op jit(solution)/shard_map/ppermute | solution.py:32
  123.4 7.5 %grads_up.1 = (bf16[4,2048,256]{2,1,0:T(8,128)(2,1)}, bf16[4,2048,256]{2,1,0:T(8,128)(2,1)}) custom-call(bf16[4,256,2048]{2,1,0:T(8,128)(2,1)} %get-tuple-element.49.x, bf16[4,256,256]{2,1,0:T(8,128)(2,1)} %get-tuple-element.54.dg, bf16[4,256,256]{2,1,0:T(8,128)(2,1)} %get-tuple-element.55.du), custom_call_target="tpu_custom_call" | custom-call | flops 12000000000 | bytes 20000000 | tf_op jit(solution)/shard_map/grads_up/pallas_call | solution.py:299
  130.9 5.1 %collective-permute-done.10.a1 = bf16[16,4,8,384]{3,2,1,0:T(8,128)(2,1)S(1)} collective-permute-done((bf16[16,4,8,384]{3,2,1,0:T(8,128)(2,1)S(1)}, bf16[16,4,8,384]{3,2,1,0:T(8,128)(2,1)S(1)}, u32[]{:S(2)}, u32[]{:S(2)}) %collective-permute-start.10) | collective-permute-done | bytes 393248 | tf_op jit(solution)/shard_map/ppermute | solution.py:32
  137.2 8.1 %all-to-all-start.2 = ((bf16[32,32,384]{2,1,0:T(8,128)(2,1)}), bf16[32,32,384]{2,1,0:T(8,128)(2,1)S(1)}, u32[]{:S(2)}, u32[]{:S(2)}) async-start(bf16[32,32,384]{2,1,0:T(8,128)(2,1)} %bitcast.17), calls=%async_computation.2 | async-start | bytes 1572864 | tf_op jit(solution)/shard_map/all_to_all | solution.py:331
  147.5 3.8 %collective-permute-start.16 = (bf16[288,128]{1,0:T(8,128)(2,1)}, bf16[288,128]{1,0:T(8,128)(2,1)S(1)}, u32[]{:S(2)}, u32[]{:S(2)}) collective-permute-start(bf16[288,128]{1,0:T(8,128)(2,1)} %get-tuple-element.64), channel_id=1, source_target_pairs={{0,2},{1,3},{2,0},{3,1},{4,6},{5,7},{6,4},{7,5},{8,10},{9,11},{10,... | collective-permute-start | bytes 221192 | tf_op jit(solution)/shard_map/ppermute | solution.py:32
  151.3 5.6 %grads_down.1 = bf16[4,256,2048]{2,1,0:T(8,128)(2,1)} custom-call(bf16[32,4,8,2048]{3,2,1,0:T(8,128)(2,1)} %bitcast.6.rest, bf16[4,256,256]{2,1,0:T(8,128)(2,1)} %get-tuple-element.70.h_in.h), custom_call_target="tpu_custom_call" | custom-call | flops 1100000000 | bytes 10000000 | tf_op jit(solution)/shard_map/grads_down/pallas_call | solution.py:321
  (46 shorter events, 17.3 us)
Async XLA Ops:
  4.1 29.4 %all-to-all-start = ((bf16[32,32,512]{2,1,0:T(8,128)(2,1)}), bf16[32,32,512]{2,1,0:T(8,128)(2,1)S(1)}, u32[]{:S(2)}, u32[]{:S(2)}) async-start(bf16[32,32,512]{2,1,0:T(8,128)(2,1)} %get-tuple-element.39), calls=%async_computation | async-start | bytes 2097152 | tf_op jit(solution)/shard_map/all_to_all | solution.py:223
  12.7 10.5 %collective-permute-start.7 = (bf16[256,512]{1,0:T(8,128)(2,1)}, bf16[256,512]{1,0:T(8,128)(2,1)S(1)}, u32[]{:S(2)}, u32[]{:S(2)}) collective-permute-start(bf16[256,512]{1,0:T(8,128)(2,1)} %c0.1), channel_id=1, source_target_pairs={{0,2},{1,3},{2,0},{3,1},{4,6},{5,7},{6,4},{7,5},{8,10},{9,11},{10,... | collective-permute-start | bytes 786440 | tf_op jit(solution)/shard_map/ppermute | solution.py:32
  16.3 12.8 %collective-permute-start.6 = (bf16[256,512]{1,0:T(8,128)(2,1)}, bf16[256,512]{1,0:T(8,128)(2,1)S(1)}, u32[]{:S(2)}, u32[]{:S(2)}) collective-permute-start(bf16[256,512]{1,0:T(8,128)(2,1)} %c0.1), channel_id=1, source_target_pairs={{0,3},{1,0},{2,1},{3,2},{4,7},{5,4},{6,5},{7,6},{8,11},{9,8},{10,9... | collective-permute-start | bytes 786440 | tf_op jit(solution)/shard_map/ppermute | solution.py:32
  16.8 12.4 %collective-permute-start.8 = (bf16[256,512]{1,0:T(8,128)(2,1)}, bf16[256,512]{1,0:T(8,128)(2,1)S(1)}, u32[]{:S(2)}, u32[]{:S(2)}) collective-permute-start(bf16[256,512]{1,0:T(8,128)(2,1)} %c0.1), channel_id=1, source_target_pairs={{0,1},{1,2},{2,3},{3,0},{4,5},{5,6},{6,7},{7,4},{8,9},{9,10},{10,1... | collective-permute-start | bytes 786440 | tf_op jit(solution)/shard_map/ppermute | solution.py:32
  33.5 60.3 %all-to-all-start.1 = ((bf16[32,32,2048]{2,1,0:T(8,128)(2,1)}), bf16[32,32,2048]{2,1,0:T(8,128)(2,1)}, u32[]{:S(2)}, u32[]{:S(2)}) async-start(bf16[32,32,2048]{2,1,0:T(8,128)(2,1)} %route_rest.1), calls=%async_computation.1 | async-start | bytes 8388608 | tf_op jit(solution)/shard_map/all_to_all | solution.py:237
  41.7 13.4 %collective-permute-start.3 = (bf16[16,4,8,512]{3,2,1,0:T(8,128)(2,1)S(1)}, bf16[16,4,8,512]{3,2,1,0:T(8,128)(2,1)S(1)}, u32[]{:S(2)}, u32[]{:S(2)}) collective-permute-start(bf16[16,4,8,512]{3,2,1,0:T(8,128)(2,1)S(1)} %get-tuple-element.71), channel_id=1, source_target_pairs={{0,3},{1,0},{2,1},{3,2},{4,7},{5,4},{6,5},{7,6},{8,11},{9,8},{10,9... | collective-permute-start | bytes 1572872 | tf_op jit(solution)/shard_map/ppermute | solution.py:32
  44.1 14.5 %collective-permute-start = (bf16[16,4,8,512]{3,2,1,0:T(8,128)(2,1)S(1)}, bf16[16,4,8,512]{3,2,1,0:T(8,128)(2,1)S(1)}, u32[]{:S(2)}, u32[]{:S(2)}) collective-permute-start(bf16[16,4,8,512]{3,2,1,0:T(8,128)(2,1)S(1)} %get-tuple-element.72), channel_id=1, source_target_pairs={{0,1},{1,2},{2,3},{3,0},{4,5},{5,6},{6,7},{7,4},{8,9},{9,10},{10,1... | collective-permute-start | bytes 1572872 | tf_op jit(solution)/shard_map/ppermute | solution.py:32
  44.1 25.4 %collective-permute-start.1 = (bf16[16,4,8,512]{3,2,1,0:T(8,128)(2,1)S(1)}, bf16[16,4,8,512]{3,2,1,0:T(8,128)(2,1)S(1)}, u32[]{:S(2)}, u32[]{:S(2)}) collective-permute-start(bf16[16,4,8,512]{3,2,1,0:T(8,128)(2,1)S(1)} %get-tuple-element.71), channel_id=1, source_target_pairs={{0,1},{1,2},{2,3},{3,0},{4,5},{5,6},{6,7},{7,4},{8,9},{9,10},{10,1... | collective-permute-start | bytes 1572872 | tf_op jit(solution)/shard_map/ppermute | solution.py:32
  44.1 25.4 %collective-permute-start.2 = (bf16[16,4,8,512]{3,2,1,0:T(8,128)(2,1)S(1)}, bf16[16,4,8,512]{3,2,1,0:T(8,128)(2,1)S(1)}, u32[]{:S(2)}, u32[]{:S(2)}) collective-permute-start(bf16[16,4,8,512]{3,2,1,0:T(8,128)(2,1)S(1)} %get-tuple-element.72), channel_id=1, source_target_pairs={{0,3},{1,0},{2,1},{3,2},{4,7},{5,4},{6,5},{7,6},{8,11},{9,8},{10,9... | collective-permute-start | bytes 1572872 | tf_op jit(solution)/shard_map/ppermute | solution.py:32
  55.1 25.7 %copy-start.3 = (bf16[16,4,8,512]{3,2,1,0:T(8,128)(2,1)}, bf16[16,4,8,512]{3,2,1,0:T(8,128)(2,1)S(1)}, u32[]{:S(2)}) copy-start(bf16[16,4,8,512]{3,2,1,0:T(8,128)(2,1)S(1)} %collective-permute-done.3.right_b) | copy-start | bytes 1572868
  55.1 22.5 %collective-permute-start.5 = (bf16[16,4,8,512]{3,2,1,0:T(8,128)(2,1)S(1)}, bf16[16,4,8,512]{3,2,1,0:T(8,128)(2,1)S(1)}, u32[]{:S(2)}, u32[]{:S(2)}) collective-permute-start(bf16[16,4,8,512]{3,2,1,0:T(8,128)(2,1)S(1)} %collective-permute-done.3.right_b), channel_id=1, source_target_pairs={{0,3},{1,0},{2,1},{3,2},{4,7},{5,4},{6,5},{7,6},{8,11},{9,8},{10,9... | collective-permute-start | bytes 1572872 | tf_op jit(solution)/shard_map/ppermute | solution.py:32
  58.6 22.2 %copy-start.4 = (bf16[16,4,8,512]{3,2,1,0:T(8,128)(2,1)}, bf16[16,4,8,512]{3,2,1,0:T(8,128)(2,1)S(1)}, u32[]{:S(2)}) copy-start(bf16[16,4,8,512]{3,2,1,0:T(8,128)(2,1)S(1)} %collective-permute-done.left_a) | copy-start | bytes 1572868
  58.6 22.1 %collective-permute-start.4 = (bf16[16,4,8,512]{3,2,1,0:T(8,128)(2,1)S(1)}, bf16[16,4,8,512]{3,2,1,0:T(8,128)(2,1)S(1)}, u32[]{:S(2)}, u32[]{:S(2)}) collective-permute-start(bf16[16,4,8,512]{3,2,1,0:T(8,128)(2,1)S(1)} %collective-permute-done.left_a), channel_id=1, source_target_pairs={{0,1},{1,2},{2,3},{3,0},{4,5},{5,6},{6,7},{7,4},{8,9},{9,10},{10,1... | collective-permute-start | bytes 1572872 | tf_op jit(solution)/shard_map/ppermute | solution.py:32
  105.2 13.2 %collective-permute-start.9 = (bf16[16,4,8,384]{3,2,1,0:T(8,128)(2,1)}, bf16[16,4,8,384]{3,2,1,0:T(8,128)(2,1)S(1)}, u32[]{:S(2)}, u32[]{:S(2)}) collective-permute-start(bf16[16,4,8,384]{3,2,1,0:T(8,128)(2,1)} %get-tuple-element.46), channel_id=1, source_target_pairs={{0,1},{1,2},{2,3},{3,0},{4,5},{5,6},{6,7},{7,4},{8,9},{9,10},{10,1... | collective-permute-start | bytes 1179656 | tf_op jit(solution)/shard_map/ppermute | solution.py:32
  106.0 13.6 %collective-permute-start.13 = (bf16[16,4,8,384]{3,2,1,0:T(8,128)(2,1)}, bf16[16,4,8,384]{3,2,1,0:T(8,128)(2,1)S(1)}, u32[]{:S(2)}, u32[]{:S(2)}) collective-permute-start(bf16[16,4,8,384]{3,2,1,0:T(8,128)(2,1)} %get-tuple-element.51), channel_id=1, source_target_pairs={{0,3},{1,0},{2,1},{3,2},{4,7},{5,4},{6,5},{7,6},{8,11},{9,8},{10,9... | collective-permute-start | bytes 1179656 | tf_op jit(solution)/shard_map/ppermute | solution.py:32
  107.9 29.3 %all-to-all-start.3 = ((bf16[32,32,640]{2,1,0:T(8,128)(2,1)}), bf16[32,32,640]{2,1,0:T(8,128)(2,1)S(1)}, u32[]{:S(2)}, u32[]{:S(2)}) async-start(bf16[32,32,640]{2,1,0:T(8,128)(2,1)} %bitcast.18), calls=%async_computation.3 | async-start | bytes 2621440 | tf_op jit(solution)/shard_map/all_to_all | solution.py:288
  115.6 15.3 %collective-permute-start.11 = (bf16[16,4,8,384]{3,2,1,0:T(8,128)(2,1)}, bf16[16,4,8,384]{3,2,1,0:T(8,128)(2,1)S(1)}, u32[]{:S(2)}, u32[]{:S(2)}) collective-permute-start(bf16[16,4,8,384]{3,2,1,0:T(8,128)(2,1)} %get-tuple-element.47), channel_id=1, source_target_pairs={{0,1},{1,2},{2,3},{3,0},{4,5},{5,6},{6,7},{7,4},{8,9},{9,10},{10,1... | collective-permute-start | bytes 1179656 | tf_op jit(solution)/shard_map/ppermute | solution.py:32
  115.7 15.2 %collective-permute-start.12 = (bf16[16,4,8,384]{3,2,1,0:T(8,128)(2,1)}, bf16[16,4,8,384]{3,2,1,0:T(8,128)(2,1)S(1)}, u32[]{:S(2)}, u32[]{:S(2)}) collective-permute-start(bf16[16,4,8,384]{3,2,1,0:T(8,128)(2,1)} %get-tuple-element.48), channel_id=1, source_target_pairs={{0,3},{1,0},{2,1},{3,2},{4,7},{5,4},{6,5},{7,6},{8,11},{9,8},{10,9... | collective-permute-start | bytes 1179656 | tf_op jit(solution)/shard_map/ppermute | solution.py:32
  119.4 16.6 %collective-permute-start.10 = (bf16[16,4,8,384]{3,2,1,0:T(8,128)(2,1)S(1)}, bf16[16,4,8,384]{3,2,1,0:T(8,128)(2,1)S(1)}, u32[]{:S(2)}, u32[]{:S(2)}) collective-permute-start(bf16[16,4,8,384]{3,2,1,0:T(8,128)(2,1)S(1)} %add_convert_fusion.1), channel_id=1, source_target_pairs={{0,1},{1,2},{2,3},{3,0},{4,5},{5,6},{6,7},{7,4},{8,9},{9,10},{10,1... | collective-permute-start | bytes 1179656 | tf_op jit(solution)/shard_map/ppermute | solution.py:32
  120.6 15.4 %collective-permute-start.14 = (bf16[16,4,8,384]{3,2,1,0:T(8,128)(2,1)S(1)}, bf16[16,4,8,384]{3,2,1,0:T(8,128)(2,1)S(1)}, u32[]{:S(2)}, u32[]{:S(2)}) collective-permute-start(bf16[16,4,8,384]{3,2,1,0:T(8,128)(2,1)S(1)} %add_convert_fusion), channel_id=1, source_target_pairs={{0,3},{1,0},{2,1},{3,2},{4,7},{5,4},{6,5},{7,6},{8,11},{9,8},{10,9... | collective-permute-start | bytes 1179656 | tf_op jit(solution)/shard_map/ppermute | solution.py:32
  137.2 22.3 %all-to-all-start.2 = ((bf16[32,32,384]{2,1,0:T(8,128)(2,1)}), bf16[32,32,384]{2,1,0:T(8,128)(2,1)S(1)}, u32[]{:S(2)}, u32[]{:S(2)}) async-start(bf16[32,32,384]{2,1,0:T(8,128)(2,1)} %bitcast.17), calls=%async_computation.2 | async-start | bytes 1572864 | tf_op jit(solution)/shard_map/all_to_all | solution.py:331
  147.5 9.4 %collective-permute-start.15 = (bf16[288,128]{1,0:T(8,128)(2,1)}, bf16[288,128]{1,0:T(8,128)(2,1)S(1)}, u32[]{:S(2)}, u32[]{:S(2)}) collective-permute-start(bf16[288,128]{1,0:T(8,128)(2,1)} %get-tuple-element.63), channel_id=1, source_target_pairs={{0,1},{1,2},{2,3},{3,0},{4,5},{5,6},{6,7},{7,4},{8,9},{9,10},{10,1... | collective-permute-start | bytes 221192 | tf_op jit(solution)/shard_map/ppermute | solution.py:32
  147.5 9.4 %collective-permute-start.16 = (bf16[288,128]{1,0:T(8,128)(2,1)}, bf16[288,128]{1,0:T(8,128)(2,1)S(1)}, u32[]{:S(2)}, u32[]{:S(2)}) collective-permute-start(bf16[288,128]{1,0:T(8,128)(2,1)} %get-tuple-element.64), channel_id=1, source_target_pairs={{0,2},{1,3},{2,0},{3,1},{4,6},{5,7},{6,4},{7,5},{8,10},{9,11},{10,... | collective-permute-start | bytes 221192 | tf_op jit(solution)/shard_map/ppermute | solution.py:32
  151.3 5.6 %collective-permute-start.17 = (bf16[288,128]{1,0:T(8,128)(2,1)}, bf16[288,128]{1,0:T(8,128)(2,1)}, u32[]{:S(2)}, u32[]{:S(2)}) collective-permute-start(bf16[288,128]{1,0:T(8,128)(2,1)} %get-tuple-element.65), channel_id=1, source_target_pairs={{0,3},{1,0},{2,1},{3,2},{4,7},{5,4},{6,5},{7,6},{8,11},{9,8},{10,9... | collective-permute-start | bytes 221192 | tf_op jit(solution)/shard_map/ppermute | solution.py:32
  (5 other events, 38.7 us)

commit v7 on v6

--- a/solution.py
+++ b/solution.py
@@ -324,7 +324,7 @@
         in_specs=[by_expert(OWN, D), hid_spec],
         out_specs=leading(QH, D),
         out_shape=shape((LOC, QH, D)),
-        compiler_params=params(),
+        compiler_params=params(56),
         cost_estimate=cost(1.1e9, 10e6),
         name="grads_down",
     )(rest, h)
@@ -344,7 +344,9 @@
     )(dest, pltpu.with_memory_space_constraint(part_back, pltpu.VMEM))
     ys = (y0, shift(y1, 1), shift(y2, 2), shift(y3, -1))
 
-    back = pltpu.with_memory_space_constraint(back, pltpu.VMEM)
+    pick, back, *ys = (
+        pltpu.with_memory_space_constraint(v, pltpu.VMEM) for v in (pick, back, *ys)
+    )
     input_grad, mix_t = pl.pallas_call(
         finish,
         out_specs=[pl.BlockSpec(memory_space=pltpu.VMEM)] * 2,

time: 163 us -> 162 us (level)
  no operation moved by 1% of the time
where the time goes in v7:
time: 162 us; the launch traced here: 161 us
  starting transfers between devices  58.4 us (36%)
  waiting for transfers between devices  54.3 us (34%)
  Pallas kernels  45.7 us (28%)
  other arithmetic  2.19 us (1%)
    ppermute x18, waiting for transfers between devices, shift(): return lax.ppermute(x, 'hidden', [(i, (i + d) % NZ) for i in range(NZ)])  46.9 us
    ppermute x18, starting transfers between devices, shift(): return lax.ppermute(x, 'hidden', [(i, (i + d) % NZ) for i in range(NZ)])  25.9 us
    pallas_call x1, Pallas kernels, on_device(): pl.pallas_call(middle, grid=(LOC,), in_specs=[smem, by_expert(OWN, D)] +...  11.4 us
    all_to_all x1, starting transfers between devices, on_device(): got = lax.all_to_all(pay, 'expert', split_axis=0, concat_axis=0, tiled=True)  8.59 us
    pallas_call x1, Pallas kernels, on_device(): pl.pallas_call(gates, grid=(LOC,), in_specs=[smem, whole((2, TOK)), by_ex...  8.25 us
    all_to_all x1, starting transfers between devices, on_device(): lax.all_to_all(pay_rest, 'expert', split_axis=0, concat_axis=0, tiled=True)  8.12 us
    all_to_all x1, starting transfers between devices, on_device(): lax.all_to_all(sums.reshape(OWN, 32, RA), 'expert', split_axis=0, concat_...  8.07 us
    all_to_all x1, starting transfers between devices, on_device(): lax.all_to_all(part.reshape(OWN, 32, WR), 'expert', split_axis=0, concat_...  7.67 us
  transfers between devices with their start and end apart: 22, of which 9 were waited for; matrix products, arithmetic and copies ran while one was open for 1% of the time, Pallas kernels for 18%

profile of v7, /device:TPU:1, one launch (start us, length us, event | category | flops | bytes accessed | tf_op | source)
XLA Modules:
  0.0 161.3 jit_solution(14598245302004978505)
XLA Ops:
  0.6 3.4 %route_first.1 = (bf16[32,32,512]{2,1,0:T(8,128)(2,1)}, s32[2,256]{1,0:T(2,128)}) custom-call(s32[2,256]{1,0:T(2,128)} %bitcast.21, bf16[256,512]{1,0:T(8,128)(2,1)} %tokens.1), custom_call_target="tpu_custom_call" | custom-call | flops 500000000 | bytes 4000000 | tf_op jit(solution)/shard_map/route_first/pallas_call | solution.py:212
  4.1 8.6 %all-to-all-start = ((bf16[32,32,512]{2,1,0:T(8,128)(2,1)}), bf16[32,32,512]{2,1,0:T(8,128)(2,1)S(1)}, u32[]{:S(2)}, u32[]{:S(2)}) async-start(bf16[32,32,512]{2,1,0:T(8,128)(2,1)} %get-tuple-element.39), calls=%async_computation | async-start | bytes 2097152 | tf_op jit(solution)/shard_map/all_to_all | solution.py:223
  12.7 3.7 %collective-permute-start.7 = (bf16[256,512]{1,0:T(8,128)(2,1)}, bf16[256,512]{1,0:T(8,128)(2,1)S(1)}, u32[]{:S(2)}, u32[]{:S(2)}) collective-permute-start(bf16[256,512]{1,0:T(8,128)(2,1)} %c0.1), channel_id=1, source_target_pairs={{0,2},{1,3},{2,0},{3,1},{4,6},{5,7},{6,4},{7,5},{8,10},{9,11},{10,... | collective-permute-start | bytes 786440 | tf_op jit(solution)/shard_map/ppermute | solution.py:32
  17.8 5.3 %collective-permute-done.7.c2 = bf16[256,512]{1,0:T(8,128)(2,1)S(1)} collective-permute-done((bf16[256,512]{1,0:T(8,128)(2,1)}, bf16[256,512]{1,0:T(8,128)(2,1)S(1)}, u32[]{:S(2)}, u32[]{:S(2)}) %collective-permute-start.7) | collective-permute-done | bytes 262176 | tf_op jit(solution)/shard_map/ppermute | solution.py:32
  23.1 6.0 %collective-permute-done.6.c1 = bf16[256,512]{1,0:T(8,128)(2,1)S(1)} collective-permute-done((bf16[256,512]{1,0:T(8,128)(2,1)}, bf16[256,512]{1,0:T(8,128)(2,1)S(1)}, u32[]{:S(2)}, u32[]{:S(2)}) %collective-permute-start.6) | collective-permute-done | bytes 262176 | tf_op jit(solution)/shard_map/ppermute | solution.py:32
  29.2 4.3 %route_rest.1 = bf16[32,32,2048]{2,1,0:T(8,128)(2,1)} custom-call(s32[1]{0:T(128)} %bitcast.z_ref, s32[2,256]{1,0:T(2,128)} %get-tuple-element.38.dest, f32[2,256]{1,0:T(2,128)} %bitcast.19, bf16[256,512]{1,0:T(8,128)(2,1)} %c0.1, bf16[256,512]{1,0:T(8,128)(2,1)S(1)} %collective-permute-done.6.c1, bf16[256,512]{1,0:T(8,128)(2,1)S(1)} %collective-permute-done.7.c2, ...), custom_call_target="tpu_custom_call" | custom-call | flops 800000000 | bytes 6000000 | tf_op jit(solution)/shard_map/route_rest/pallas_call | solution.py:227
  33.5 8.1 %all-to-all-start.1 = ((bf16[32,32,2048]{2,1,0:T(8,128)(2,1)}), bf16[32,32,2048]{2,1,0:T(8,128)(2,1)}, u32[]{:S(2)}, u32[]{:S(2)}) async-start(bf16[32,32,2048]{2,1,0:T(8,128)(2,1)} %route_rest.1), calls=%async_computation.1 | async-start | bytes 8388608 | tf_op jit(solution)/shard_map/all_to_all | solution.py:237
  44.1 2.7 %collective-permute-start.2 = (bf16[16,4,8,512]{3,2,1,0:T(8,128)(2,1)S(1)}, bf16[16,4,8,512]{3,2,1,0:T(8,128)(2,1)S(1)}, u32[]{:S(2)}, u32[]{:S(2)}) collective-permute-start(bf16[16,4,8,512]{3,2,1,0:T(8,128)(2,1)S(1)} %get-tuple-element.72), channel_id=1, source_target_pairs={{0,3},{1,0},{2,1},{3,2},{4,7},{5,4},{6,5},{7,6},{8,11},{9,8},{10,9... | collective-permute-start | bytes 1572872 | tf_op jit(solution)/shard_map/ppermute | solution.py:32
  46.8 8.3 %collective-permute-done.3.right_b = bf16[16,4,8,512]{3,2,1,0:T(8,128)(2,1)S(1)} collective-permute-done((bf16[16,4,8,512]{3,2,1,0:T(8,128)(2,1)S(1)}, bf16[16,4,8,512]{3,2,1,0:T(8,128)(2,1)S(1)}, u32[]{:S(2)}, u32[]{:S(2)}) %collective-permute-start.3) | collective-permute-done | bytes 524320 | tf_op jit(solution)/shard_map/ppermute | solution.py:32
  55.1 3.5 %collective-permute-start.5 = (bf16[16,4,8,512]{3,2,1,0:T(8,128)(2,1)S(1)}, bf16[16,4,8,512]{3,2,1,0:T(8,128)(2,1)S(1)}, u32[]{:S(2)}, u32[]{:S(2)}) collective-permute-start(bf16[16,4,8,512]{3,2,1,0:T(8,128)(2,1)S(1)} %collective-permute-done.3.right_b), channel_id=1, source_target_pairs={{0,3},{1,0},{2,1},{3,2},{4,7},{5,4},{6,5},{7,6},{8,11},{9,8},{10,9... | collective-permute-start | bytes 1572872 | tf_op jit(solution)/shard_map/ppermute | solution.py:32
  58.6 10.9 %collective-permute-done.1.left_b = bf16[16,4,8,512]{3,2,1,0:T(8,128)(2,1)S(1)} collective-permute-done((bf16[16,4,8,512]{3,2,1,0:T(8,128)(2,1)S(1)}, bf16[16,4,8,512]{3,2,1,0:T(8,128)(2,1)S(1)}, u32[]{:S(2)}, u32[]{:S(2)}) %collective-permute-start.1) | collective-permute-done | bytes 524320 | tf_op jit(solution)/shard_map/ppermute | solution.py:32
  69.5 8.0 %collective-permute-done.5.far_b = bf16[16,4,8,512]{3,2,1,0:T(8,128)(2,1)S(1)} collective-permute-done((bf16[16,4,8,512]{3,2,1,0:T(8,128)(2,1)S(1)}, bf16[16,4,8,512]{3,2,1,0:T(8,128)(2,1)S(1)}, u32[]{:S(2)}, u32[]{:S(2)}) %collective-permute-start.5) | collective-permute-done | bytes 524320 | tf_op jit(solution)/shard_map/ppermute | solution.py:32
  77.6 3.2 %collective-permute-done.4.far_a = bf16[16,4,8,512]{3,2,1,0:T(8,128)(2,1)S(1)} collective-permute-done((bf16[16,4,8,512]{3,2,1,0:T(8,128)(2,1)S(1)}, bf16[16,4,8,512]{3,2,1,0:T(8,128)(2,1)S(1)}, u32[]{:S(2)}, u32[]{:S(2)}) %collective-permute-start.4) | collective-permute-done | bytes 524320 | tf_op jit(solution)/shard_map/ppermute | solution.py:32
  80.8 8.2 %gates.1 = (bf16[4,256,2048]{2,1,0:T(8,128)(2,1)}, bf16[4,256,256]{2,1,0:T(8,128)(2,1)}, f32[4,256,256]{2,1,0:T(8,128)}, f32[4,256,256]{2,1,0:T(8,128)}, bf16[256,1024]{1,0:T(8,128)(2,1)}) custom-call(s32[1]{0:T(128)} %bitcast.z_ref, s32[2,256]{1,0:T(2,128)} %get-tuple-element.38.dest, bf16[32,4,8,512]{3,2,1,0:T(8,128)(2,1)} %bitcast.16, ...), custom_call_target="tpu_custom_call" | custom-call | flops 2200000000 | bytes 19000000 | tf_op jit(solution)/shard_map/gates/pallas_call | solution.py:256
  89.0 4.8 %all-to-all-done.1 = bf16[32,32,2048]{2,1,0:T(8,128)(2,1)} async-done(((bf16[32,32,2048]{2,1,0:T(8,128)(2,1)}), bf16[32,32,2048]{2,1,0:T(8,128)(2,1)}, u32[]{:S(2)}, u32[]{:S(2)}) %all-to-all-start.1) | async-done | bytes 4194336 | tf_op jit(solution)/shard_map/all_to_all | solution.py:237
  93.8 11.4 %middle.1 = (bf16[16,4,8,384]{3,2,1,0:T(8,128)(2,1)}, bf16[16,4,8,384]{3,2,1,0:T(8,128)(2,1)}, bf16[16,4,8,384]{3,2,1,0:T(8,128)(2,1)}, bf16[16,4,8,384]{3,2,1,0...) custom-call(s32[1]{0:T(128)} %bitcast.z_ref, ...), custom_call_target="tpu_custom_call" | custom-call | flops 2700000000 | bytes 27000000 | tf_op jit(solution)/shard_map/middle/pallas_call | solution.py:271
  107.9 7.7 %all-to-all-start.3 = ((bf16[32,32,640]{2,1,0:T(8,128)(2,1)}), bf16[32,32,640]{2,1,0:T(8,128)(2,1)S(1)}, u32[]{:S(2)}, u32[]{:S(2)}) async-start(bf16[32,32,640]{2,1,0:T(8,128)(2,1)} %bitcast.18), calls=%async_computation.3 | async-start | bytes 2621440 | tf_op jit(solution)/shard_map/all_to_all | solution.py:288
  115.7 2.7 %collective-permute-start.12 = (bf16[16,4,8,384]{3,2,1,0:T(8,128)(2,1)}, bf16[16,4,8,384]{3,2,1,0:T(8,128)(2,1)S(1)}, u32[]{:S(2)}, u32[]{:S(2)}) collective-permute-start(bf16[16,4,8,384]{3,2,1,0:T(8,128)(2,1)} %get-tuple-element.48), channel_id=1, source_target_pairs={{0,3},{1,0},{2,1},{3,2},{4,7},{5,4},{6,5},{7,6},{8,11},{9,8},{10,9... | collective-permute-start | bytes 1179656 | tf_op jit(solution)/shard_map/ppermute | solution.py:32
  120.6 2.7 %collective-permute-start.14 = (bf16[16,4,8,384]{3,2,1,0:T(8,128)(2,1)S(1)}, bf16[16,4,8,384]{3,2,1,0:T(8,128)(2,1)S(1)}, u32[]{:S(2)}, u32[]{:S(2)}) collective-permute-start(bf16[16,4,8,384]{3,2,1,0:T(8,128)(2,1)S(1)} %add_convert_fusion), channel_id=1, source_target_pairs={{0,3},{1,0},{2,1},{3,2},{4,7},{5,4},{6,5},{7,6},{8,11},{9,8},{10,9... | collective-permute-start | bytes 1179656 | tf_op jit(solution)/shard_map/ppermute | solution.py:32
  123.4 7.5 %grads_up.1 = (bf16[4,2048,256]{2,1,0:T(8,128)(2,1)}, bf16[4,2048,256]{2,1,0:T(8,128)(2,1)}) custom-call(bf16[4,256,2048]{2,1,0:T(8,128)(2,1)} %get-tuple-element.49.x, bf16[4,256,256]{2,1,0:T(8,128)(2,1)} %get-tuple-element.54.dg, bf16[4,256,256]{2,1,0:T(8,128)(2,1)} %get-tuple-element.55.du), custom_call_target="tpu_custom_call" | custom-call | flops 12000000000 | bytes 20000000 | tf_op jit(solution)/shard_map/grads_up/pallas_call | solution.py:299
  130.9 5.1 %collective-permute-done.10.a1 = bf16[16,4,8,384]{3,2,1,0:T(8,128)(2,1)S(1)} collective-permute-done((bf16[16,4,8,384]{3,2,1,0:T(8,128)(2,1)S(1)}, bf16[16,4,8,384]{3,2,1,0:T(8,128)(2,1)S(1)}, u32[]{:S(2)}, u32[]{:S(2)}) %collective-permute-start.10) | collective-permute-done | bytes 393248 | tf_op jit(solution)/shard_map/ppermute | solution.py:32
  137.2 8.1 %all-to-all-start.2 = ((bf16[32,32,384]{2,1,0:T(8,128)(2,1)}), bf16[32,32,384]{2,1,0:T(8,128)(2,1)S(1)}, u32[]{:S(2)}, u32[]{:S(2)}) async-start(bf16[32,32,384]{2,1,0:T(8,128)(2,1)} %bitcast.17), calls=%async_computation.2 | async-start | bytes 1572864 | tf_op jit(solution)/shard_map/all_to_all | solution.py:331
  147.5 3.8 %collective-permute-start.16 = (bf16[288,128]{1,0:T(8,128)(2,1)}, bf16[288,128]{1,0:T(8,128)(2,1)S(1)}, u32[]{:S(2)}, u32[]{:S(2)}) collective-permute-start(bf16[288,128]{1,0:T(8,128)(2,1)} %get-tuple-element.64), channel_id=1, source_target_pairs={{0,2},{1,3},{2,0},{3,1},{4,6},{5,7},{6,4},{7,5},{8,10},{9,11},{10,... | collective-permute-start | bytes 221192 | tf_op jit(solution)/shard_map/ppermute | solution.py:32
  151.3 5.6 %grads_down.1 = bf16[4,256,2048]{2,1,0:T(8,128)(2,1)} custom-call(bf16[32,4,8,2048]{3,2,1,0:T(8,128)(2,1)} %bitcast.6.rest, bf16[4,256,256]{2,1,0:T(8,128)(2,1)} %get-tuple-element.70.h_in.h), custom_call_target="tpu_custom_call" | custom-call | flops 1100000000 | bytes 10000000 | tf_op jit(solution)/shard_map/grads_down/pallas_call | solution.py:321
  (46 shorter events, 16.8 us)
Async XLA Ops:
  4.1 29.4 %all-to-all-start = ((bf16[32,32,512]{2,1,0:T(8,128)(2,1)}), bf16[32,32,512]{2,1,0:T(8,128)(2,1)S(1)}, u32[]{:S(2)}, u32[]{:S(2)}) async-start(bf16[32,32,512]{2,1,0:T(8,128)(2,1)} %get-tuple-element.39), calls=%async_computation | async-start | bytes 2097152 | tf_op jit(solution)/shard_map/all_to_all | solution.py:223
  12.7 10.5 %collective-permute-start.7 = (bf16[256,512]{1,0:T(8,128)(2,1)}, bf16[256,512]{1,0:T(8,128)(2,1)S(1)}, u32[]{:S(2)}, u32[]{:S(2)}) collective-permute-start(bf16[256,512]{1,0:T(8,128)(2,1)} %c0.1), channel_id=1, source_target_pairs={{0,2},{1,3},{2,0},{3,1},{4,6},{5,7},{6,4},{7,5},{8,10},{9,11},{10,... | collective-permute-start | bytes 786440 | tf_op jit(solution)/shard_map/ppermute | solution.py:32
  16.3 12.8 %collective-permute-start.6 = (bf16[256,512]{1,0:T(8,128)(2,1)}, bf16[256,512]{1,0:T(8,128)(2,1)S(1)}, u32[]{:S(2)}, u32[]{:S(2)}) collective-permute-start(bf16[256,512]{1,0:T(8,128)(2,1)} %c0.1), channel_id=1, source_target_pairs={{0,3},{1,0},{2,1},{3,2},{4,7},{5,4},{6,5},{7,6},{8,11},{9,8},{10,9... | collective-permute-start | bytes 786440 | tf_op jit(solution)/shard_map/ppermute | solution.py:32
  16.8 12.4 %collective-permute-start.8 = (bf16[256,512]{1,0:T(8,128)(2,1)}, bf16[256,512]{1,0:T(8,128)(2,1)S(1)}, u32[]{:S(2)}, u32[]{:S(2)}) collective-permute-start(bf16[256,512]{1,0:T(8,128)(2,1)} %c0.1), channel_id=1, source_target_pairs={{0,1},{1,2},{2,3},{3,0},{4,5},{5,6},{6,7},{7,4},{8,9},{9,10},{10,1... | collective-permute-start | bytes 786440 | tf_op jit(solution)/shard_map/ppermute | solution.py:32
  33.5 60.3 %all-to-all-start.1 = ((bf16[32,32,2048]{2,1,0:T(8,128)(2,1)}), bf16[32,32,2048]{2,1,0:T(8,128)(2,1)}, u32[]{:S(2)}, u32[]{:S(2)}) async-start(bf16[32,32,2048]{2,1,0:T(8,128)(2,1)} %route_rest.1), calls=%async_computation.1 | async-start | bytes 8388608 | tf_op jit(solution)/shard_map/all_to_all | solution.py:237
  41.7 13.4 %collective-permute-start.3 = (bf16[16,4,8,512]{3,2,1,0:T(8,128)(2,1)S(1)}, bf16[16,4,8,512]{3,2,1,0:T(8,128)(2,1)S(1)}, u32[]{:S(2)}, u32[]{:S(2)}) collective-permute-start(bf16[16,4,8,512]{3,2,1,0:T(8,128)(2,1)S(1)} %get-tuple-element.71), channel_id=1, source_target_pairs={{0,3},{1,0},{2,1},{3,2},{4,7},{5,4},{6,5},{7,6},{8,11},{9,8},{10,9... | collective-permute-start | bytes 1572872 | tf_op jit(solution)/shard_map/ppermute | solution.py:32
  44.1 14.5 %collective-permute-start = (bf16[16,4,8,512]{3,2,1,0:T(8,128)(2,1)S(1)}, bf16[16,4,8,512]{3,2,1,0:T(8,128)(2,1)S(1)}, u32[]{:S(2)}, u32[]{:S(2)}) collective-permute-start(bf16[16,4,8,512]{3,2,1,0:T(8,128)(2,1)S(1)} %get-tuple-element.72), channel_id=1, source_target_pairs={{0,1},{1,2},{2,3},{3,0},{4,5},{5,6},{6,7},{7,4},{8,9},{9,10},{10,1... | collective-permute-start | bytes 1572872 | tf_op jit(solution)/shard_map/ppermute | solution.py:32
  44.1 25.4 %collective-permute-start.1 = (bf16[16,4,8,512]{3,2,1,0:T(8,128)(2,1)S(1)}, bf16[16,4,8,512]{3,2,1,0:T(8,128)(2,1)S(1)}, u32[]{:S(2)}, u32[]{:S(2)}) collective-permute-start(bf16[16,4,8,512]{3,2,1,0:T(8,128)(2,1)S(1)} %get-tuple-element.71), channel_id=1, source_target_pairs={{0,1},{1,2},{2,3},{3,0},{4,5},{5,6},{6,7},{7,4},{8,9},{9,10},{10,1... | collective-permute-start | bytes 1572872 | tf_op jit(solution)/shard_map/ppermute | solution.py:32
  44.1 25.4 %collective-permute-start.2 = (bf16[16,4,8,512]{3,2,1,0:T(8,128)(2,1)S(1)}, bf16[16,4,8,512]{3,2,1,0:T(8,128)(2,1)S(1)}, u32[]{:S(2)}, u32[]{:S(2)}) collective-permute-start(bf16[16,4,8,512]{3,2,1,0:T(8,128)(2,1)S(1)} %get-tuple-element.72), channel_id=1, source_target_pairs={{0,3},{1,0},{2,1},{3,2},{4,7},{5,4},{6,5},{7,6},{8,11},{9,8},{10,9... | collective-permute-start | bytes 1572872 | tf_op jit(solution)/shard_map/ppermute | solution.py:32
  55.1 25.7 %copy-start.5 = (bf16[16,4,8,512]{3,2,1,0:T(8,128)(2,1)}, bf16[16,4,8,512]{3,2,1,0:T(8,128)(2,1)S(1)}, u32[]{:S(2)}) copy-start(bf16[16,4,8,512]{3,2,1,0:T(8,128)(2,1)S(1)} %collective-permute-done.3.right_b) | copy-start | bytes 1572868
  55.1 22.5 %collective-permute-start.5 = (bf16[16,4,8,512]{3,2,1,0:T(8,128)(2,1)S(1)}, bf16[16,4,8,512]{3,2,1,0:T(8,128)(2,1)S(1)}, u32[]{:S(2)}, u32[]{:S(2)}) collective-permute-start(bf16[16,4,8,512]{3,2,1,0:T(8,128)(2,1)S(1)} %collective-permute-done.3.right_b), channel_id=1, source_target_pairs={{0,3},{1,0},{2,1},{3,2},{4,7},{5,4},{6,5},{7,6},{8,11},{9,8},{10,9... | collective-permute-start | bytes 1572872 | tf_op jit(solution)/shard_map/ppermute | solution.py:32
  58.6 22.2 %copy-start.6 = (bf16[16,4,8,512]{3,2,1,0:T(8,128)(2,1)}, bf16[16,4,8,512]{3,2,1,0:T(8,128)(2,1)S(1)}, u32[]{:S(2)}) copy-start(bf16[16,4,8,512]{3,2,1,0:T(8,128)(2,1)S(1)} %collective-permute-done.left_a) | copy-start | bytes 1572868
  58.6 22.1 %collective-permute-start.4 = (bf16[16,4,8,512]{3,2,1,0:T(8,128)(2,1)S(1)}, bf16[16,4,8,512]{3,2,1,0:T(8,128)(2,1)S(1)}, u32[]{:S(2)}, u32[]{:S(2)}) collective-permute-start(bf16[16,4,8,512]{3,2,1,0:T(8,128)(2,1)S(1)} %collective-permute-done.left_a), channel_id=1, source_target_pairs={{0,1},{1,2},{2,3},{3,0},{4,5},{5,6},{6,7},{7,4},{8,9},{9,10},{10,1... | collective-permute-start | bytes 1572872 | tf_op jit(solution)/shard_map/ppermute | solution.py:32
  105.2 13.2 %collective-permute-start.9 = (bf16[16,4,8,384]{3,2,1,0:T(8,128)(2,1)}, bf16[16,4,8,384]{3,2,1,0:T(8,128)(2,1)S(1)}, u32[]{:S(2)}, u32[]{:S(2)}) collective-permute-start(bf16[16,4,8,384]{3,2,1,0:T(8,128)(2,1)} %get-tuple-element.46), channel_id=1, source_target_pairs={{0,1},{1,2},{2,3},{3,0},{4,5},{5,6},{6,7},{7,4},{8,9},{9,10},{10,1... | collective-permute-start | bytes 1179656 | tf_op jit(solution)/shard_map/ppermute | solution.py:32
  106.0 13.6 %collective-permute-start.13 = (bf16[16,4,8,384]{3,2,1,0:T(8,128)(2,1)}, bf16[16,4,8,384]{3,2,1,0:T(8,128)(2,1)S(1)}, u32[]{:S(2)}, u32[]{:S(2)}) collective-permute-start(bf16[16,4,8,384]{3,2,1,0:T(8,128)(2,1)} %get-tuple-element.51), channel_id=1, source_target_pairs={{0,3},{1,0},{2,1},{3,2},{4,7},{5,4},{6,5},{7,6},{8,11},{9,8},{10,9... | collective-permute-start | bytes 1179656 | tf_op jit(solution)/shard_map/ppermute | solution.py:32
  107.9 29.3 %all-to-all-start.3 = ((bf16[32,32,640]{2,1,0:T(8,128)(2,1)}), bf16[32,32,640]{2,1,0:T(8,128)(2,1)S(1)}, u32[]{:S(2)}, u32[]{:S(2)}) async-start(bf16[32,32,640]{2,1,0:T(8,128)(2,1)} %bitcast.18), calls=%async_computation.3 | async-start | bytes 2621440 | tf_op jit(solution)/shard_map/all_to_all | solution.py:288
  115.6 15.3 %collective-permute-start.11 = (bf16[16,4,8,384]{3,2,1,0:T(8,128)(2,1)}, bf16[16,4,8,384]{3,2,1,0:T(8,128)(2,1)S(1)}, u32[]{:S(2)}, u32[]{:S(2)}) collective-permute-start(bf16[16,4,8,384]{3,2,1,0:T(8,128)(2,1)} %get-tuple-element.47), channel_id=1, source_target_pairs={{0,1},{1,2},{2,3},{3,0},{4,5},{5,6},{6,7},{7,4},{8,9},{9,10},{10,1... | collective-permute-start | bytes 1179656 | tf_op jit(solution)/shard_map/ppermute | solution.py:32
  115.7 15.2 %collective-permute-start.12 = (bf16[16,4,8,384]{3,2,1,0:T(8,128)(2,1)}, bf16[16,4,8,384]{3,2,1,0:T(8,128)(2,1)S(1)}, u32[]{:S(2)}, u32[]{:S(2)}) collective-permute-start(bf16[16,4,8,384]{3,2,1,0:T(8,128)(2,1)} %get-tuple-element.48), channel_id=1, source_target_pairs={{0,3},{1,0},{2,1},{3,2},{4,7},{5,4},{6,5},{7,6},{8,11},{9,8},{10,9... | collective-permute-start | bytes 1179656 | tf_op jit(solution)/shard_map/ppermute | solution.py:32
  119.4 16.6 %collective-permute-start.10 = (bf16[16,4,8,384]{3,2,1,0:T(8,128)(2,1)S(1)}, bf16[16,4,8,384]{3,2,1,0:T(8,128)(2,1)S(1)}, u32[]{:S(2)}, u32[]{:S(2)}) collective-permute-start(bf16[16,4,8,384]{3,2,1,0:T(8,128)(2,1)S(1)} %add_convert_fusion.1), channel_id=1, source_target_pairs={{0,1},{1,2},{2,3},{3,0},{4,5},{5,6},{6,7},{7,4},{8,9},{9,10},{10,1... | collective-permute-start | bytes 1179656 | tf_op jit(solution)/shard_map/ppermute | solution.py:32
  120.6 15.4 %collective-permute-start.14 = (bf16[16,4,8,384]{3,2,1,0:T(8,128)(2,1)S(1)}, bf16[16,4,8,384]{3,2,1,0:T(8,128)(2,1)S(1)}, u32[]{:S(2)}, u32[]{:S(2)}) collective-permute-start(bf16[16,4,8,384]{3,2,1,0:T(8,128)(2,1)S(1)} %add_convert_fusion), channel_id=1, source_target_pairs={{0,3},{1,0},{2,1},{3,2},{4,7},{5,4},{6,5},{7,6},{8,11},{9,8},{10,9... | collective-permute-start | bytes 1179656 | tf_op jit(solution)/shard_map/ppermute | solution.py:32
  137.2 22.3 %all-to-all-start.2 = ((bf16[32,32,384]{2,1,0:T(8,128)(2,1)}), bf16[32,32,384]{2,1,0:T(8,128)(2,1)S(1)}, u32[]{:S(2)}, u32[]{:S(2)}) async-start(bf16[32,32,384]{2,1,0:T(8,128)(2,1)} %bitcast.17), calls=%async_computation.2 | async-start | bytes 1572864 | tf_op jit(solution)/shard_map/all_to_all | solution.py:331
  147.5 9.5 %collective-permute-start.15 = (bf16[288,128]{1,0:T(8,128)(2,1)}, bf16[288,128]{1,0:T(8,128)(2,1)S(1)}, u32[]{:S(2)}, u32[]{:S(2)}) collective-permute-start(bf16[288,128]{1,0:T(8,128)(2,1)} %get-tuple-element.63), channel_id=1, source_target_pairs={{0,1},{1,2},{2,3},{3,0},{4,5},{5,6},{6,7},{7,4},{8,9},{9,10},{10,1... | collective-permute-start | bytes 221192 | tf_op jit(solution)/shard_map/ppermute | solution.py:32
  147.5 9.5 %collective-permute-start.16 = (bf16[288,128]{1,0:T(8,128)(2,1)}, bf16[288,128]{1,0:T(8,128)(2,1)S(1)}, u32[]{:S(2)}, u32[]{:S(2)}) collective-permute-start(bf16[288,128]{1,0:T(8,128)(2,1)} %get-tuple-element.64), channel_id=1, source_target_pairs={{0,2},{1,3},{2,0},{3,1},{4,6},{5,7},{6,4},{7,5},{8,10},{9,11},{10,... | collective-permute-start | bytes 221192 | tf_op jit(solution)/shard_map/ppermute | solution.py:32
  151.3 5.7 %collective-permute-start.17 = (bf16[288,128]{1,0:T(8,128)(2,1)}, bf16[288,128]{1,0:T(8,128)(2,1)S(1)}, u32[]{:S(2)}, u32[]{:S(2)}) collective-permute-start(bf16[288,128]{1,0:T(8,128)(2,1)} %get-tuple-element.65), channel_id=1, source_target_pairs={{0,3},{1,0},{2,1},{3,2},{4,7},{5,4},{6,5},{7,6},{8,11},{9,8},{10,9... | collective-permute-start | bytes 221192 | tf_op jit(solution)/shard_map/ppermute | solution.py:32
  (5 other events, 49.9 us)

commit v8 on v7

--- a/solution.py
+++ b/solution.py
@@ -251,7 +251,7 @@
         pltpu.with_memory_space_constraint(v, pltpu.VMEM) for v in (left_b, right_t, far_t, far_b)
     )
     rows = OWN * CAP
-    hid, hid_f = shape((LOC, rows, QH)), shape((LOC, rows, QH), F32)
+    hid, hid_f = shape((LOC, rows, QH)), pltpu.VMEM((LOC, rows, QH), F32)
     hid_spec = leading(rows, QH)
     x_slots, h, silu, slope, pick = pl.pallas_call(
         gates,
@@ -267,6 +267,7 @@
         name="gates",
     )(z, dest, got, left_t, left_b, right_t, right_b, far_t, far_b, gate_proj, up_proj)
 
+    silu, slope = (pltpu.with_memory_space_constraint(v, pltpu.VMEM) for v in (silu, slope))
     half_part = shape((half, LOC, CAP, RA))
     o0t, o0b, o1t, o1b, o2t, o2b, o3t, o3b, part, dg, du = pl.pallas_call(
         middle,
@@ -275,7 +276,7 @@
         + [leading(D, QH), leading(D, QH), leading(QH, D)],
         out_specs=[by_expert(half, RA)] * 8 + [by_expert(OWN, WR)] + [hid_spec] * 2,
         out_shape=[half_part] * 8 + [shape((OWN, LOC, CAP, WR)), hid, hid],
-        compiler_params=params(),
+        compiler_params=params(58),
         cost_estimate=cost(2.7e9, 27e6),
         name="middle",
     )(z, rest, h, silu, slope, gate_proj, up_proj, down_proj)

time: 162 us -> 162 us (level)
  no operation moved by 1% of the time
where the time goes in v8:
time: 162 us; the launch traced here: 161 us
  starting transfers between devices  58.4 us (36%)
  waiting for transfers between devices  55 us (34%)
  Pallas kernels  44.6 us (28%)
  other arithmetic  2.19 us (1%)
    ppermute x18, waiting for transfers between devices, shift(): return lax.ppermute(x, 'hidden', [(i, (i + d) % NZ) for i in range(NZ)])  46.9 us
    ppermute x18, starting transfers between devices, shift(): return lax.ppermute(x, 'hidden', [(i, (i + d) % NZ) for i in range(NZ)])  25.9 us
    pallas_call x1, Pallas kernels, on_device(): pl.pallas_call(middle, grid=(LOC,), in_specs=[smem, by_expert(OWN, D)] +...  11 us
    all_to_all x1, starting transfers between devices, on_device(): got = lax.all_to_all(pay, 'expert', split_axis=0, concat_axis=0, tiled=True)  8.59 us
    all_to_all x1, starting transfers between devices, on_device(): lax.all_to_all(pay_rest, 'expert', split_axis=0, concat_axis=0, tiled=True)  8.12 us
    all_to_all x1, starting transfers between devices, on_device(): lax.all_to_all(sums.reshape(OWN, 32, RA), 'expert', split_axis=0, concat_...  8.07 us
    all_to_all x1, starting transfers between devices, on_device(): lax.all_to_all(part.reshape(OWN, 32, WR), 'expert', split_axis=0, concat_...  7.67 us
    pallas_call x1, Pallas kernels, on_device(): pl.pallas_call(gates, grid=(LOC,), in_specs=[smem, whole((2, TOK)), by_ex...  7.54 us
  transfers between devices with their start and end apart: 22, of which 9 were waited for; matrix products, arithmetic and copies ran while one was open for 1% of the time, Pallas kernels for 18%

profile of v8, /device:TPU:1, one launch (start us, length us, event | category | flops | bytes accessed | tf_op | source)
XLA Modules:
  0.0 161.0 jit_solution(15679112991090390657)
XLA Ops:
  0.6 3.4 %route_first.1 = (bf16[32,32,512]{2,1,0:T(8,128)(2,1)}, s32[2,256]{1,0:T(2,128)}) custom-call(s32[2,256]{1,0:T(2,128)} %bitcast.21, bf16[256,512]{1,0:T(8,128)(2,1)} %tokens.1), custom_call_target="tpu_custom_call" | custom-call | flops 500000000 | bytes 4000000 | tf_op jit(solution)/shard_map/route_first/pallas_call | solution.py:212
  4.1 8.6 %all-to-all-start = ((bf16[32,32,512]{2,1,0:T(8,128)(2,1)}), bf16[32,32,512]{2,1,0:T(8,128)(2,1)S(1)}, u32[]{:S(2)}, u32[]{:S(2)}) async-start(bf16[32,32,512]{2,1,0:T(8,128)(2,1)} %get-tuple-element.39), calls=%async_computation | async-start | bytes 2097152 | tf_op jit(solution)/shard_map/all_to_all | solution.py:223
  12.7 3.7 %collective-permute-start.7 = (bf16[256,512]{1,0:T(8,128)(2,1)}, bf16[256,512]{1,0:T(8,128)(2,1)S(1)}, u32[]{:S(2)}, u32[]{:S(2)}) collective-permute-start(bf16[256,512]{1,0:T(8,128)(2,1)} %c0.1), channel_id=1, source_target_pairs={{0,2},{1,3},{2,0},{3,1},{4,6},{5,7},{6,4},{7,5},{8,10},{9,11},{10,... | collective-permute-start | bytes 786440 | tf_op jit(solution)/shard_map/ppermute | solution.py:32
  17.8 5.3 %collective-permute-done.7.c2 = bf16[256,512]{1,0:T(8,128)(2,1)S(1)} collective-permute-done((bf16[256,512]{1,0:T(8,128)(2,1)}, bf16[256,512]{1,0:T(8,128)(2,1)S(1)}, u32[]{:S(2)}, u32[]{:S(2)}) %collective-permute-start.7) | collective-permute-done | bytes 262176 | tf_op jit(solution)/shard_map/ppermute | solution.py:32
  23.1 6.0 %collective-permute-done.6.c1 = bf16[256,512]{1,0:T(8,128)(2,1)S(1)} collective-permute-done((bf16[256,512]{1,0:T(8,128)(2,1)}, bf16[256,512]{1,0:T(8,128)(2,1)S(1)}, u32[]{:S(2)}, u32[]{:S(2)}) %collective-permute-start.6) | collective-permute-done | bytes 262176 | tf_op jit(solution)/shard_map/ppermute | solution.py:32
  29.2 4.3 %route_rest.1 = bf16[32,32,2048]{2,1,0:T(8,128)(2,1)} custom-call(s32[1]{0:T(128)} %bitcast.z_ref, s32[2,256]{1,0:T(2,128)} %get-tuple-element.38.dest, f32[2,256]{1,0:T(2,128)} %bitcast.19, bf16[256,512]{1,0:T(8,128)(2,1)} %c0.1, bf16[256,512]{1,0:T(8,128)(2,1)S(1)} %collective-permute-done.6.c1, bf16[256,512]{1,0:T(8,128)(2,1)S(1)} %collective-permute-done.7.c2, ...), custom_call_target="tpu_custom_call" | custom-call | flops 800000000 | bytes 6000000 | tf_op jit(solution)/shard_map/route_rest/pallas_call | solution.py:227
  33.5 8.1 %all-to-all-start.1 = ((bf16[32,32,2048]{2,1,0:T(8,128)(2,1)}), bf16[32,32,2048]{2,1,0:T(8,128)(2,1)}, u32[]{:S(2)}, u32[]{:S(2)}) async-start(bf16[32,32,2048]{2,1,0:T(8,128)(2,1)} %route_rest.1), calls=%async_computation.1 | async-start | bytes 8388608 | tf_op jit(solution)/shard_map/all_to_all | solution.py:237
  44.1 2.7 %collective-permute-start.2 = (bf16[16,4,8,512]{3,2,1,0:T(8,128)(2,1)S(1)}, bf16[16,4,8,512]{3,2,1,0:T(8,128)(2,1)S(1)}, u32[]{:S(2)}, u32[]{:S(2)}) collective-permute-start(bf16[16,4,8,512]{3,2,1,0:T(8,128)(2,1)S(1)} %get-tuple-element.72), channel_id=1, source_target_pairs={{0,3},{1,0},{2,1},{3,2},{4,7},{5,4},{6,5},{7,6},{8,11},{9,8},{10,9... | collective-permute-start | bytes 1572872 | tf_op jit(solution)/shard_map/ppermute | solution.py:32
  46.8 8.3 %collective-permute-done.3.right_b = bf16[16,4,8,512]{3,2,1,0:T(8,128)(2,1)S(1)} collective-permute-done((bf16[16,4,8,512]{3,2,1,0:T(8,128)(2,1)S(1)}, bf16[16,4,8,512]{3,2,1,0:T(8,128)(2,1)S(1)}, u32[]{:S(2)}, u32[]{:S(2)}) %collective-permute-start.3) | collective-permute-done | bytes 524320 | tf_op jit(solution)/shard_map/ppermute | solution.py:32
  55.1 3.5 %collective-permute-start.5 = (bf16[16,4,8,512]{3,2,1,0:T(8,128)(2,1)S(1)}, bf16[16,4,8,512]{3,2,1,0:T(8,128)(2,1)S(1)}, u32[]{:S(2)}, u32[]{:S(2)}) collective-permute-start(bf16[16,4,8,512]{3,2,1,0:T(8,128)(2,1)S(1)} %collective-permute-done.3.right_b), channel_id=1, source_target_pairs={{0,3},{1,0},{2,1},{3,2},{4,7},{5,4},{6,5},{7,6},{8,11},{9,8},{10,9... | collective-permute-start | bytes 1572872 | tf_op jit(solution)/shard_map/ppermute | solution.py:32
  58.6 10.9 %collective-permute-done.1.left_b = bf16[16,4,8,512]{3,2,1,0:T(8,128)(2,1)S(1)} collective-permute-done((bf16[16,4,8,512]{3,2,1,0:T(8,128)(2,1)S(1)}, bf16[16,4,8,512]{3,2,1,0:T(8,128)(2,1)S(1)}, u32[]{:S(2)}, u32[]{:S(2)}) %collective-permute-start.1) | collective-permute-done | bytes 524320 | tf_op jit(solution)/shard_map/ppermute | solution.py:32
  69.5 8.0 %collective-permute-done.5.far_b = bf16[16,4,8,512]{3,2,1,0:T(8,128)(2,1)S(1)} collective-permute-done((bf16[16,4,8,512]{3,2,1,0:T(8,128)(2,1)S(1)}, bf16[16,4,8,512]{3,2,1,0:T(8,128)(2,1)S(1)}, u32[]{:S(2)}, u32[]{:S(2)}) %collective-permute-start.5) | collective-permute-done | bytes 524320 | tf_op jit(solution)/shard_map/ppermute | solution.py:32
  77.6 3.2 %collective-permute-done.4.far_a = bf16[16,4,8,512]{3,2,1,0:T(8,128)(2,1)S(1)} collective-permute-done((bf16[16,4,8,512]{3,2,1,0:T(8,128)(2,1)S(1)}, bf16[16,4,8,512]{3,2,1,0:T(8,128)(2,1)S(1)}, u32[]{:S(2)}, u32[]{:S(2)}) %collective-permute-start.4) | collective-permute-done | bytes 524320 | tf_op jit(solution)/shard_map/ppermute | solution.py:32
  80.8 7.5 %gates.1 = (bf16[4,256,2048]{2,1,0:T(8,128)(2,1)}, bf16[4,256,256]{2,1,0:T(8,128)(2,1)}, f32[4,256,256]{2,1,0:T(8,128)S(1)}, f32[4,256,256]{2,1,0:T(8,128)S(1)}, bf16[256,1024]{1,0:T(8,128)(2,1)}) custom-call(s32[1]{0:T(128)} %bitcast.z_ref, s32[2,256]{1,0:T(2,128)} %get-tuple-element.38.dest, bf16[32,4,8,512]{3,2,1,0:T(8,128)(2,1)} %bitcast.16, ...), custom_call_target="tpu_custom_call" | custom-call | flops 2200000000 | bytes 19000000 | tf_op jit(solution)/shard_map/gates/pallas_call | solution.py:256
  88.3 5.5 %all-to-all-done.1 = bf16[32,32,2048]{2,1,0:T(8,128)(2,1)} async-done(((bf16[32,32,2048]{2,1,0:T(8,128)(2,1)}), bf16[32,32,2048]{2,1,0:T(8,128)(2,1)}, u32[]{:S(2)}, u32[]{:S(2)}) %all-to-all-start.1) | async-done | bytes 4194336 | tf_op jit(solution)/shard_map/all_to_all | solution.py:237
  93.8 11.0 %middle.1 = (bf16[16,4,8,384]{3,2,1,0:T(8,128)(2,1)}, bf16[16,4,8,384]{3,2,1,0:T(8,128)(2,1)}, bf16[16,4,8,384]{3,2,1,0:T(8,128)(2,1)}, bf16[16,4,8,384]{3,2,1,0...) custom-call(s32[1]{0:T(128)} %bitcast.z_ref, ...), custom_call_target="tpu_custom_call" | custom-call | flops 2700000000 | bytes 27000000 | tf_op jit(solution)/shard_map/middle/pallas_call | solution.py:272
  107.6 7.7 %all-to-all-start.3 = ((bf16[32,32,640]{2,1,0:T(8,128)(2,1)}), bf16[32,32,640]{2,1,0:T(8,128)(2,1)S(1)}, u32[]{:S(2)}, u32[]{:S(2)}) async-start(bf16[32,32,640]{2,1,0:T(8,128)(2,1)} %bitcast.18), calls=%async_computation.3 | async-start | bytes 2621440 | tf_op jit(solution)/shard_map/all_to_all | solution.py:289
  115.4 2.7 %collective-permute-start.12 = (bf16[16,4,8,384]{3,2,1,0:T(8,128)(2,1)}, bf16[16,4,8,384]{3,2,1,0:T(8,128)(2,1)S(1)}, u32[]{:S(2)}, u32[]{:S(2)}) collective-permute-start(bf16[16,4,8,384]{3,2,1,0:T(8,128)(2,1)} %get-tuple-element.48), channel_id=1, source_target_pairs={{0,3},{1,0},{2,1},{3,2},{4,7},{5,4},{6,5},{7,6},{8,11},{9,8},{10,9... | collective-permute-start | bytes 1179656 | tf_op jit(solution)/shard_map/ppermute | solution.py:32
  120.3 2.7 %collective-permute-start.14 = (bf16[16,4,8,384]{3,2,1,0:T(8,128)(2,1)S(1)}, bf16[16,4,8,384]{3,2,1,0:T(8,128)(2,1)S(1)}, u32[]{:S(2)}, u32[]{:S(2)}) collective-permute-start(bf16[16,4,8,384]{3,2,1,0:T(8,128)(2,1)S(1)} %add_convert_fusion), channel_id=1, source_target_pairs={{0,3},{1,0},{2,1},{3,2},{4,7},{5,4},{6,5},{7,6},{8,11},{9,8},{10,9... | collective-permute-start | bytes 1179656 | tf_op jit(solution)/shard_map/ppermute | solution.py:32
  123.0 7.5 %grads_up.1 = (bf16[4,2048,256]{2,1,0:T(8,128)(2,1)}, bf16[4,2048,256]{2,1,0:T(8,128)(2,1)}) custom-call(bf16[4,256,2048]{2,1,0:T(8,128)(2,1)} %get-tuple-element.49.x, bf16[4,256,256]{2,1,0:T(8,128)(2,1)} %get-tuple-element.54.dg, bf16[4,256,256]{2,1,0:T(8,128)(2,1)} %get-tuple-element.55.du), custom_call_target="tpu_custom_call" | custom-call | flops 12000000000 | bytes 20000000 | tf_op jit(solution)/shard_map/grads_up/pallas_call | solution.py:300
  130.5 5.1 %collective-permute-done.10.a1 = bf16[16,4,8,384]{3,2,1,0:T(8,128)(2,1)S(1)} collective-permute-done((bf16[16,4,8,384]{3,2,1,0:T(8,128)(2,1)S(1)}, bf16[16,4,8,384]{3,2,1,0:T(8,128)(2,1)S(1)}, u32[]{:S(2)}, u32[]{:S(2)}) %collective-permute-start.10) | collective-permute-done | bytes 393248 | tf_op jit(solution)/shard_map/ppermute | solution.py:32
  136.9 8.1 %all-to-all-start.2 = ((bf16[32,32,384]{2,1,0:T(8,128)(2,1)}), bf16[32,32,384]{2,1,0:T(8,128)(2,1)S(1)}, u32[]{:S(2)}, u32[]{:S(2)}) async-start(bf16[32,32,384]{2,1,0:T(8,128)(2,1)} %bitcast.17), calls=%async_computation.2 | async-start | bytes 1572864 | tf_op jit(solution)/shard_map/all_to_all | solution.py:332
  147.1 3.9 %collective-permute-start.16 = (bf16[288,128]{1,0:T(8,128)(2,1)}, bf16[288,128]{1,0:T(8,128)(2,1)S(1)}, u32[]{:S(2)}, u32[]{:S(2)}) collective-permute-start(bf16[288,128]{1,0:T(8,128)(2,1)} %get-tuple-element.64), channel_id=1, source_target_pairs={{0,2},{1,3},{2,0},{3,1},{4,6},{5,7},{6,4},{7,5},{8,10},{9,11},{10,... | collective-permute-start | bytes 221192 | tf_op jit(solution)/shard_map/ppermute | solution.py:32
  151.0 5.6 %grads_down.1 = bf16[4,256,2048]{2,1,0:T(8,128)(2,1)} custom-call(bf16[32,4,8,2048]{3,2,1,0:T(8,128)(2,1)} %bitcast.6.rest, bf16[4,256,256]{2,1,0:T(8,128)(2,1)} %get-tuple-element.70.h_in.h), custom_call_target="tpu_custom_call" | custom-call | flops 1100000000 | bytes 10000000 | tf_op jit(solution)/shard_map/grads_down/pallas_call | solution.py:322
  (46 shorter events, 16.8 us)
Async XLA Ops:
  4.1 29.4 %all-to-all-start = ((bf16[32,32,512]{2,1,0:T(8,128)(2,1)}), bf16[32,32,512]{2,1,0:T(8,128)(2,1)S(1)}, u32[]{:S(2)}, u32[]{:S(2)}) async-start(bf16[32,32,512]{2,1,0:T(8,128)(2,1)} %get-tuple-element.39), calls=%async_computation | async-start | bytes 2097152 | tf_op jit(solution)/shard_map/all_to_all | solution.py:223
  12.7 10.5 %collective-permute-start.7 = (bf16[256,512]{1,0:T(8,128)(2,1)}, bf16[256,512]{1,0:T(8,128)(2,1)S(1)}, u32[]{:S(2)}, u32[]{:S(2)}) collective-permute-start(bf16[256,512]{1,0:T(8,128)(2,1)} %c0.1), channel_id=1, source_target_pairs={{0,2},{1,3},{2,0},{3,1},{4,6},{5,7},{6,4},{7,5},{8,10},{9,11},{10,... | collective-permute-start | bytes 786440 | tf_op jit(solution)/shard_map/ppermute | solution.py:32
  16.3 12.8 %collective-permute-start.6 = (bf16[256,512]{1,0:T(8,128)(2,1)}, bf16[256,512]{1,0:T(8,128)(2,1)S(1)}, u32[]{:S(2)}, u32[]{:S(2)}) collective-permute-start(bf16[256,512]{1,0:T(8,128)(2,1)} %c0.1), channel_id=1, source_target_pairs={{0,3},{1,0},{2,1},{3,2},{4,7},{5,4},{6,5},{7,6},{8,11},{9,8},{10,9... | collective-permute-start | bytes 786440 | tf_op jit(solution)/shard_map/ppermute | solution.py:32
  16.8 12.4 %collective-permute-start.8 = (bf16[256,512]{1,0:T(8,128)(2,1)}, bf16[256,512]{1,0:T(8,128)(2,1)S(1)}, u32[]{:S(2)}, u32[]{:S(2)}) collective-permute-start(bf16[256,512]{1,0:T(8,128)(2,1)} %c0.1), channel_id=1, source_target_pairs={{0,1},{1,2},{2,3},{3,0},{4,5},{5,6},{6,7},{7,4},{8,9},{9,10},{10,1... | collective-permute-start | bytes 786440 | tf_op jit(solution)/shard_map/ppermute | solution.py:32
  33.5 60.3 %all-to-all-start.1 = ((bf16[32,32,2048]{2,1,0:T(8,128)(2,1)}), bf16[32,32,2048]{2,1,0:T(8,128)(2,1)}, u32[]{:S(2)}, u32[]{:S(2)}) async-start(bf16[32,32,2048]{2,1,0:T(8,128)(2,1)} %route_rest.1), calls=%async_computation.1 | async-start | bytes 8388608 | tf_op jit(solution)/shard_map/all_to_all | solution.py:237
  41.7 13.4 %collective-permute-start.3 = (bf16[16,4,8,512]{3,2,1,0:T(8,128)(2,1)S(1)}, bf16[16,4,8,512]{3,2,1,0:T(8,128)(2,1)S(1)}, u32[]{:S(2)}, u32[]{:S(2)}) collective-permute-start(bf16[16,4,8,512]{3,2,1,0:T(8,128)(2,1)S(1)} %get-tuple-element.71), channel_id=1, source_target_pairs={{0,3},{1,0},{2,1},{3,2},{4,7},{5,4},{6,5},{7,6},{8,11},{9,8},{10,9... | collective-permute-start | bytes 1572872 | tf_op jit(solution)/shard_map/ppermute | solution.py:32
  44.1 14.5 %collective-permute-start = (bf16[16,4,8,512]{3,2,1,0:T(8,128)(2,1)S(1)}, bf16[16,4,8,512]{3,2,1,0:T(8,128)(2,1)S(1)}, u32[]{:S(2)}, u32[]{:S(2)}) collective-permute-start(bf16[16,4,8,512]{3,2,1,0:T(8,128)(2,1)S(1)} %get-tuple-element.72), channel_id=1, source_target_pairs={{0,1},{1,2},{2,3},{3,0},{4,5},{5,6},{6,7},{7,4},{8,9},{9,10},{10,1... | collective-permute-start | bytes 1572872 | tf_op jit(solution)/shard_map/ppermute | solution.py:32
  44.1 25.4 %collective-permute-start.1 = (bf16[16,4,8,512]{3,2,1,0:T(8,128)(2,1)S(1)}, bf16[16,4,8,512]{3,2,1,0:T(8,128)(2,1)S(1)}, u32[]{:S(2)}, u32[]{:S(2)}) collective-permute-start(bf16[16,4,8,512]{3,2,1,0:T(8,128)(2,1)S(1)} %get-tuple-element.71), channel_id=1, source_target_pairs={{0,1},{1,2},{2,3},{3,0},{4,5},{5,6},{6,7},{7,4},{8,9},{9,10},{10,1... | collective-permute-start | bytes 1572872 | tf_op jit(solution)/shard_map/ppermute | solution.py:32
  44.1 25.4 %collective-permute-start.2 = (bf16[16,4,8,512]{3,2,1,0:T(8,128)(2,1)S(1)}, bf16[16,4,8,512]{3,2,1,0:T(8,128)(2,1)S(1)}, u32[]{:S(2)}, u32[]{:S(2)}) collective-permute-start(bf16[16,4,8,512]{3,2,1,0:T(8,128)(2,1)S(1)} %get-tuple-element.72), channel_id=1, source_target_pairs={{0,3},{1,0},{2,1},{3,2},{4,7},{5,4},{6,5},{7,6},{8,11},{9,8},{10,9... | collective-permute-start | bytes 1572872 | tf_op jit(solution)/shard_map/ppermute | solution.py:32
  55.1 25.7 %copy-start.5 = (bf16[16,4,8,512]{3,2,1,0:T(8,128)(2,1)}, bf16[16,4,8,512]{3,2,1,0:T(8,128)(2,1)S(1)}, u32[]{:S(2)}) copy-start(bf16[16,4,8,512]{3,2,1,0:T(8,128)(2,1)S(1)} %collective-permute-done.3.right_b) | copy-start | bytes 1572868
  55.1 22.5 %collective-permute-start.5 = (bf16[16,4,8,512]{3,2,1,0:T(8,128)(2,1)S(1)}, bf16[16,4,8,512]{3,2,1,0:T(8,128)(2,1)S(1)}, u32[]{:S(2)}, u32[]{:S(2)}) collective-permute-start(bf16[16,4,8,512]{3,2,1,0:T(8,128)(2,1)S(1)} %collective-permute-done.3.right_b), channel_id=1, source_target_pairs={{0,3},{1,0},{2,1},{3,2},{4,7},{5,4},{6,5},{7,6},{8,11},{9,8},{10,9... | collective-permute-start | bytes 1572872 | tf_op jit(solution)/shard_map/ppermute | solution.py:32
  58.6 22.2 %copy-start.6 = (bf16[16,4,8,512]{3,2,1,0:T(8,128)(2,1)}, bf16[16,4,8,512]{3,2,1,0:T(8,128)(2,1)S(1)}, u32[]{:S(2)}) copy-start(bf16[16,4,8,512]{3,2,1,0:T(8,128)(2,1)S(1)} %collective-permute-done.left_a) | copy-start | bytes 1572868
  58.6 22.1 %collective-permute-start.4 = (bf16[16,4,8,512]{3,2,1,0:T(8,128)(2,1)S(1)}, bf16[16,4,8,512]{3,2,1,0:T(8,128)(2,1)S(1)}, u32[]{:S(2)}, u32[]{:S(2)}) collective-permute-start(bf16[16,4,8,512]{3,2,1,0:T(8,128)(2,1)S(1)} %collective-permute-done.left_a), channel_id=1, source_target_pairs={{0,1},{1,2},{2,3},{3,0},{4,5},{5,6},{6,7},{7,4},{8,9},{9,10},{10,1... | collective-permute-start | bytes 1572872 | tf_op jit(solution)/shard_map/ppermute | solution.py:32
  104.8 13.2 %collective-permute-start.9 = (bf16[16,4,8,384]{3,2,1,0:T(8,128)(2,1)}, bf16[16,4,8,384]{3,2,1,0:T(8,128)(2,1)S(1)}, u32[]{:S(2)}, u32[]{:S(2)}) collective-permute-start(bf16[16,4,8,384]{3,2,1,0:T(8,128)(2,1)} %get-tuple-element.46), channel_id=1, source_target_pairs={{0,1},{1,2},{2,3},{3,0},{4,5},{5,6},{6,7},{7,4},{8,9},{9,10},{10,1... | collective-permute-start | bytes 1179656 | tf_op jit(solution)/shard_map/ppermute | solution.py:32
  105.6 13.6 %collective-permute-start.13 = (bf16[16,4,8,384]{3,2,1,0:T(8,128)(2,1)}, bf16[16,4,8,384]{3,2,1,0:T(8,128)(2,1)S(1)}, u32[]{:S(2)}, u32[]{:S(2)}) collective-permute-start(bf16[16,4,8,384]{3,2,1,0:T(8,128)(2,1)} %get-tuple-element.51), channel_id=1, source_target_pairs={{0,3},{1,0},{2,1},{3,2},{4,7},{5,4},{6,5},{7,6},{8,11},{9,8},{10,9... | collective-permute-start | bytes 1179656 | tf_op jit(solution)/shard_map/ppermute | solution.py:32
  107.6 29.3 %all-to-all-start.3 = ((bf16[32,32,640]{2,1,0:T(8,128)(2,1)}), bf16[32,32,640]{2,1,0:T(8,128)(2,1)S(1)}, u32[]{:S(2)}, u32[]{:S(2)}) async-start(bf16[32,32,640]{2,1,0:T(8,128)(2,1)} %bitcast.18), calls=%async_computation.3 | async-start | bytes 2621440 | tf_op jit(solution)/shard_map/all_to_all | solution.py:289
  115.3 15.3 %collective-permute-start.11 = (bf16[16,4,8,384]{3,2,1,0:T(8,128)(2,1)}, bf16[16,4,8,384]{3,2,1,0:T(8,128)(2,1)S(1)}, u32[]{:S(2)}, u32[]{:S(2)}) collective-permute-start(bf16[16,4,8,384]{3,2,1,0:T(8,128)(2,1)} %get-tuple-element.47), channel_id=1, source_target_pairs={{0,1},{1,2},{2,3},{3,0},{4,5},{5,6},{6,7},{7,4},{8,9},{9,10},{10,1... | collective-permute-start | bytes 1179656 | tf_op jit(solution)/shard_map/ppermute | solution.py:32
  115.4 15.2 %collective-permute-start.12 = (bf16[16,4,8,384]{3,2,1,0:T(8,128)(2,1)}, bf16[16,4,8,384]{3,2,1,0:T(8,128)(2,1)S(1)}, u32[]{:S(2)}, u32[]{:S(2)}) collective-permute-start(bf16[16,4,8,384]{3,2,1,0:T(8,128)(2,1)} %get-tuple-element.48), channel_id=1, source_target_pairs={{0,3},{1,0},{2,1},{3,2},{4,7},{5,4},{6,5},{7,6},{8,11},{9,8},{10,9... | collective-permute-start | bytes 1179656 | tf_op jit(solution)/shard_map/ppermute | solution.py:32
  119.1 16.6 %collective-permute-start.10 = (bf16[16,4,8,384]{3,2,1,0:T(8,128)(2,1)S(1)}, bf16[16,4,8,384]{3,2,1,0:T(8,128)(2,1)S(1)}, u32[]{:S(2)}, u32[]{:S(2)}) collective-permute-start(bf16[16,4,8,384]{3,2,1,0:T(8,128)(2,1)S(1)} %add_convert_fusion.1), channel_id=1, source_target_pairs={{0,1},{1,2},{2,3},{3,0},{4,5},{5,6},{6,7},{7,4},{8,9},{9,10},{10,1... | collective-permute-start | bytes 1179656 | tf_op jit(solution)/shard_map/ppermute | solution.py:32
  120.3 15.4 %collective-permute-start.14 = (bf16[16,4,8,384]{3,2,1,0:T(8,128)(2,1)S(1)}, bf16[16,4,8,384]{3,2,1,0:T(8,128)(2,1)S(1)}, u32[]{:S(2)}, u32[]{:S(2)}) collective-permute-start(bf16[16,4,8,384]{3,2,1,0:T(8,128)(2,1)S(1)} %add_convert_fusion), channel_id=1, source_target_pairs={{0,3},{1,0},{2,1},{3,2},{4,7},{5,4},{6,5},{7,6},{8,11},{9,8},{10,9... | collective-permute-start | bytes 1179656 | tf_op jit(solution)/shard_map/ppermute | solution.py:32
  136.9 22.3 %all-to-all-start.2 = ((bf16[32,32,384]{2,1,0:T(8,128)(2,1)}), bf16[32,32,384]{2,1,0:T(8,128)(2,1)S(1)}, u32[]{:S(2)}, u32[]{:S(2)}) async-start(bf16[32,32,384]{2,1,0:T(8,128)(2,1)} %bitcast.17), calls=%async_computation.2 | async-start | bytes 1572864 | tf_op jit(solution)/shard_map/all_to_all | solution.py:332
  147.1 9.5 %collective-permute-start.15 = (bf16[288,128]{1,0:T(8,128)(2,1)}, bf16[288,128]{1,0:T(8,128)(2,1)S(1)}, u32[]{:S(2)}, u32[]{:S(2)}) collective-permute-start(bf16[288,128]{1,0:T(8,128)(2,1)} %get-tuple-element.63), channel_id=1, source_target_pairs={{0,1},{1,2},{2,3},{3,0},{4,5},{5,6},{6,7},{7,4},{8,9},{9,10},{10,1... | collective-permute-start | bytes 221192 | tf_op jit(solution)/shard_map/ppermute | solution.py:32
  147.1 9.5 %collective-permute-start.16 = (bf16[288,128]{1,0:T(8,128)(2,1)}, bf16[288,128]{1,0:T(8,128)(2,1)S(1)}, u32[]{:S(2)}, u32[]{:S(2)}) collective-permute-start(bf16[288,128]{1,0:T(8,128)(2,1)} %get-tuple-element.64), channel_id=1, source_target_pairs={{0,2},{1,3},{2,0},{3,1},{4,6},{5,7},{6,4},{7,5},{8,10},{9,11},{10,... | collective-permute-start | bytes 221192 | tf_op jit(solution)/shard_map/ppermute | solution.py:32
  151.0 5.7 %collective-permute-start.17 = (bf16[288,128]{1,0:T(8,128)(2,1)}, bf16[288,128]{1,0:T(8,128)(2,1)S(1)}, u32[]{:S(2)}, u32[]{:S(2)}) collective-permute-start(bf16[288,128]{1,0:T(8,128)(2,1)} %get-tuple-element.65), channel_id=1, source_target_pairs={{0,3},{1,0},{2,1},{3,2},{4,7},{5,4},{6,5},{7,6},{8,11},{9,8},{10,9... | collective-permute-start | bytes 221192 | tf_op jit(solution)/shard_map/ppermute | solution.py:32
  (5 other events, 49.9 us)
